TPU v7x, 256 devices: a whole 4x4x8 slice. The times are simulated.
256 devices in a mesh: dp: 2 (over x_lo), space: 128 (over z, y, x_hi, core).
Axes of the slice: x: 4 (x_hi: 2, x_lo: 2; x = x_hi * 2 + x_lo), y: 4, z: 8, core: 2. Of those that a mesh axis runs over, the one named last changes fastest.
Arguments:
- latent: bfloat16 [2, 1024, 128, 512], P('dp', 'space'), may hold values from -6 to 6
- cotangent: bfloat16 [2, 1024, 128, 512], P('dp', 'space'), may hold values from -6 to 6
- w_qkv: bfloat16 [512, 1536], replicated, may hold values from -1.6840242 to 1.6840242
- w_out: bfloat16 [512, 512], replicated, may hold values from -0.25 to 0.25
- norm_gain: float32 [512], replicated, may hold values from 0.1 to 1.9
- norm_bias: float32 [512], replicated, may hold values from -3 to 3
Outputs:
- output: bfloat16 [2, 1024, 128, 512], P('dp', 'space')
- grad_input: bfloat16 [2, 1024, 128, 512], P('dp', 'space')
- grad_qkv: float32 [786432], P(('dp', 'space'))
- grad_out: float32 [262144], P(('dp', 'space'))
- grad_norm: float32 [2, 512], replicated
All inputs are finite; a program needn't handle non-finite values.
Results may differ from a plain program's by a relative error of at most 0.015.
The roundings to bfloat16 on the way count: a program that leaves them out, or rounds other values in their place, can miss the bound.
Values may be sent and summed in bfloat16 or wider, within the bound.
No kernel may reach another device: no remote copies, remote signals or barrier semaphores. Data moves between devices by JAX's collectives and lax.ppermute only.
A program may use at most 128 MiB of HBM per device.

v0:
```python
import math

import jax
import jax.numpy as jnp
from jax import lax
from jax.sharding import PartitionSpec as P

HEADS = 16
GRID = 8


def norm_parts(values, norm_gain, norm_bias):
    center = jnp.mean(values, -1, keepdims=True)
    offset = values - center
    variance = jnp.mean(offset * offset, -1, keepdims=True)
    inverse = lax.rsqrt(variance + 1e-05)
    scaled = offset * inverse
    normed = (scaled * norm_gain + norm_bias).astype(jnp.bfloat16)
    return (scaled, inverse, normed)


def window_pass(projected, grad_heads):
    blocks, length, width = grad_heads.shape
    head_size = width // HEADS
    factor = 1.0 / math.sqrt(head_size)
    queries = projected[..., :width].reshape(blocks, length, HEADS, head_size)
    keys_all = projected[..., width : 2 * width].reshape(blocks, length, HEADS, head_size)
    values_all = projected[..., 2 * width :].reshape(blocks, length, HEADS, head_size)
    grad_wide = grad_heads.reshape(blocks, length, HEADS, head_size)
    scores = (
        jnp.einsum("bqhd,bkhd->bhqk", queries, keys_all, preferred_element_type=jnp.float32)
        * factor
    )
    highest = jnp.max(scores, -1, keepdims=True)
    weights = jnp.exp(scores - highest)
    probs = weights / jnp.sum(weights, -1, keepdims=True)
    probs_low = probs.astype(jnp.bfloat16)
    attended = jnp.einsum(
        "bhqk,bkhd->bqhd", probs_low, values_all, preferred_element_type=jnp.float32
    ).astype(jnp.bfloat16)
    grad_probs = jnp.einsum(
        "bqhd,bkhd->bhqk", grad_wide, values_all, preferred_element_type=jnp.float32
    )
    grad_values = jnp.einsum(
        "bhqk,bqhd->bkhd", probs_low, grad_wide, preferred_element_type=jnp.float32
    ).astype(jnp.bfloat16)
    grad_scores = (probs * (grad_probs - jnp.sum(probs * grad_probs, -1, keepdims=True))).astype(
        jnp.bfloat16
    )
    grad_queries = (
        jnp.einsum("bhqk,bkhd->bqhd", grad_scores, keys_all, preferred_element_type=jnp.float32)
        * factor
    ).astype(jnp.bfloat16)
    grad_keys = (
        jnp.einsum("bhqk,bqhd->bkhd", grad_scores, queries, preferred_element_type=jnp.float32)
        * factor
    ).astype(jnp.bfloat16)
    grad_proj = jnp.concatenate(
        [
            grad_queries.reshape(blocks, length, width),
            grad_keys.reshape(blocks, length, width),
            grad_values.reshape(blocks, length, width),
        ],
        -1,
    )
    return (attended.reshape(blocks, length, width), grad_proj)


def to_pieces(tensor):
    columns = tensor.shape[2]
    depth = tensor.shape[-1]
    tensor = tensor.reshape(GRID, GRID, columns // GRID, depth).transpose(0, 2, 1, 3)
    return tensor.reshape(columns, GRID, depth)


def from_pieces(tensor):
    columns = tensor.shape[0]
    depth = tensor.shape[-1]
    tensor = tensor.reshape(GRID, columns // GRID, GRID, depth).transpose(0, 2, 1, 3)
    return tensor.reshape(1, GRID, columns, depth)


def pieces_to_windows(tensor, spaces):
    columns = tensor.shape[0]
    depth = tensor.shape[-1]
    tensor = tensor.reshape(GRID, spaces // GRID, columns // spaces, GRID, depth).transpose(
        1, 2, 0, 3, 4
    )
    return tensor.reshape(columns // GRID, GRID * GRID, depth)


def windows_to_pieces(tensor, spaces):
    columns = tensor.shape[0] * GRID
    depth = tensor.shape[-1]
    tensor = tensor.reshape(spaces // GRID, columns // spaces, GRID, GRID, depth).transpose(
        2, 0, 1, 3, 4
    )
    return tensor.reshape(columns, GRID, depth)


def front_pass(flat_latent, flat_grad, w_qkv, w_out, norm_gain, norm_bias):
    scaled, inverse, normed = norm_parts(flat_latent.astype(jnp.float32), norm_gain, norm_bias)
    projected = jnp.dot(normed, w_qkv, preferred_element_type=jnp.float32).astype(jnp.bfloat16)
    grad_heads = lax.dot_general(
        flat_grad, w_out, (((1,), (1,)), ((), ())), preferred_element_type=jnp.float32
    ).astype(jnp.bfloat16)
    return (scaled, inverse, normed, projected, grad_heads)


def back_pass(
    flat_latent, flat_grad, scaled, inverse, normed, attended, grad_proj, w_qkv, w_out, norm_gain
):
    output = (
        flat_latent.astype(jnp.float32)
        + jnp.dot(attended, w_out, preferred_element_type=jnp.float32)
    ).astype(jnp.bfloat16)
    term_out = lax.dot_general(
        attended, flat_grad, (((0,), (0,)), ((), ())), preferred_element_type=jnp.float32
    )
    term_qkv = lax.dot_general(
        normed, grad_proj, (((0,), (0,)), ((), ())), preferred_element_type=jnp.float32
    )
    grad_normed = lax.dot_general(
        grad_proj, w_qkv, (((1,), (1,)), ((), ())), preferred_element_type=jnp.float32
    )
    grad_hat = grad_normed * norm_gain
    grad_input = flat_grad.astype(jnp.float32) + inverse * (
        grad_hat
        - jnp.mean(grad_hat, -1, keepdims=True)
        - scaled * jnp.mean(grad_hat * scaled, -1, keepdims=True)
    )
    term_norm = jnp.stack([jnp.sum(grad_normed * scaled, 0), jnp.sum(grad_normed, 0)])
    return (output, grad_input.astype(jnp.bfloat16), term_qkv, term_out, term_norm)


def body(latent, cotangent, w_qkv, w_out, norm_gain, norm_bias):
    channels = latent.shape[-1]
    columns = latent.shape[2]
    spaces = lax.axis_size("space")
    flat_latent = latent.reshape(-1, channels)
    flat_grad = cotangent.reshape(-1, channels)
    scaled, inverse, normed, projected, grad_heads = front_pass(
        flat_latent, flat_grad, w_qkv, w_out, norm_gain, norm_bias
    )
    moved_proj, moved_heads = (
        lax.all_to_all(
            to_pieces(projected.reshape(1, GRID, columns, 3 * channels)),
            "space",
            split_axis=0,
            concat_axis=0,
            tiled=True,
        ),
        lax.all_to_all(
            to_pieces(grad_heads.reshape(1, GRID, columns, channels)),
            "space",
            split_axis=0,
            concat_axis=0,
            tiled=True,
        ),
    )
    attended_w, grad_proj_w = window_pass(
        pieces_to_windows(moved_proj, spaces), pieces_to_windows(moved_heads, spaces)
    )
    back_attended, back_proj = (
        lax.all_to_all(
            windows_to_pieces(attended_w, spaces), "space", split_axis=0, concat_axis=0, tiled=True
        ),
        lax.all_to_all(
            windows_to_pieces(grad_proj_w, spaces), "space", split_axis=0, concat_axis=0, tiled=True
        ),
    )
    attended = from_pieces(back_attended).reshape(-1, channels)
    grad_proj = from_pieces(back_proj).reshape(-1, 3 * channels)
    output, grad_input, term_qkv, term_out, term_norm = back_pass(
        flat_latent,
        flat_grad,
        scaled,
        inverse,
        normed,
        attended,
        grad_proj,
        w_qkv,
        w_out,
        norm_gain,
    )
    result = output.reshape(1, GRID, columns, channels)
    grad_result = grad_input.reshape(1, GRID, columns, channels)
    grad_qkv, grad_out = (
        lax.psum_scatter(term_qkv.reshape(-1), ("dp", "space"), scatter_dimension=0, tiled=True),
        lax.psum_scatter(term_out.reshape(-1), ("dp", "space"), scatter_dimension=0, tiled=True),
    )
    grad_norm = lax.psum(term_norm, ("dp", "space"))
    return (result, grad_result, grad_qkv, grad_out, grad_norm)


def solution(mesh):
    in_specs = (P("dp", "space", None, None), P("dp", "space", None, None), P(), P(), P(), P())
    out_specs = (
        P("dp", "space", None, None),
        P("dp", "space", None, None),
        P(("dp", "space")),
        P(("dp", "space")),
        P(),
    )
    return jax.shard_map(body, mesh=mesh, in_specs=in_specs, out_specs=out_specs, check_vma=False)
```

profile of v0, /device:TPU:2, one launch (start us, length us, event | category | flops | bytes accessed | tf_op | source)
XLA Modules:
  0.0 637.4 jit_solution(9621432190110126840)
XLA Ops:
  7.2 0.0 copy-start
  7.2 2.2 convolution_convert_fusion.1
  9.4 0.0 copy-start.2
  9.4 1.6 copy.45
  11.0 15.6 %all-to-all-start.2 = ((bf16[128,8,512]{2,1,0:T(8,128)(2,1)}), bf16[128,8,512]{2,1,0:T(8,128)(2,1)}, u32[]{:S(2)}, u32[]{:S(2)}) async-start(bf16[128,8,512]{2,1,0:T(8,128)(2,1)} %bitcast.131), calls=%async_computation.2 | async-start | bytes 2097152 | tf_op jit(solution)/shard_map/all_to_all | solution.py:153
  26.6 0.2 convert_reduce_fusion
  26.8 0.5 fusion.7
  27.4 0.4 fusion.17
  27.8 1.8 convolution_convert_fusion
  29.6 3.5 copy.36
  33.1 24.8 %all-to-all-done.2 = bf16[128,8,512]{2,1,0:T(8,128)(2,1)} async-done(((bf16[128,8,512]{2,1,0:T(8,128)(2,1)}), bf16[128,8,512]{2,1,0:T(8,128)(2,1)}, u32[]{:S(2)}, u32[]{:S(2)}) %all-to-all-start.2) | async-done | bytes 1048608 | tf_op jit(solution)/shard_map/all_to_all | solution.py:153
  57.9 7.5 %all-to-all-start = ((bf16[128,8,1536]{2,1,0:T(8,128)(2,1)}), bf16[128,8,1536]{2,1,0:T(8,128)(2,1)}, u32[]{:S(2)}, u32[]{:S(2)}) async-start(bf16[128,8,1536]{2,1,0:T(8,128)(2,1)} %bitcast.123), calls=%async_computation | async-start | bytes 6291456 | tf_op jit(solution)/shard_map/all_to_all | solution.py:146
  65.4 2.3 copy.46
  67.7 5.9 reshape_reshape.22
  73.6 5.8 copy.47
  79.3 59.2 %all-to-all-done = bf16[128,8,1536]{2,1,0:T(8,128)(2,1)} async-done(((bf16[128,8,1536]{2,1,0:T(8,128)(2,1)}), bf16[128,8,1536]{2,1,0:T(8,128)(2,1)}, u32[]{:S(2)}, u32[]{:S(2)}) %all-to-all-start) | async-done | bytes 3145760 | tf_op jit(solution)/shard_map/all_to_all | solution.py:146
  138.5 2.2 copy.63
  140.7 1.8 fusion.40
  142.5 2.8 copy.38
  145.3 2.7 copy.39
  148.0 2.7 copy.40
  150.7 8.8 %fusion.41 = (f32[16,16,64]{2,1,0:T(8,128)S(1)}, f32[16,16,64,64]{2,3,1,0:T(8,128)}) fusion(bf16[16,64,16,32]{1,3,2,0:T(8,128)(2,1)} %bitcast.127, bf16[16,64,16,32]{1,3,2,0:T(8,128)(2,1)} %bitcast.125), kind=kOutput, calls=%fused_computation.58 | convolution fusion | flops 70254656 | bytes 6356992 | tf_op jit(solution)/shard_map/sub | solution.py:35
  159.6 6.7 %convert_bitcast_fusion.1 = bf16[16,64,16,32]{1,3,2,0:T(8,128)(2,1)} fusion(bf16[16,64,16,32]{1,3,2,0:T(8,128)(2,1)} %bitcast.136, f32[16,16,64,64]{2,3,1,0:T(8,128)} %get-tuple-element.19, f32[16,16,64]{2,1,0:T(8,128)S(1)} %get-tuple-element.18), kind=kOutput, calls=%fused_computation.38 | convolution fusion | flops 69730304 | bytes 6356992 | tf_op jit(solution)/shard_map/bhqk,bkhd->bqhd/dot_general | solution.py:38
  166.3 1.1 copy-done.7
  167.3 3.7 convert_bitcast_fusion
  171.0 5.5 multiply_reduce_fusion
  176.5 5.7 copy.42
  182.2 6.8 %reshape_reshape.19 = bf16[16,1,8,8,512]{4,3,2,0,1:T(8,128)(2,1)} reshape(bf16[16,64,16,32]{3,2,1,0:T(8,128)(2,1)} %copy.42) | data formatting | bytes 2097152 | tf_op jit(solution)/shard_map/reshape;reshape | solution.py:95
  188.9 2.3 copy.43
  191.2 10.0 %all-to-all-start.1 = ((bf16[128,8,512]{2,1,0:T(8,128)(2,1)}), bf16[128,8,512]{2,1,0:T(8,128)(2,1)}, u32[]{:S(2)}, u32[]{:S(2)}) async-start(bf16[128,8,512]{2,1,0:T(8,128)(2,1)} %bitcast.130), calls=%async_computation.1 | async-start | bytes 2097152 | tf_op jit(solution)/shard_map/all_to_all | solution.py:165
  201.3 5.7 copy.54
  206.9 6.8 %concatenate.12 = bf16[16,1,8,8,512]{4,3,2,0,1:T(8,128)(2,1)} reshape(bf16[16,64,16,32]{3,2,1,0:T(8,128)(2,1)} %copy.54) | data formatting | bytes 2097152 | tf_op jit(solution)/shard_map/concatenate | solution.py:58
  213.7 7.3 %multiply_convert_fusion = bf16[16,16,64,64]{2,3,1,0:T(8,128)(2,1)S(1)} fusion(f32[16,16,64,64]{2,3,1,0:T(8,128)} %get-tuple-element.21, f32[16,16,64]{2,1,0:T(8,128)S(1)} %get-tuple-element.20, f32[16,16,64,64]{2,3,1,0:T(8,128)} %get-tuple-element.19, f32[16,16,64]{2,1,0:T(8,128)S(1)} %get-tuple-element.18), kind=kLoop, calls=%fused_computation.1 | loop fusion | flops 4194304 | bytes 10616832 | tf_op jit(solution)/shard_map/convert_element_type | solution.py:47
  221.0 1.9 copy-done.1
  223.0 3.7 fusion.34
  226.6 5.7 copy.51
  232.3 6.8 %concatenate.11 = bf16[16,1,8,8,512]{4,3,2,0,1:T(8,128)(2,1)} reshape(bf16[16,64,16,32]{3,2,1,0:T(8,128)(2,1)} %copy.51) | data formatting | bytes 2097152 | tf_op jit(solution)/shard_map/concatenate | solution.py:58
  239.1 5.4 fusion.33
  244.4 5.7 copy.49
  250.1 6.8 %concatenate.10 = bf16[16,1,8,8,512]{4,3,2,0,1:T(8,128)(2,1)} reshape(bf16[16,64,16,32]{3,2,1,0:T(8,128)(2,1)} %copy.49) | data formatting | bytes 2097152 | tf_op jit(solution)/shard_map/concatenate | solution.py:58
  256.9 2.0 maximum_bitcast_fusion
  258.9 2.0 copy.55
  260.9 14.5 %all-to-all-start.3 = ((bf16[128,8,1536]{2,1,0:T(8,128)(2,1)}), bf16[128,8,1536]{2,1,0:T(8,128)(2,1)}, u32[]{:S(2)}, u32[]{:S(2)}) async-start(bf16[128,8,1536]{2,1,0:T(8,128)(2,1)} %bitcast.122), calls=%async_computation.3 | async-start | bytes 6291456 | tf_op jit(solution)/shard_map/all_to_all | solution.py:168
  275.4 0.0 all-reduce.5.cloned.1.call-start
  275.4 0.0 copy-start.9
  275.4 1.4 fusion.10
  276.8 1.6 copy.44
  278.4 0.7 convolution_bitcast_fusion
  279.2 0.2 copy-done.10
  279.4 1.2 copy.61
  280.6 68.0 %all-to-all-done.3 = bf16[128,8,1536]{2,1,0:T(8,128)(2,1)} async-done(((bf16[128,8,1536]{2,1,0:T(8,128)(2,1)}), bf16[128,8,1536]{2,1,0:T(8,128)(2,1)}, u32[]{:S(2)}, u32[]{:S(2)}) %all-to-all-start.3) | async-done | bytes 3145760 | tf_op jit(solution)/shard_map/all_to_all | solution.py:168
  348.6 3.0 copy.56
  351.6 1.7 copy-done.5
  353.3 3.5 fusion.42
  356.8 4.4 reshape.159
  361.2 0.0 all-reduce.5.cloned.1.call-update
  361.2 1.0 copy-done.14
  362.2 3.1 fusion.24
  365.3 3.4 fusion.23
  368.8 76.5 %psum.7 = f32[2,512]{1,0:T(2,128)} all-reduce(f32[2,512]{1,0:T(2,128)S(1)} %pad_maximum_fusion), channel_id=1, replica_groups=mesh['dp'=2,'space'=128] {'dp','space'}, use_global_device_ids=true, to_apply=%region_11.0 | all-reduce | flops 1024 | bytes 8192 | tf_op jit(solution)/shard_map/psum | solution.py:192
  445.3 3.1 fusion.22
  448.4 179.4 %all-reduce.5.cloned.1.call-done = (f32[786432]{0:T(1024)}, f32[262144]{0:T(1024)}) async-done(((f32[786432]{0:T(1024)}, f32[262144]{0:T(1024)}), (f32[786432]{0:T(1024)}, f32[262144]{0:T(1024)})) %all-reduce.5.cloned.1.call-update) | async-done | bytes 4194320
  627.7 1.3 dynamic-slice
  629.1 1.3 dynamic-slice.1
  (27 shorter events, 0.1 us)
Async XLA Ops:
  7.2 20.6 %copy-start = (bf16[512,1536]{1,0:T(8,128)(2,1)S(1)}, bf16[512,1536]{1,0:T(8,128)(2,1)}, u32[]{:S(2)}) copy-start(bf16[512,1536]{1,0:T(8,128)(2,1)} %param.8) | copy-start | bytes 4718596
  9.4 17.2 %copy-start.2 = (bf16[1,8,128,512]{3,2,1,0:T(8,128)(2,1)S(1)}, bf16[1,8,128,512]{3,2,1,0:T(8,128)(2,1)}, u32[]{:S(2)}) copy-start(bf16[1,8,128,512]{3,2,1,0:T(8,128)(2,1)} %param.6) | copy-start | bytes 3145732
  11.0 16.3 %copy-start.12 = (f32[512]{0:T(512)S(1)}, f32[512]{0:T(512)}, u32[]{:S(2)}) copy-start(f32[512]{0:T(512)} %param.10) | copy-start | bytes 6148
  11.0 16.4 %copy-start.13 = (f32[512]{0:T(512)S(1)}, f32[512]{0:T(512)}, u32[]{:S(2)}) copy-start(f32[512]{0:T(512)} %param.11) | copy-start | bytes 6148
  11.0 46.9 %all-to-all-start.2 = ((bf16[128,8,512]{2,1,0:T(8,128)(2,1)}), bf16[128,8,512]{2,1,0:T(8,128)(2,1)}, u32[]{:S(2)}, u32[]{:S(2)}) async-start(bf16[128,8,512]{2,1,0:T(8,128)(2,1)} %bitcast.131), calls=%async_computation.2 | async-start | bytes 2097152 | tf_op jit(solution)/shard_map/all_to_all | solution.py:153
  57.9 80.6 %all-to-all-start = ((bf16[128,8,1536]{2,1,0:T(8,128)(2,1)}), bf16[128,8,1536]{2,1,0:T(8,128)(2,1)}, u32[]{:S(2)}, u32[]{:S(2)}) async-start(bf16[128,8,1536]{2,1,0:T(8,128)(2,1)} %bitcast.123), calls=%async_computation | async-start | bytes 6291456 | tf_op jit(solution)/shard_map/all_to_all | solution.py:146
  159.6 6.7 %copy-start.4 = (f32[16,16,64,64]{2,3,1,0:T(8,128)S(1)}, f32[16,16,64,64]{2,3,1,0:T(8,128)}, u32[]{:S(2)}) copy-start(f32[16,16,64,64]{2,3,1,0:T(8,128)} %get-tuple-element.19) | copy-start | bytes 12582916
  159.6 7.7 %copy-start.7 = (bf16[16,64,16,32]{1,3,2,0:T(8,128)(2,1)S(1)}, bf16[16,64,16,32]{1,3,2,0:T(8,128)(2,1)}, u32[]{:S(2)}) copy-start(bf16[16,64,16,32]{1,3,2,0:T(8,128)(2,1)} %copy.47) | copy-start | bytes 3145732
  167.3 3.7 copy-start.8
  191.2 69.6 %all-to-all-start.1 = ((bf16[128,8,512]{2,1,0:T(8,128)(2,1)}), bf16[128,8,512]{2,1,0:T(8,128)(2,1)}, u32[]{:S(2)}, u32[]{:S(2)}) async-start(bf16[128,8,512]{2,1,0:T(8,128)(2,1)} %bitcast.130), calls=%async_computation.1 | async-start | bytes 2097152 | tf_op jit(solution)/shard_map/all_to_all | solution.py:165
  213.7 9.2 %copy-start.3 = (bf16[16,64,512]{1,2,0:T(8,128)(2,1)S(1)}, bf16[16,64,512]{1,2,0:T(8,128)(2,1)}, u32[]{:S(2)}) copy-start(bf16[16,64,512]{1,2,0:T(8,128)(2,1)} %copy.39) | copy-start | bytes 3145732
  221.0 1.9 copy-start.1
  260.9 87.7 %all-to-all-start.3 = ((bf16[128,8,1536]{2,1,0:T(8,128)(2,1)}), bf16[128,8,1536]{2,1,0:T(8,128)(2,1)}, u32[]{:S(2)}, u32[]{:S(2)}) async-start(bf16[128,8,1536]{2,1,0:T(8,128)(2,1)} %bitcast.122), calls=%async_computation.3 | async-start | bytes 6291456 | tf_op jit(solution)/shard_map/all_to_all | solution.py:168
  275.4 352.4 %all-reduce.5.cloned.1.call-start = ((), (), s32[]{:S(2)}) async-start(), calls=%async_computation.4 | async-start | bytes 8388608
  275.4 3.0 copy-start.9
  278.4 1.0 copy-start.10
  348.6 4.7 copy-start.11
  351.6 1.7 copy-start.5
  361.2 1.0 copy-start.14
  362.2 3.1 copy-start.6
Sparse Core Ops, SparseCore 0:
  361.3 266.3 all-reduce.4
where the time goes:
time: 646 us; the launch traced here: 637 us
  waiting for transfers between devices  331 us (51%)
  local copies, waits for them, and re-layouts  104 us (16%)
  blocking collectives  76.5 us (12%)
  matrix products  48.4 us (7%)
  starting transfers between devices  47.6 us (7%)
  other arithmetic  15 us (2%)
  between operations  14.5 us (2%)
    unnamed x2, waiting for transfers between devices  179 us
    psum x1, blocking collectives, body(): grad_norm = lax.psum(term_norm, ('dp', 'space'))  76.5 us
    all_to_all x1, waiting for transfers between devices, body(): lax.all_to_all(windows_to_pieces(grad_proj_w, spaces), 'space', split_axi...  68 us
    all_to_all x1, waiting for transfers between devices, body(): lax.all_to_all(to_pieces(projected.reshape(1, GRID, columns, 3 * channels...  59.2 us
    all_to_all x1, waiting for transfers between devices, body(): lax.all_to_all(to_pieces(grad_heads.reshape(1, GRID, columns, channels)),...  24.8 us
    concatenate x3, local copies, waits for them, and re-layouts, window_pass(): jnp.concatenate([grad_queries.reshape(blocks, length, width), grad_keys.r...  20.4 us
    all_to_all x1, starting transfers between devices, body(): lax.all_to_all(to_pieces(grad_heads.reshape(1, GRID, columns, channels)),...  15.6 us
    all_to_all x1, starting transfers between devices, body(): lax.all_to_all(windows_to_pieces(grad_proj_w, spaces), 'space', split_axi...  14.5 us
  transfers between devices with their start and end apart: 5, of which 4 were waited for; matrix products, arithmetic and copies ran while one was open for 15% of the time, Pallas kernels for 0%

commit v1 on v0

v1 whole, which is shorter than its diff:
```python
import functools
import math

import jax
import jax.numpy as jnp
from jax import lax
from jax.experimental import pallas as pl
from jax.experimental.pallas import tpu as pltpu
from jax.sharding import PartitionSpec as P

HEADS = 16
GRID = 8
CHUNKS = 2
BLOCK = 4
PACK = 4
VMEM_LIMIT = 56 * 1024 * 1024


def column_order(columns, transposed):
    inner = columns // GRID
    row = lax.broadcasted_iota(jnp.int32, (columns, columns), 0)
    col = lax.broadcasted_iota(jnp.int32, (columns, columns), 1)
    if transposed:
        row, col = col, row
    hit = (row // GRID == col % inner) & (row % GRID == col // inner)
    return jnp.where(hit, 1.0, 0.0).astype(jnp.bfloat16)


def pack_kernel(latent_ref, cotangent_ref, *out_refs):
    columns = latent_ref.shape[1]
    rows = columns // CHUNKS
    order = column_order(columns, False)
    for spot in range(GRID):
        for half, ref in enumerate((latent_ref, cotangent_ref)):
            moved = jnp.dot(order, ref[spot], preferred_element_type=jnp.float32)
            moved = moved.astype(jnp.bfloat16)
            for chunk in range(CHUNKS):
                out_refs[chunk][spot, half] = moved[chunk * rows : (chunk + 1) * rows]


def unpack_kernel(*refs):
    piece_refs = refs[:CHUNKS]
    output_ref, grad_ref = refs[CHUNKS:]
    columns = output_ref.shape[1]
    order = column_order(columns, True)
    for spot in range(GRID):
        for half, ref in enumerate((output_ref, grad_ref)):
            rows = jnp.concatenate([piece_ref[spot, half] for piece_ref in piece_refs], 0)
            moved = jnp.dot(order, rows, preferred_element_type=jnp.float32)
            ref[spot] = moved.astype(jnp.bfloat16)


def dot_nt(a, b):
    return lax.dot_general(a, b, (((1,), (1,)), ((), ())), preferred_element_type=jnp.float32)


def dot_tn(a, b):
    return lax.dot_general(a, b, (((0,), (0,)), ((), ())), preferred_element_type=jnp.float32)


def window_kernel(first, last, *refs):
    piece_ref, w_qkv_ref, w_out_ref, gain_ref, bias_ref = refs[:5]
    rest = refs[5:]
    if not first:
        old_qkv_ref, old_out_ref, old_norm_ref = rest[:3]
        rest = rest[3:]
    out_ref = rest[0]
    normed_ref, attended_ref, proj_ref, heads_ref, grad_ref, cot_ref = rest[-6:]
    if last:
        shares_ref = rest[1]
    else:
        grad_qkv_ref, grad_out_ref, grad_norm_ref = rest[1:4]
    width = w_out_ref.shape[0]
    head_size = width // HEADS
    factor = 1.0 / math.sqrt(head_size)
    lanes = PACK * head_size
    cells = GRID * GRID
    rows = piece_ref.shape[2]
    steps = rows // (BLOCK * GRID)
    span = BLOCK * cells

    lane_head = lax.broadcasted_iota(jnp.int32, (PACK * cells, lanes), 1) // head_size
    row_head = lax.broadcasted_iota(jnp.int32, (PACK * cells, lanes), 0) // cells
    own = jnp.where(lane_head == row_head, 1.0, 0.0).astype(jnp.bfloat16)
    lane_of = lax.broadcasted_iota(jnp.int32, (cells, lanes), 1) // head_size

    def spread(part):
        return jnp.concatenate([part] * PACK, 0) * own

    def gather_heads(wide):
        result = wide[:cells]
        for h in range(1, PACK):
            result = jnp.where(lane_of == h, wide[h * cells : (h + 1) * cells], result)
        return result

    def step(i, norm_sums):
        at = pl.multiple_of(i * (BLOCK * GRID), BLOCK * GRID)
        base = pl.multiple_of(i * span, span)

        def load(half):
            parts = [
                piece_ref[spot, half, pl.ds(at, BLOCK * GRID), :]
                .astype(jnp.float32)
                .reshape(BLOCK, GRID, width)
                for spot in range(GRID)
            ]
            return jnp.stack(parts, 1).reshape(span, width)

        latent = load(0)
        cotangent = load(1)
        center = jnp.mean(latent, -1, keepdims=True)
        offset = latent - center
        variance = jnp.mean(offset * offset, -1, keepdims=True)
        inverse = lax.rsqrt(variance + 1e-05)
        scaled = offset * inverse
        normed = (scaled * gain_ref[...] + bias_ref[...]).astype(jnp.bfloat16)
        cot_low = cotangent.astype(jnp.bfloat16)
        normed_ref[pl.ds(base, span), :] = normed
        cot_ref[pl.ds(base, span), :] = cot_low
        proj_ref[...] = jnp.dot(
            normed, w_qkv_ref[...], preferred_element_type=jnp.float32
        ).astype(jnp.bfloat16)
        heads_ref[...] = dot_nt(cot_low, w_out_ref[...]).astype(jnp.bfloat16)
        for w in range(BLOCK):
            own_rows = slice(w * cells, (w + 1) * cells)
            store_rows = pl.ds(base + w * cells, cells)
            for g in range(HEADS // PACK):
                lo = g * lanes
                queries = proj_ref[own_rows, lo : lo + lanes]
                keys = proj_ref[own_rows, width + lo : width + lo + lanes]
                values = proj_ref[own_rows, 2 * width + lo : 2 * width + lo + lanes]
                grads = heads_ref[own_rows, lo : lo + lanes]
                wide_q = spread(queries)
                wide_g = spread(grads)
                scores = dot_nt(keys, wide_q) * factor
                highest = jnp.max(scores, 0, keepdims=True)
                weights = jnp.exp(scores - highest)
                probs = weights / jnp.sum(weights, 0, keepdims=True)
                probs_low = probs.astype(jnp.bfloat16)
                grad_probs = dot_nt(values, wide_g)
                mean_grad = jnp.sum(probs * grad_probs, 0, keepdims=True)
                grad_scores = (probs * (grad_probs - mean_grad)).astype(jnp.bfloat16)
                attended = gather_heads(dot_tn(probs_low, values))
                grad_q = gather_heads(dot_tn(grad_scores, keys)) * factor
                grad_k = jnp.dot(grad_scores, wide_q, preferred_element_type=jnp.float32) * factor
                grad_v = jnp.dot(probs_low, wide_g, preferred_element_type=jnp.float32)
                attended_ref[store_rows, lo : lo + lanes] = attended.astype(jnp.bfloat16)
                grad_ref[store_rows, lo : lo + lanes] = grad_q.astype(jnp.bfloat16)
                grad_ref[store_rows, width + lo : width + lo + lanes] = grad_k.astype(jnp.bfloat16)
                grad_ref[store_rows, 2 * width + lo : 2 * width + lo + lanes] = grad_v.astype(
                    jnp.bfloat16
                )
        output = latent + jnp.dot(
            attended_ref[pl.ds(base, span), :], w_out_ref[...], preferred_element_type=jnp.float32
        )
        grad_normed = dot_nt(grad_ref[pl.ds(base, span), :], w_qkv_ref[...])
        grad_hat = grad_normed * gain_ref[...]
        grad_input = cotangent + inverse * (
            grad_hat
            - jnp.mean(grad_hat, -1, keepdims=True)
            - scaled * jnp.mean(grad_hat * scaled, -1, keepdims=True)
        )
        for half, value in enumerate((output, grad_input)):
            value = value.reshape(BLOCK, GRID, GRID, width)
            for s in range(GRID):
                piece = value[:, s].reshape(BLOCK * GRID, width)
                out_ref[s, half, pl.ds(at, BLOCK * GRID), :] = piece.astype(jnp.bfloat16)
        gain_sum = jnp.sum(grad_normed * scaled, 0, keepdims=True)
        bias_sum = jnp.sum(grad_normed, 0, keepdims=True)
        return (norm_sums[0] + gain_sum, norm_sums[1] + bias_sum)

    if first:
        start = (jnp.zeros((1, width), jnp.float32), jnp.zeros((1, width), jnp.float32))
    else:
        start = (old_norm_ref[0:1, :], old_norm_ref[1:2, :])
    sums = lax.fori_loop(0, steps, step, start)
    grad_qkv = dot_tn(normed_ref[...], grad_ref[...])
    grad_out = dot_tn(attended_ref[...], cot_ref[...])
    if not first:
        grad_qkv = grad_qkv + old_qkv_ref[...]
        grad_out = grad_out + old_out_ref[...]
    if not last:
        grad_norm_ref[0:1, :] = sums[0]
        grad_norm_ref[1:2, :] = sums[1]
        grad_qkv_ref[...] = grad_qkv
        grad_out_ref[...] = grad_out
        return
    low = jnp.bfloat16
    order = share_order(width, shares_ref.shape[0])
    for lo, part in ((0, grad_qkv), (3 * width, grad_out)):
        part = jnp.dot(order, part.astype(low), preferred_element_type=jnp.float32).astype(low)
        part = part.reshape(shares_ref.shape[0], shares_ref.shape[1], part.shape[1])
        shares_ref[:, :, lo : lo + part.shape[2]] = part
    norm = jnp.concatenate([s[:, i : i + 128] for s in sums for i in range(0, width, 128)], 0)
    high = norm.astype(low).astype(jnp.float32)
    norm = jnp.concatenate([high, norm - high], 0).astype(low)
    shares_ref[:, :, 4 * width :] = jnp.broadcast_to(norm[None], (shares_ref.shape[0],) + norm.shape)


def share_order(width, planes):
    pair = width // (planes * GRID)
    near = planes // 2
    row = lax.broadcasted_iota(jnp.int32, (width, width), 0)
    col = lax.broadcasted_iota(jnp.int32, (width, width), 1)
    at = row % pair
    spot = row // pair % GRID
    plane = row // (pair * GRID)
    source = ((plane // near * GRID + spot) * near + plane % near) * pair + at
    return jnp.where(col == source, 1.0, 0.0).astype(jnp.bfloat16)


def first_sum_kernel(shares_ref, out_ref):
    low = jnp.bfloat16
    total = jnp.sum(shares_ref[...].astype(jnp.float32), 0)
    rows, wide = total.shape
    count = rows // GRID
    main = wide - 128
    norm = total[:GRID, main:] + total[GRID:, main:]
    high = norm.astype(low).astype(jnp.float32)
    rest = norm - high
    high = jnp.concatenate([high[i : i + 1] for i in range(GRID)], 1)
    rest = jnp.concatenate([rest[i : i + 1] for i in range(GRID)], 1)
    norm = jnp.concatenate([high, rest], 0).astype(low)
    out_ref[:, :, :main] = total[:, :main].reshape(GRID, count, main).astype(low)
    out_ref[:, :, main:] = jnp.broadcast_to(norm[None], (GRID,) + norm.shape)


def second_sum_kernel(shares_ref, qkv_ref, out_ref, norm_ref):
    total = jnp.sum(shares_ref[...].astype(jnp.float32), 0)
    width = out_ref.shape[1]
    qkv_ref[...] = total[:, : 3 * width]
    out_ref[...] = total[:, 3 * width : 4 * width]
    norm = total[0:1, 4 * width :] + total[1:2, 4 * width :]
    norm_ref[0:1, :] = norm[:, :width]
    norm_ref[1:2, :] = norm[:, width:]


VMEM = pl.BlockSpec(memory_space=pltpu.VMEM)
PARAMS = pltpu.CompilerParams(vmem_limit_bytes=VMEM_LIMIT)


def pack(latent, cotangent):
    spots, columns, width = latent.shape
    piece = jax.ShapeDtypeStruct((spots, 2, columns // CHUNKS, width), jnp.bfloat16)
    return pl.pallas_call(
        pack_kernel,
        out_shape=[piece] * CHUNKS,
        in_specs=[VMEM] * 2,
        out_specs=[VMEM] * CHUNKS,
        compiler_params=PARAMS,
        name="pack",
    )(latent, cotangent)


def unpack(pieces, columns):
    spots, _, _, width = pieces[0].shape
    whole = jax.ShapeDtypeStruct((spots, columns, width), jnp.bfloat16)
    return pl.pallas_call(
        unpack_kernel,
        out_shape=[whole] * 2,
        in_specs=[VMEM] * CHUNKS,
        out_specs=[VMEM] * 2,
        compiler_params=PARAMS,
        name="unpack",
    )(*pieces)


def windows(pieces, w_qkv, w_out, gain, bias, old, last):
    _, _, rows, width = pieces.shape
    tokens = GRID * rows
    span = BLOCK * GRID * GRID
    low = jnp.bfloat16
    flops = 2 * tokens * width * width * 12 + 6 * 2 * tokens * width * GRID * GRID * PACK
    if last:
        sums = [jax.ShapeDtypeStruct((last, width // last, 4 * width + 128), low)]
    else:
        sums = [
            jax.ShapeDtypeStruct((width, 3 * width), jnp.float32),
            jax.ShapeDtypeStruct((width, width), jnp.float32),
            jax.ShapeDtypeStruct((2, width), jnp.float32),
        ]
    return pl.pallas_call(
        functools.partial(window_kernel, not old, last),
        out_shape=[jax.ShapeDtypeStruct(pieces.shape, low)] + sums,
        in_specs=[VMEM] * (5 + len(old)),
        out_specs=[VMEM] * (1 + len(sums)),
        scratch_shapes=[
            pltpu.VMEM((tokens, width), low),
            pltpu.VMEM((tokens, width), low),
            pltpu.VMEM((span, 3 * width), low),
            pltpu.VMEM((span, width), low),
            pltpu.VMEM((tokens, 3 * width), low),
            pltpu.VMEM((tokens, width), low),
        ],
        compiler_params=PARAMS,
        cost_estimate=pl.CostEstimate(
            flops=flops, bytes_accessed=12 * 2**20, transcendentals=tokens * HEADS * GRID * GRID
        ),
        name="windows",
    )(pieces, w_qkv, w_out, gain, bias, *old)


def first_sum(shares):
    _, rows, wide = shares.shape
    result = jax.ShapeDtypeStruct((GRID, rows // GRID, wide - 128 + GRID * 128), jnp.bfloat16)
    return pl.pallas_call(
        first_sum_kernel,
        out_shape=result,
        in_specs=[VMEM],
        out_specs=VMEM,
        compiler_params=PARAMS,
        name="first_sum",
    )(shares)


def second_sum(shares, width):
    _, rows, _ = shares.shape
    return pl.pallas_call(
        second_sum_kernel,
        out_shape=[
            jax.ShapeDtypeStruct((rows, 3 * width), jnp.float32),
            jax.ShapeDtypeStruct((rows, width), jnp.float32),
            jax.ShapeDtypeStruct((2, width), jnp.float32),
        ],
        in_specs=[VMEM],
        out_specs=[VMEM] * 3,
        compiler_params=PARAMS,
        name="second_sum",
    )(shares)


PLANE = ("dp", "y", "x_hi", "core")


def swap(value, axes):
    return lax.all_to_all(value, axes, split_axis=0, concat_axis=0, tiled=True)


def body(latent, cotangent, w_qkv, w_out, norm_gain, norm_bias):
    _, _, columns, width = latent.shape
    planes = math.prod(lax.axis_size(name) for name in PLANE)
    pieces = pack(latent[0], cotangent[0])
    gain = norm_gain.reshape(1, width)
    bias = norm_bias.reshape(1, width)
    arrived = []
    for piece in pieces:
        if arrived:
            arrived[-1], piece = lax.optimization_barrier((arrived[-1], piece))
        arrived.append(swap(piece, "z"))
    sums = []
    returned = []
    for chunk in range(CHUNKS):
        result, *sums = windows(
            arrived[chunk], w_qkv, w_out, gain, bias, sums, planes if chunk == CHUNKS - 1 else 0
        )
        if returned:
            returned[-1], result = lax.optimization_barrier((returned[-1], result))
        returned.append(swap(result, "z"))
    shares = first_sum(swap(sums[0], PLANE))
    grad_qkv, grad_out, grad_norm = second_sum(swap(shares, "z"), width)
    output, grad_input = unpack(returned, columns)
    return (output[None], grad_input[None], grad_qkv.reshape(-1), grad_out.reshape(-1), grad_norm)


def solution(mesh):
    sizes = (mesh.shape["dp"], GRID, mesh.shape["space"] // GRID // 4, 2, 2)
    parts = jax.sharding.Mesh(mesh.devices.reshape(sizes), ("dp", "z", "y", "x_hi", "core"))
    space = ("z", "y", "x_hi", "core")
    in_specs = (P("dp", space, None, None), P("dp", space, None, None), P(), P(), P(), P())
    out_specs = (
        P("dp", space, None, None),
        P("dp", space, None, None),
        P(("dp",) + space),
        P(("dp",) + space),
        P(),
    )
    return jax.shard_map(body, mesh=parts, in_specs=in_specs, out_specs=out_specs, check_vma=False)
```

time: 646 us -> 192 us (0.30); the launches traced: 637 us -> 190 us
  waiting for transfers between devices: 331 us -> 76.2 us
  local copies, waits for them, and re-layouts: 104 us -> 4.21 us
  Pallas kernels: 0 us -> 49.9 us
  matrix products: 48.4 us -> 0 us
  blocking collectives: 76.5 us -> 37.3 us
  starting transfers between devices: 47.6 us -> 21.8 us
  other arithmetic: 15 us -> 0 us
  between operations: 14.5 us -> 0.71 us
    unnamed x2 -> x0, waiting for transfers between devices: 179 us -> none
    psum x1 -> x0, blocking collectives: 76.5 us -> none  [body(): grad_norm = lax.psum(term_norm, ('dp', 'space'))]
    all_to_all x4 -> x5, waiting for transfers between devices: 152 us -> 76.2 us  [swap(): return lax.all_to_all(value, axes, split_axis=0, concat_axis=0, tiled=True)]
    pallas_call x0 -> x6, Pallas kernels: none -> 49.9 us  [the longest x2 38.5 us: windows(): pl.pallas_call(functools.partial(window_kernel, not old, last), out_shape...]
    dot_general x11 -> x0, matrix products: 39.6 us -> none  [the longest x1 6.68 us: window_pass(): jnp.einsum('bhqk,bkhd->bqhd', probs_low, values_all, preferred_element_ty...]
    all_to_all x0 -> x1, blocking collectives: none -> 37.3 us  [swap(): return lax.all_to_all(value, axes, split_axis=0, concat_axis=0, tiled=True)]
    all_to_all x4 -> x5, starting transfers between devices: 47.6 us -> 21.8 us  [swap(): return lax.all_to_all(value, axes, split_axis=0, concat_axis=0, tiled=True)]
    another operation x5 -> x0, local copies, waits for them, and re-layouts: 23.5 us -> none  [the longest x2 11.7 us: window_pass(): grad_wide = grad_heads.reshape(blocks, length, HEADS, head_size)]
  transfers between devices with their start and end apart: 5 -> 5, of which waited for: 4 -> 5; matrix products, arithmetic and copies ran while one was open for 15% -> 0% of each run, Pallas kernels for 0% -> 24%
where the time goes in v1:
time: 192 us; the launch traced here: 190 us
  waiting for transfers between devices  76.2 us (40%)
  Pallas kernels  49.9 us (26%)
  blocking collectives  37.3 us (19%)
  starting transfers between devices  21.8 us (11%)
  local copies, waits for them, and re-layouts  4.21 us (2%)
    all_to_all x5, waiting for transfers between devices, swap(): return lax.all_to_all(value, axes, split_axis=0, concat_axis=0, tiled=True)  76.2 us
    pallas_call x2, Pallas kernels, windows(): pl.pallas_call(functools.partial(window_kernel, not old, last), out_shape...  38.5 us
    all_to_all x1, blocking collectives, swap(): return lax.all_to_all(value, axes, split_axis=0, concat_axis=0, tiled=True)  37.3 us
    all_to_all x5, starting transfers between devices, swap(): return lax.all_to_all(value, axes, split_axis=0, concat_axis=0, tiled=True)  21.8 us
  transfers between devices with their start and end apart: 5, of which 5 were waited for; matrix products, arithmetic and copies ran while one was open for 0% of the time, Pallas kernels for 24%

profile of v1, /device:TPU:2, one launch (start us, length us, event | category | flops | bytes accessed | tf_op | source)
XLA Modules:
  0.0 190.1 jit_solution(11303114204709221494)
XLA Ops:
  0.6 3.5 %pack.1 = (bf16[8,2,64,512]{3,2,1,0:T(8,128)(2,1)}, bf16[8,2,64,512]{3,2,1,0:T(8,128)(2,1)}) custom-call(bf16[8,128,512]{2,1,0:T(8,128)(2,1)} %bitcast.8, bf16[8,128,512]{2,1,0:T(8,128)(2,1)} %bitcast.9), custom_call_target="tpu_custom_call" | custom-call | tf_op jit(solution)/shard_map/pack/pallas_call | solution.py:245
  4.2 37.3 %all_to_all.30.refs_0_ = bf16[8,2,64,512]{3,2,1,0:T(8,128)(2,1)} all-to-all(bf16[8,2,64,512]{3,2,1,0:T(8,128)(2,1)} %get-tuple-element.22), channel_id=1, replica_groups=mesh['dp'=2,'z'=8,'y'=4,'x_hi'=2,'core'=2] {'z'}, dimensions={0} | all-to-all | bytes 2097152 | tf_op jit(solution)/shard_map/all_to_all | solution.py:336
  41.5 3.6 %all-to-all-start.2 = ((bf16[8,2,64,512]{3,2,1,0:T(8,128)(2,1)}), bf16[8,2,64,512]{3,2,1,0:T(8,128)(2,1)S(1)}, u32[]{:S(2)}, u32[]{:S(2)}) async-start(bf16[8,2,64,512]{3,2,1,0:T(8,128)(2,1)} %get-tuple-element.26), calls=%async_computation.2 | async-start | bytes 2097152 | tf_op jit(solution)/shard_map/all_to_all | solution.py:336
  45.0 18.2 %windows.2 = (bf16[8,2,64,512]{3,2,1,0:T(8,128)(2,1)}, f32[512,1536]{1,0:T(8,128)}, f32[512,512]{1,0:T(8,128)}, f32[2,512]{1,0:T(2,128)}) custom-call(bf16[8,2,64,512]{3,2,1,0:T(8,128)(2,1)} %all_to_all.30.refs_0_, bf16[512,1536]{1,0:T(8,128)(2,1)} %refs_1_.3, bf16[512,512]{1,0:T(8,128)(2,1)} %refs_2_.3, f32[1,512]{1,0:T(1,128)} %bitcast.14, f32[1,512]{1,0:T(1,128)} %bitcast.16), custom_call_target="tpu_custom_call" | custom-call | flops 4026531840 | bytes 12582912 | tf_op jit(solution)/shard_map/windows/pallas_call | solution.py:282
  63.2 8.9 %all-to-all-done.2.refs_0_ = bf16[8,2,64,512]{3,2,1,0:T(8,128)(2,1)S(1)} async-done(((bf16[8,2,64,512]{3,2,1,0:T(8,128)(2,1)}), bf16[8,2,64,512]{3,2,1,0:T(8,128)(2,1)S(1)}, u32[]{:S(2)}, u32[]{:S(2)}) %all-to-all-start.2) | async-done | bytes 1048608 | tf_op jit(solution)/shard_map/all_to_all | solution.py:336
  72.2 0.0 copy-start.3
  72.2 3.7 %all-to-all-start.1 = ((bf16[8,2,64,512]{3,2,1,0:T(8,128)(2,1)}), bf16[8,2,64,512]{3,2,1,0:T(8,128)(2,1)S(1)}, u32[]{:S(2)}, u32[]{:S(2)}) async-start(bf16[8,2,64,512]{3,2,1,0:T(8,128)(2,1)} %get-tuple-element.25), calls=%async_computation.1 | async-start | bytes 2097152 | tf_op jit(solution)/shard_map/all_to_all | solution.py:336
  75.9 0.0 copy-done.3
  75.9 20.3 %windows.3 = (bf16[8,2,64,512]{3,2,1,0:T(8,128)(2,1)}, bf16[32,16,2176]{2,1,0:T(8,128)(2,1)}) custom-call(bf16[8,2,64,512]{3,2,1,0:T(8,128)(2,1)} %copy-done.3, bf16[512,1536]{1,0:T(8,128)(2,1)} %refs_1_.3, bf16[512,512]{1,0:T(8,128)(2,1)} %refs_2_.3, f32[1,512]{1,0:T(1,128)} %bitcast.15, f32[1,512]{1,0:T(1,128)} %bitcast.17, ...), custom_call_target="tpu_custom_call" | custom-call | flops 4026531840 | bytes 12582912 | tf_op jit(solution)/shard_map/windows/pallas_call | solution.py:282
  96.3 6.9 %all-to-all-done.1.refs_0_ = bf16[8,2,64,512]{3,2,1,0:T(8,128)(2,1)S(1)} async-done(((bf16[8,2,64,512]{3,2,1,0:T(8,128)(2,1)}), bf16[8,2,64,512]{3,2,1,0:T(8,128)(2,1)S(1)}, u32[]{:S(2)}, u32[]{:S(2)}) %all-to-all-start.1) | async-done | bytes 1048608 | tf_op jit(solution)/shard_map/all_to_all | solution.py:336
  103.2 0.0 copy-start.1
  103.2 1.0 copy-done.1
  104.2 7.6 %all-to-all-start.4 = ((bf16[32,16,2176]{2,1,0:T(8,128)(2,1)}), bf16[32,16,2176]{2,1,0:T(8,128)(2,1)S(1)}, u32[]{:S(2)}, u32[]{:S(2)}) async-start(bf16[32,16,2176]{2,1,0:T(8,128)(2,1)} %get-tuple-element.35), calls=%async_computation.4 | async-start | bytes 4456448 | tf_op jit(solution)/shard_map/all_to_all | solution.py:336
  111.8 29.0 %all-to-all-done.4.shares_ref = bf16[32,16,2176]{2,1,0:T(8,128)(2,1)S(1)} async-done(((bf16[32,16,2176]{2,1,0:T(8,128)(2,1)}), bf16[32,16,2176]{2,1,0:T(8,128)(2,1)S(1)}, u32[]{:S(2)}, u32[]{:S(2)}) %all-to-all-start.4) | async-done | bytes 2228256 | tf_op jit(solution)/shard_map/all_to_all | solution.py:336
  140.8 0.0 copy-start
  140.8 3.6 %all-to-all-start.3 = ((bf16[8,2,64,512]{3,2,1,0:T(8,128)(2,1)}), bf16[8,2,64,512]{3,2,1,0:T(8,128)(2,1)S(1)}, u32[]{:S(2)}, u32[]{:S(2)}) async-start(bf16[8,2,64,512]{3,2,1,0:T(8,128)(2,1)} %get-tuple-element.32), calls=%async_computation.3 | async-start | bytes 2097152 | tf_op jit(solution)/shard_map/all_to_all | solution.py:336
  144.4 0.0 copy-done
  144.4 2.7 %first_sum.1 = bf16[8,2,3072]{2,1,0:T(2,128)(2,1)} custom-call(bf16[32,16,2176]{2,1,0:T(8,128)(2,1)} %copy-done), custom_call_target="tpu_custom_call" | custom-call | tf_op jit(solution)/shard_map/first_sum/pallas_call | solution.py:306
  147.1 26.1 %all-to-all-done.3.refs_1_ = bf16[8,2,64,512]{3,2,1,0:T(8,128)(2,1)S(1)} async-done(((bf16[8,2,64,512]{3,2,1,0:T(8,128)(2,1)}), bf16[8,2,64,512]{3,2,1,0:T(8,128)(2,1)S(1)}, u32[]{:S(2)}, u32[]{:S(2)}) %all-to-all-start.3) | async-done | bytes 1048608 | tf_op jit(solution)/shard_map/all_to_all | solution.py:336
  173.2 0.0 copy-start.2
  173.2 3.4 %all-to-all-start.5 = ((bf16[8,2,3072]{2,1,0:T(2,128)(2,1)}), bf16[8,2,3072]{2,1,0:T(2,128)(2,1)S(1)}, u32[]{:S(2)}, u32[]{:S(2)}) async-start(bf16[8,2,3072]{2,1,0:T(2,128)(2,1)} %first_sum.1), calls=%async_computation.5 | async-start | bytes 196608 | tf_op jit(solution)/shard_map/all_to_all | solution.py:336
  176.5 0.0 copy-done.2
  176.5 3.5 %unpack.1 = (bf16[8,128,512]{2,1,0:T(8,128)(2,1)}, bf16[8,128,512]{2,1,0:T(8,128)(2,1)}) custom-call(bf16[8,2,64,512]{3,2,1,0:T(8,128)(2,1)} %copy-done.1, bf16[8,2,64,512]{3,2,1,0:T(8,128)(2,1)} %copy-done.2), custom_call_target="tpu_custom_call" | custom-call | tf_op jit(solution)/shard_map/unpack/pallas_call | solution.py:258
  180.1 5.3 %all-to-all-done.5.shares_ref = bf16[8,2,3072]{2,1,0:T(2,128)(2,1)S(1)} async-done(((bf16[8,2,3072]{2,1,0:T(2,128)(2,1)}), bf16[8,2,3072]{2,1,0:T(2,128)(2,1)S(1)}, u32[]{:S(2)}, u32[]{:S(2)}) %all-to-all-start.5) | async-done | bytes 98336 | tf_op jit(solution)/shard_map/all_to_all | solution.py:336
  185.3 0.0 copy-start.4
  185.3 0.6 copy-done.4
  185.9 1.6 second_sum.1
  187.5 1.3 reshape.24
  188.9 1.3 copy.11
Async XLA Ops:
  41.5 30.7 %all-to-all-start.2 = ((bf16[8,2,64,512]{3,2,1,0:T(8,128)(2,1)}), bf16[8,2,64,512]{3,2,1,0:T(8,128)(2,1)S(1)}, u32[]{:S(2)}, u32[]{:S(2)}) async-start(bf16[8,2,64,512]{3,2,1,0:T(8,128)(2,1)} %get-tuple-element.26), calls=%async_computation.2 | async-start | bytes 2097152 | tf_op jit(solution)/shard_map/all_to_all | solution.py:336
  72.2 3.8 %copy-start.3 = (bf16[8,2,64,512]{3,2,1,0:T(8,128)(2,1)}, bf16[8,2,64,512]{3,2,1,0:T(8,128)(2,1)S(1)}, u32[]{:S(2)}) copy-start(bf16[8,2,64,512]{3,2,1,0:T(8,128)(2,1)S(1)} %all-to-all-done.2.refs_0_) | copy-start | bytes 3145732
  72.2 31.0 %all-to-all-start.1 = ((bf16[8,2,64,512]{3,2,1,0:T(8,128)(2,1)}), bf16[8,2,64,512]{3,2,1,0:T(8,128)(2,1)S(1)}, u32[]{:S(2)}, u32[]{:S(2)}) async-start(bf16[8,2,64,512]{3,2,1,0:T(8,128)(2,1)} %get-tuple-element.25), calls=%async_computation.1 | async-start | bytes 2097152 | tf_op jit(solution)/shard_map/all_to_all | solution.py:336
  103.2 1.0 copy-start.1
  104.2 36.6 %all-to-all-start.4 = ((bf16[32,16,2176]{2,1,0:T(8,128)(2,1)}), bf16[32,16,2176]{2,1,0:T(8,128)(2,1)S(1)}, u32[]{:S(2)}, u32[]{:S(2)}) async-start(bf16[32,16,2176]{2,1,0:T(8,128)(2,1)} %get-tuple-element.35), calls=%async_computation.4 | async-start | bytes 4456448 | tf_op jit(solution)/shard_map/all_to_all | solution.py:336
  140.8 3.6 %copy-start = (bf16[32,16,2176]{2,1,0:T(8,128)(2,1)}, bf16[32,16,2176]{2,1,0:T(8,128)(2,1)S(1)}, u32[]{:S(2)}) copy-start(bf16[32,16,2176]{2,1,0:T(8,128)(2,1)S(1)} %all-to-all-done.4.shares_ref) | copy-start | bytes 6684676
  140.8 32.4 %all-to-all-start.3 = ((bf16[8,2,64,512]{3,2,1,0:T(8,128)(2,1)}), bf16[8,2,64,512]{3,2,1,0:T(8,128)(2,1)S(1)}, u32[]{:S(2)}, u32[]{:S(2)}) async-start(bf16[8,2,64,512]{3,2,1,0:T(8,128)(2,1)} %get-tuple-element.32), calls=%async_computation.3 | async-start | bytes 2097152 | tf_op jit(solution)/shard_map/all_to_all | solution.py:336
  173.2 3.4 %copy-start.2 = (bf16[8,2,64,512]{3,2,1,0:T(8,128)(2,1)}, bf16[8,2,64,512]{3,2,1,0:T(8,128)(2,1)S(1)}, u32[]{:S(2)}) copy-start(bf16[8,2,64,512]{3,2,1,0:T(8,128)(2,1)S(1)} %all-to-all-done.3.refs_1_) | copy-start | bytes 3145732
  173.2 12.1 %all-to-all-start.5 = ((bf16[8,2,3072]{2,1,0:T(2,128)(2,1)}), bf16[8,2,3072]{2,1,0:T(2,128)(2,1)S(1)}, u32[]{:S(2)}, u32[]{:S(2)}) async-start(bf16[8,2,3072]{2,1,0:T(2,128)(2,1)} %first_sum.1), calls=%async_computation.5 | async-start | bytes 196608 | tf_op jit(solution)/shard_map/all_to_all | solution.py:336
  185.3 0.6 copy-start.4

commit v2 on v0

v2 whole, which is shorter than its diff:
```python
import functools
import math

import jax
import jax.numpy as jnp
from jax import lax
from jax.experimental import pallas as pl
from jax.experimental.pallas import tpu as pltpu
from jax.sharding import PartitionSpec as P

HEADS = 16
GRID = 8
STEPS = 2
PACK = 4
UNROLL = 4
VMEM_LIMIT = 56 * 1024 * 1024
SMALL_LIMIT = 12 * 1024 * 1024
LOW = jnp.bfloat16
NEAR = (1, 7)


def dot_nn(a, b):
    return jnp.dot(a, b, preferred_element_type=jnp.float32)


def dot_nt(a, b):
    return lax.dot_general(a, b, (((1,), (1,)), ((), ())), preferred_element_type=jnp.float32)


def dot_tn(a, b):
    return lax.dot_general(a, b, (((0,), (0,)), ((), ())), preferred_element_type=jnp.float32)


def column_order(columns, back):
    inner = columns // GRID
    row = lax.broadcasted_iota(jnp.int32, (columns, columns), 0)
    col = lax.broadcasted_iota(jnp.int32, (columns, columns), 1)
    if back:
        row, col = col, row
    hit = (row // GRID == col % inner) & (row % GRID == col // inner)
    return jnp.where(hit, 1.0, 0.0).astype(LOW)


def to_windows(slabs_ref, cells_ref):
    spots, columns, width = slabs_ref.shape
    order = column_order(columns, False)
    for a in range(spots):
        moved = dot_nn(order, slabs_ref[a])
        cells_ref[:, a] = moved.reshape(columns // GRID, GRID, width)


def from_windows(cells_ref, a):
    inner, _, side, width = cells_ref.shape
    moved = cells_ref[:, a].reshape(inner * side, width).astype(LOW)
    return dot_nn(column_order(inner * side, True), moved).astype(LOW)


def step_rows(cells_ref, step):
    inner, spots, side, width = cells_ref.shape
    part = inner // STEPS
    return cells_ref[step * part : (step + 1) * part].reshape(part * spots * side, width)


def put_rows(cells_ref, step, value):
    inner, spots, side, width = cells_ref.shape
    part = inner // STEPS
    cells_ref[step * part : (step + 1) * part] = value.reshape(part, spots, side, width)


def norm_parts(values):
    center = jnp.mean(values, -1, keepdims=True)
    offset = values - center
    variance = jnp.mean(offset * offset, -1, keepdims=True)
    inverse = lax.rsqrt(variance + 1e-05)
    return offset * inverse, inverse


class Heads:
    def __init__(self, width):
        self.head_size = width // HEADS
        self.lanes = PACK * self.head_size
        self.cells = GRID * GRID
        self.factor = 1.0 / math.sqrt(self.head_size)
        shape = (PACK * self.cells, self.lanes)
        lane_head = lax.broadcasted_iota(jnp.int32, shape, 1) // self.head_size
        row_head = lax.broadcasted_iota(jnp.int32, shape, 0) // self.cells
        self.own = jnp.where(lane_head == row_head, 1.0, 0.0).astype(LOW)
        self.lane_of = lax.broadcasted_iota(jnp.int32, (self.cells, self.lanes), 1) // self.head_size
        self.slices = [slice(g * self.lanes, (g + 1) * self.lanes) for g in range(HEADS // PACK)]

    def spread(self, part):
        return jnp.concatenate([part] * PACK, 0) * self.own

    def gather(self, wide):
        result = wide[: self.cells]
        for h in range(1, PACK):
            result = jnp.where(self.lane_of == h, wide[h * self.cells : (h + 1) * self.cells], result)
        return result

    def probs(self, keys, wide_q):
        scores = [dot_nt(k, q) * self.factor for k, q in zip(keys, wide_q)]
        weights = [jnp.exp(s - jnp.max(s, 0, keepdims=True)) for s in scores]
        return [e * (1.0 / jnp.sum(e, 0, keepdims=True)) for e in weights]


def forward_kernel(slabs_ref, w_qkv_ref, w_out_ref, gain_ref, bias_ref, *refs):
    piece_refs = refs[:GRID]
    latent_ref, proj_ref, attended_ref, cells_ref = refs[GRID:]
    width = w_out_ref.shape[0]
    rows = latent_ref.shape[0] // STEPS
    to_windows(slabs_ref, cells_ref)
    for step in range(STEPS):
        at = slice(step * rows, (step + 1) * rows)
        latent = step_rows(cells_ref, step)
        latent_ref[at, :] = latent.astype(LOW)
        scaled, _ = norm_parts(latent)
        normed = (scaled * gain_ref[...] + bias_ref[...]).astype(LOW)
        proj_ref[at, :] = dot_nn(normed, w_qkv_ref[...]).astype(LOW)
    heads = Heads(width)

    def window(w, carry):
        at = pl.ds(pl.multiple_of(w * heads.cells, heads.cells), heads.cells)
        keys = [proj_ref[at, width + s.start : width + s.stop] for s in heads.slices]
        wide_q = [heads.spread(proj_ref[at, s]) for s in heads.slices]
        probs = [p.astype(LOW) for p in heads.probs(keys, wide_q)]
        for s, p in zip(heads.slices, probs):
            values = proj_ref[at, 2 * width + s.start : 2 * width + s.stop]
            attended_ref[at, s] = heads.gather(dot_tn(p, values)).astype(LOW)
        return carry

    lax.fori_loop(0, latent_ref.shape[0] // heads.cells, window, 0, unroll=UNROLL)
    for step in range(STEPS):
        at = slice(step * rows, (step + 1) * rows)
        value = step_rows(cells_ref, step) + dot_nn(attended_ref[at, :], w_out_ref[...])
        put_rows(cells_ref, step, value)
    spot = lax.axis_index("z")
    for shift in range(GRID):
        piece_refs[shift][...] = from_windows(cells_ref, lax.rem(spot + GRID - shift, GRID))


def backward_kernel(
    slabs_ref, latent_ref, proj_ref, attended_ref, w_qkv_ref, w_out_ref, gain_ref, bias_ref, *refs
):
    near_refs, piece_refs = refs[:2], refs[2 : 2 + GRID]
    keep_ref, send_ref, cells_ref, cot_ref, heads_ref, grad_ref, normed_ref = refs[2 + GRID :]
    width = w_out_ref.shape[0]
    rows = latent_ref.shape[0] // STEPS
    to_windows(slabs_ref, cells_ref)
    for step in range(STEPS):
        at = slice(step * rows, (step + 1) * rows)
        cot_ref[at, :] = step_rows(cells_ref, step).astype(LOW)
        heads_ref[at, :] = dot_nt(cot_ref[at, :], w_out_ref[...]).astype(LOW)
    heads = Heads(width)

    def window(w, carry):
        at = pl.ds(pl.multiple_of(w * heads.cells, heads.cells), heads.cells)
        keys = [proj_ref[at, width + s.start : width + s.stop] for s in heads.slices]
        values = [proj_ref[at, 2 * width + s.start : 2 * width + s.stop] for s in heads.slices]
        wide_q = [heads.spread(proj_ref[at, s]) for s in heads.slices]
        wide_g = [heads.spread(heads_ref[at, s]) for s in heads.slices]
        grad_probs = [dot_nt(v, g) for v, g in zip(values, wide_g)]
        probs = heads.probs(keys, wide_q)
        grad_scores = [
            (p * (d - jnp.sum(p * d, 0, keepdims=True))).astype(LOW)
            for p, d in zip(probs, grad_probs)
        ]
        for i, s in enumerate(heads.slices):
            grad_v = dot_nn(probs[i].astype(LOW), wide_g[i])
            grad_k = dot_nn(grad_scores[i], wide_q[i]) * heads.factor
            grad_q = heads.gather(dot_tn(grad_scores[i], keys[i])) * heads.factor
            for j, part in enumerate((grad_q, grad_k, grad_v)):
                grad_ref[at, j * width + s.start : j * width + s.stop] = part.astype(LOW)
        return carry

    lax.fori_loop(0, latent_ref.shape[0] // heads.cells, window, 0, unroll=UNROLL)
    gain_sum = jnp.zeros((1, width), jnp.float32)
    bias_sum = jnp.zeros((1, width), jnp.float32)
    for step in range(STEPS):
        at = slice(step * rows, (step + 1) * rows)
        scaled, inverse = norm_parts(latent_ref[at, :].astype(jnp.float32))
        normed_ref[at, :] = (scaled * gain_ref[...] + bias_ref[...]).astype(LOW)
        grad_normed = dot_nt(grad_ref[at, :], w_qkv_ref[...])
        gain_sum += jnp.sum(grad_normed * scaled, 0, keepdims=True)
        bias_sum += jnp.sum(grad_normed, 0, keepdims=True)
        grad_hat = grad_normed * gain_ref[...]
        value = step_rows(cells_ref, step) + inverse * (
            grad_hat
            - jnp.mean(grad_hat, -1, keepdims=True)
            - scaled * jnp.mean(grad_hat * scaled, -1, keepdims=True)
        )
        put_rows(cells_ref, step, value)
    spot = lax.axis_index("z")
    for shift in range(GRID):
        piece = from_windows(cells_ref, lax.rem(spot + GRID - shift, GRID))
        if shift in NEAR:
            piece_refs[shift][0] = near_refs[NEAR.index(shift)][...]
            piece_refs[shift][1] = piece
        else:
            piece_refs[shift][...] = piece
    norm = [s[:, i : i + 128] for s in (gain_sum, bias_sum) for i in range(0, width, 128)]
    norm = jnp.concatenate(norm, 0)
    high = norm.astype(LOW).astype(jnp.float32)
    norm = jnp.concatenate([high, norm - high], 0).astype(LOW)
    parts = [
        (0, dot_tn(normed_ref[...], grad_ref[...]).astype(LOW)),
        (3 * width, dot_tn(attended_ref[...], cot_ref[...]).astype(LOW)),
    ]
    planes, share, _ = keep_ref.shape
    core = lax.axis_index("core")
    for ref, core_at in ((keep_ref, core), (send_ref, 1 - core)):
        order = share_order(width, planes, core_at)
        for lo, part in parts:
            part = dot_nn(order, part).astype(LOW).reshape(planes, share, part.shape[1])
            ref[:, :, lo : lo + part.shape[2]] = part
        ref[:, :, 4 * width :] = jnp.broadcast_to(norm[None], (planes,) + norm.shape)


def share_order(width, planes, core):
    pair = width // (2 * planes * GRID)
    near = planes // 2
    row = lax.broadcasted_iota(jnp.int32, (width // 2, width), 0)
    col = lax.broadcasted_iota(jnp.int32, (width // 2, width), 1)
    plane = row // (pair * GRID)
    spot = row // pair % GRID
    source = (((plane // near * GRID + spot) * near + plane % near) * 2 + core) * pair + row % pair
    return jnp.where(col == source, 1.0, 0.0).astype(LOW)


def first_sum_kernel(shares_ref, out_ref):
    total = jnp.sum(shares_ref[...].astype(jnp.float32), 0)
    rows, wide = total.shape
    count = rows // GRID
    main = wide - 128
    norm = total[:GRID, main:] + total[GRID:, main:]
    high = norm.astype(LOW).astype(jnp.float32)
    rest = norm - high
    high = jnp.concatenate([high[i : i + 1] for i in range(GRID)], 1)
    rest = jnp.concatenate([rest[i : i + 1] for i in range(GRID)], 1)
    norm = jnp.concatenate([high, rest], 0).astype(LOW)
    out_ref[:, :, :main] = total[:, :main].reshape(GRID, count, main).astype(LOW)
    out_ref[:, :, main:] = jnp.broadcast_to(norm[None], (GRID,) + norm.shape)


def second_sum_kernel(shares_ref, qkv_ref, out_ref, norm_ref):
    total = jnp.sum(shares_ref[...].astype(jnp.float32), 0)
    width = norm_ref.shape[1]
    for row in range(total.shape[0]):
        qkv_ref[row * 3 * width : (row + 1) * 3 * width] = total[row, : 3 * width]
        out_ref[row * width : (row + 1) * width] = total[row, 3 * width : 4 * width]
    norm = total[0:1, 4 * width :] + total[1:2, 4 * width :]
    norm_ref[0:1, :] = norm[:, :width]
    norm_ref[1:2, :] = norm[:, width:]


def gather_kernel(*refs):
    spot = lax.axis_index("z")
    out_ref, grad_ref = refs[2 * GRID - 2 :]
    near = [refs[NEAR.index(shift)] if shift in NEAR else None for shift in range(GRID)]
    rest = list(refs[2 : 2 * GRID - 2])
    for shift in range(GRID):
        at = lax.rem(spot + shift, GRID)
        if shift in NEAR:
            out_ref[at] = near[shift][0]
            grad_ref[at] = near[shift][1]
        else:
            out_ref[at] = rest.pop(0)[...]
            grad_ref[at] = rest.pop(0)[...]


VMEM = pl.BlockSpec(memory_space=pltpu.VMEM)
SHAPE = jax.ShapeDtypeStruct


def call(kernel, name, out_shape, *args, scratch=(), flops=0, moved=0, exps=0, limit=SMALL_LIMIT):
    return pl.pallas_call(
        kernel,
        out_shape=out_shape,
        in_specs=[VMEM] * len(args),
        out_specs=jax.tree.map(lambda _: VMEM, out_shape),
        scratch_shapes=list(scratch),
        compiler_params=pltpu.CompilerParams(vmem_limit_bytes=limit),
        cost_estimate=pl.CostEstimate(flops=flops, bytes_accessed=moved, transcendentals=exps),
        name=name,
    )(*args)


def forward(slabs, w_qkv, w_out, gain, bias):
    spots, columns, width = slabs.shape
    tokens = spots * columns
    flops = 2 * tokens * width * (4 * width + 2 * GRID * GRID * PACK)
    return call(
        forward_kernel,
        "forward",
        [SHAPE((columns, width), LOW)] * spots
        + [
            SHAPE((tokens, width), LOW),
            SHAPE((tokens, 3 * width), LOW),
            SHAPE((tokens, width), LOW),
        ],
        slabs,
        w_qkv,
        w_out,
        gain,
        bias,
        scratch=[pltpu.VMEM((columns // GRID, spots, GRID, width), jnp.float32)],
        flops=flops,
        moved=10 * 2**20,
        exps=tokens * HEADS * GRID * GRID,
        limit=VMEM_LIMIT,
    )


def backward(slabs, saved, near, w_qkv, w_out, gain, bias, planes):
    spots, columns, width = slabs.shape
    tokens = spots * columns
    share = width // (2 * planes)
    wide = 4 * width + 128
    flops = 2 * tokens * width * (9 * width + 5 * GRID * GRID * PACK)
    results = call(
        backward_kernel,
        "backward",
        [
            SHAPE(((2,) if shift in NEAR else ()) + (columns, width), LOW)
            for shift in range(spots)
        ]
        + [SHAPE((planes, share, wide), LOW)] * 2,
        slabs,
        *saved,
        w_qkv,
        w_out,
        gain,
        bias,
        *near,
        scratch=[
            pltpu.VMEM((columns // GRID, spots, GRID, width), jnp.float32),
            pltpu.VMEM((tokens, width), LOW),
            pltpu.VMEM((tokens, width), LOW),
            pltpu.VMEM((tokens, 3 * width), LOW),
            pltpu.VMEM((tokens, width), LOW),
        ],
        flops=flops,
        moved=16 * 2**20,
        exps=tokens * HEADS * GRID * GRID,
        limit=VMEM_LIMIT,
    )
    return results[:spots], results[spots:]


def first_sum(shares):
    _, rows, wide = shares.shape
    result = SHAPE((GRID, rows // GRID, wide - 128 + GRID * 128), LOW)
    return call(first_sum_kernel, "first_sum", result, shares)


def second_sum(shares, width):
    _, rows, _ = shares.shape
    result = [
        SHAPE((rows * 3 * width,), jnp.float32),
        SHAPE((rows * width,), jnp.float32),
        SHAPE((2, width), jnp.float32),
    ]
    return call(second_sum_kernel, "second_sum", result, shares)


def gather_slabs(outs, grads):
    columns, width = outs[0].shape
    pairs = [part for shift in range(GRID) if shift not in NEAR for part in (outs[shift], grads[shift])]
    near = [grads[shift] for shift in NEAR]
    return call(gather_kernel, "gather_slabs", [SHAPE((GRID, columns, width), LOW)] * 2, *near, *pairs)


def swap(value, axes):
    return lax.all_to_all(value, axes, split_axis=0, concat_axis=0, tiled=True)


def turn(value, shift):
    if shift % GRID == 0:
        return value
    return lax.ppermute(value, "z", [(a, (a + shift) % GRID) for a in range(GRID)])


def add(a, b):
    return (a.astype(jnp.float32) + b.astype(jnp.float32)).astype(LOW)


def body(latent, cotangent, w_qkv, w_out, norm_gain, norm_bias):
    width = latent.shape[-1]
    planes = lax.axis_size("dp") * lax.axis_size("y") * lax.axis_size("x_hi")
    gain = norm_gain.reshape(1, width)
    bias = norm_bias.reshape(1, width)
    slabs, cotangent = lax.optimization_barrier((swap(latent[0], "z"), cotangent[0]))
    cotangent = swap(cotangent, "z")
    results = forward(slabs, w_qkv, w_out, gain, bias)
    outs, saved = list(results[:GRID]), results[GRID:]
    near = [outs[shift] for shift in NEAR]
    outs = [piece if shift in NEAR else turn(piece, -shift) for shift, piece in enumerate(outs)]
    grads, (keep, send) = backward(cotangent, saved, near, w_qkv, w_out, gain, bias, planes)
    outs, keep, send = lax.optimization_barrier((outs, keep, send))
    grads = [turn(piece, -shift) for shift, piece in enumerate(grads)]
    shares = add(keep, lax.ppermute(send, "core", [(0, 1), (1, 0)]))
    grads[2], grads[6], shares = lax.optimization_barrier((grads[2], grads[6], shares))
    shares = first_sum(swap(shares, ("dp", "y", "x_hi")))
    grads[3:6], shares = lax.optimization_barrier((grads[3:6], shares))
    grad_qkv, grad_out, grad_norm = second_sum(swap(shares, "z"), width)
    output, grad_input = gather_slabs(outs, grads)
    return (output[None], grad_input[None], grad_qkv, grad_out, grad_norm)


def solution(mesh):
    sizes = (mesh.shape["dp"], GRID, mesh.shape["space"] // GRID // 4, 2, 2)
    parts = jax.sharding.Mesh(mesh.devices.reshape(sizes), ("dp", "z", "y", "x_hi", "core"))
    space = ("z", "y", "x_hi", "core")
    in_specs = (P("dp", space, None, None), P("dp", space, None, None), P(), P(), P(), P())
    out_specs = (
        P("dp", space, None, None),
        P("dp", space, None, None),
        P(("dp",) + space),
        P(("dp",) + space),
        P(),
    )
    return jax.shard_map(body, mesh=parts, in_specs=in_specs, out_specs=out_specs, check_vma=False)
```

time: 646 us -> 148 us (0.23); the launches traced: 637 us -> 148 us
  waiting for transfers between devices: 331 us -> 27.7 us
  local copies, waits for them, and re-layouts: 104 us -> 0.98 us
  matrix products: 48.4 us -> 0 us
  blocking collectives: 76.5 us -> 37.3 us
  Pallas kernels: 0 us -> 37.6 us
  between operations: 14.5 us -> 0.75 us
  other arithmetic: 15 us -> 2.53 us
    unnamed x2 -> x0, waiting for transfers between devices: 179 us -> none
    all_to_all x4 -> x3, waiting for transfers between devices: 152 us -> 15.2 us  [swap(): return lax.all_to_all(value, axes, split_axis=0, concat_axis=0, tiled=True)]
    psum x1 -> x0, blocking collectives: 76.5 us -> none  [body(): grad_norm = lax.psum(term_norm, ('dp', 'space'))]
    dot_general x11 -> x0, matrix products: 39.6 us -> none  [the longest x1 6.68 us: window_pass(): jnp.einsum('bhqk,bkhd->bqhd', probs_low, values_all, preferred_element_ty...]
    pallas_call x0 -> x5, Pallas kernels: none -> 37.6 us  [call(): pl.pallas_call(kernel, out_shape=out_shape, in_specs=[VMEM] * len(args),...]
    all_to_all x0 -> x1, blocking collectives: none -> 37.3 us  [swap(): return lax.all_to_all(value, axes, split_axis=0, concat_axis=0, tiled=True)]
    all_to_all x4 -> x3, starting transfers between devices: 47.6 us -> 15.9 us  [swap(): return lax.all_to_all(value, axes, split_axis=0, concat_axis=0, tiled=True)]
    ppermute x0 -> x13, starting transfers between devices: none -> 25.3 us  [the longest x12 25.3 us: turn(): lax.ppermute(value, 'z', [(a, (a + shift) % GRID) for a in range(GRID)])]
  transfers between devices with their start and end apart: 5 -> 16, of which waited for: 4 -> 6; matrix products, arithmetic and copies ran while one was open for 15% -> 2% of each run, Pallas kernels for 0% -> 25%
where the time goes in v2:
time: 148 us
  starting transfers between devices  41.3 us (28%)
  Pallas kernels  37.6 us (25%)
  blocking collectives  37.3 us (25%)
  waiting for transfers between devices  27.7 us (19%)
  other arithmetic  2.53 us (2%)
    pallas_call x5, Pallas kernels, call(): pl.pallas_call(kernel, out_shape=out_shape, in_specs=[VMEM] * len(args),...  37.6 us
    all_to_all x1, blocking collectives, swap(): return lax.all_to_all(value, axes, split_axis=0, concat_axis=0, tiled=True)  37.3 us
    ppermute x12, starting transfers between devices, turn(): lax.ppermute(value, 'z', [(a, (a + shift) % GRID) for a in range(GRID)])  25.3 us
    all_to_all x3, starting transfers between devices, swap(): return lax.all_to_all(value, axes, split_axis=0, concat_axis=0, tiled=True)  15.9 us
    all_to_all x3, waiting for transfers between devices, swap(): return lax.all_to_all(value, axes, split_axis=0, concat_axis=0, tiled=True)  15.2 us
    ppermute x12, waiting for transfers between devices, turn(): lax.ppermute(value, 'z', [(a, (a + shift) % GRID) for a in range(GRID)])  12.5 us
  transfers between devices with their start and end apart: 16, of which 6 were waited for; matrix products, arithmetic and copies ran while one was open for 2% of the time, Pallas kernels for 25%

profile of v2, /device:TPU:2, one launch (start us, length us, event | category | flops | bytes accessed | tf_op | source)
XLA Modules:
  0.0 148.1 jit_solution(9495599497047475709)
XLA Ops:
  0.6 37.3 %all_to_all.20.slabs_ref = bf16[8,128,512]{2,1,0:T(8,128)(2,1)} all-to-all(bf16[8,128,512]{2,1,0:T(8,128)(2,1)} %bitcast.6), channel_id=1, replica_groups=mesh['dp'=2,'z'=8,'y'=4,'x_hi'=2,'core'=2] {'z'}, dimensions={0} | all-to-all | bytes 2097152 | tf_op jit(solution)/shard_map/all_to_all | solution.py:373
  37.9 3.6 %all-to-all-start.1 = ((bf16[8,128,512]{2,1,0:T(8,128)(2,1)}), bf16[8,128,512]{2,1,0:T(8,128)(2,1)S(1)}, u32[]{:S(2)}, u32[]{:S(2)}) async-start(bf16[8,128,512]{2,1,0:T(8,128)(2,1)} %bitcast.1), calls=%async_computation.1 | async-start | bytes 2097152 | tf_op jit(solution)/shard_map/all_to_all | solution.py:373
  41.5 14.0 %forward.1 = (bf16[128,512]{1,0:T(8,128)(2,1)}, bf16[128,512]{1,0:T(8,128)(2,1)}, bf16[128,512]{1,0:T(8,128)(2,1)}, bf16[128,512]{1,0:T(8,128)(2,1)}, bf16[128,5...) custom-call(bf16[8,128,512]{2,1,0:T(8,128)(2,1)} %all_to_all.20.slab, ...), custom_call_target="tpu_custom_call" | custom-call | flops 2684354560 | bytes 10485760 | tf_op jit(solution)/shard_map/forward/pallas_call | solution.py:275
  55.5 4.1 %collective-permute-start.2 = (bf16[128,512]{1,0:T(8,128)(2,1)}, bf16[128,512]{1,0:T(8,128)(2,1)S(1)}, u32[]{:S(2)}, u32[]{:S(2)}) collective-permute-start(bf16[128,512]{1,0:T(8,128)(2,1)} %get-tuple-element.58), channel_id=1, source_target_pairs={{0,96},{16,112},{32,0},{48,16},{64,32},{80,48},{96,64},{112,80},{1... | collective-permute-start | bytes 393224 | tf_op jit(solution)/shard_map/ppermute | solution.py:379
  59.6 2.3 %collective-permute-start.3 = (bf16[128,512]{1,0:T(8,128)(2,1)}, bf16[128,512]{1,0:T(8,128)(2,1)S(1)}, u32[]{:S(2)}, u32[]{:S(2)}) collective-permute-start(bf16[128,512]{1,0:T(8,128)(2,1)} %get-tuple-element.59), channel_id=1, source_target_pairs={{0,80},{16,96},{32,112},{48,0},{64,16},{80,32},{96,48},{112,64},{1... | collective-permute-start | bytes 393224 | tf_op jit(solution)/shard_map/ppermute | solution.py:379
  61.9 2.7 %collective-permute-start.4 = (bf16[128,512]{1,0:T(8,128)(2,1)}, bf16[128,512]{1,0:T(8,128)(2,1)S(1)}, u32[]{:S(2)}, u32[]{:S(2)}) collective-permute-start(bf16[128,512]{1,0:T(8,128)(2,1)} %get-tuple-element.60), channel_id=1, source_target_pairs={{0,64},{16,80},{32,96},{48,112},{64,0},{80,16},{96,32},{112,48},{1... | collective-permute-start | bytes 393224 | tf_op jit(solution)/shard_map/ppermute | solution.py:379
  64.6 1.1 collective-permute-start.5
  65.7 3.6 %collective-permute-start.6 = (bf16[128,512]{1,0:T(8,128)(2,1)}, bf16[128,512]{1,0:T(8,128)(2,1)S(1)}, u32[]{:S(2)}, u32[]{:S(2)}) collective-permute-start(bf16[128,512]{1,0:T(8,128)(2,1)} %get-tuple-element.62), channel_id=1, source_target_pairs={{0,32},{16,48},{32,64},{48,80},{64,96},{80,112},{96,0},{112,16},{1... | collective-permute-start | bytes 393224 | tf_op jit(solution)/shard_map/ppermute | solution.py:379
  69.3 0.4 all-to-all-done.1.slabs_ref
  69.8 0.0 copy-start.2
  69.8 1.0 copy-done.2
  70.7 20.5 %backward.1 = (bf16[128,512]{1,0:T(8,128)(2,1)}, bf16[2,128,512]{2,1,0:T(8,128)(2,1)}, bf16[128,512]{1,0:T(8,128)(2,1)}, bf16[128,512]{1,0:T(8,128)(2,1)}, bf16[...) custom-call(bf16[8,128,512]{2,1,0:T(8,128)(2,1)} %copy-done.2, ...), custom_call_target="tpu_custom_call" | custom-call | flops 6174015488 | bytes 16777216 | tf_op jit(solution)/shard_map/backward/pallas_call | solution.py:275
  91.3 0.0 collective-permute-done.2.refs_4_
  91.3 0.0 collective-permute-done.3.refs_6_
  91.3 0.0 collective-permute-done.4.refs_8_
  91.3 0.0 collective-permute-done.5.refs_10_
  91.3 0.0 collective-permute-done.6.refs_12_
  91.3 0.1 collective-permute-start.9
  91.4 3.7 %collective-permute-start.7 = (bf16[128,512]{1,0:T(8,128)(2,1)}, bf16[128,512]{1,0:T(8,128)(2,1)S(1)}, u32[]{:S(2)}, u32[]{:S(2)}) collective-permute-start(bf16[128,512]{1,0:T(8,128)(2,1)} %get-tuple-element.68), channel_id=1, source_target_pairs={{0,96},{16,112},{32,0},{48,16},{64,32},{80,48},{96,64},{112,80},{1... | collective-permute-start | bytes 393224 | tf_op jit(solution)/shard_map/ppermute | solution.py:379
  95.2 0.0 collective-permute-start.8
  95.2 0.0 collective-permute-done.9
  95.2 2.5 %add_convert_fusion = bf16[16,16,2176]{2,1,0:T(8,128)(2,1)} fusion(bf16[16,16,2176]{2,1,0:T(8,128)(2,1)S(1)} %collective-permute-done.9, bf16[16,16,2176]{2,1,0:T(8,128)(2,1)} %get-tuple-element.70), kind=kLoop, calls=%fused_computation | loop fusion | flops 2228224 | bytes 3342336 | tf_op jit(solution)/shard_map/convert_element_type | solution.py:383
  97.7 0.0 copy-start.3
  97.7 4.0 %collective-permute-done.7.refs_5_ = bf16[128,512]{1,0:T(8,128)(2,1)S(1)} collective-permute-done((bf16[128,512]{1,0:T(8,128)(2,1)}, bf16[128,512]{1,0:T(8,128)(2,1)S(1)}, u32[]{:S(2)}, u32[]{:S(2)}) %collective-permute-start.7) | collective-permute-done | bytes 131104 | tf_op jit(solution)/shard_map/ppermute | solution.py:379
  101.7 4.2 %collective-permute-done.8.refs_13_ = bf16[128,512]{1,0:T(8,128)(2,1)S(1)} collective-permute-done((bf16[128,512]{1,0:T(8,128)(2,1)}, bf16[128,512]{1,0:T(8,128)(2,1)S(1)}, u32[]{:S(2)}, u32[]{:S(2)}) %collective-permute-start.8) | collective-permute-done | bytes 131104 | tf_op jit(solution)/shard_map/ppermute | solution.py:379
  105.9 7.5 %all-to-all-start.2 = ((bf16[16,16,2176]{2,1,0:T(8,128)(2,1)}), bf16[16,16,2176]{2,1,0:T(8,128)(2,1)S(1)}, u32[]{:S(2)}, u32[]{:S(2)}) async-start(bf16[16,16,2176]{2,1,0:T(8,128)(2,1)} %add_convert_fusion), calls=%async_computation.2 | async-start | bytes 2228224 | tf_op jit(solution)/shard_map/all_to_all | solution.py:373
  113.4 0.0 copy-start
  113.4 0.0 copy-start.1
  113.4 0.1 collective-permute-start.10
  113.5 4.1 %collective-permute-start.11 = (bf16[128,512]{1,0:T(8,128)(2,1)}, bf16[128,512]{1,0:T(8,128)(2,1)S(1)}, u32[]{:S(2)}, u32[]{:S(2)}) collective-permute-start(bf16[128,512]{1,0:T(8,128)(2,1)} %get-tuple-element.75), channel_id=1, source_target_pairs={{0,64},{16,80},{32,96},{48,112},{64,0},{80,16},{96,32},{112,48},{1... | collective-permute-start | bytes 393224 | tf_op jit(solution)/shard_map/ppermute | solution.py:379
  117.6 0.0 collective-permute-start.12
  117.6 3.5 %collective-permute-start = (bf16[2,128,512]{2,1,0:T(8,128)(2,1)}, bf16[2,128,512]{2,1,0:T(8,128)(2,1)S(1)}, u32[]{:S(2)}, u32[]{:S(2)}) collective-permute-start(bf16[2,128,512]{2,1,0:T(8,128)(2,1)} %get-tuple-element.55), channel_id=1, source_target_pairs={{0,112},{16,0},{32,16},{48,32},{64,48},{80,64},{96,80},{112,96},{1... | collective-permute-start | bytes 786440 | tf_op jit(solution)/shard_map/ppermute | solution.py:379
  121.1 0.0 copy-done.3
  121.1 0.0 collective-permute-start.1
  121.1 7.5 %all-to-all-done.2.shares_ref = bf16[16,16,2176]{2,1,0:T(8,128)(2,1)S(1)} async-done(((bf16[16,16,2176]{2,1,0:T(8,128)(2,1)}), bf16[16,16,2176]{2,1,0:T(8,128)(2,1)S(1)}, u32[]{:S(2)}, u32[]{:S(2)}) %all-to-all-start.2) | async-done | bytes 1114144 | tf_op jit(solution)/shard_map/all_to_all | solution.py:373
  128.6 0.9 first_sum.1
  129.5 0.0 collective-permute-done.10.refs_7_
  129.5 0.0 collective-permute-done.11.refs_9_
  129.5 4.3 %collective-permute-done.12.refs_11_ = bf16[128,512]{1,0:T(8,128)(2,1)S(1)} collective-permute-done((bf16[128,512]{1,0:T(8,128)(2,1)}, bf16[128,512]{1,0:T(8,128)(2,1)S(1)}, u32[]{:S(2)}, u32[]{:S(2)}) %collective-permute-start.12) | collective-permute-done | bytes 131104 | tf_op jit(solution)/shard_map/ppermute | solution.py:379
  133.8 4.9 %all-to-all-start.3 = ((bf16[8,2,3072]{2,1,0:T(2,128)(2,1)}), bf16[8,2,3072]{2,1,0:T(2,128)(2,1)S(1)}, u32[]{:S(2)}, u32[]{:S(2)}) async-start(bf16[8,2,3072]{2,1,0:T(2,128)(2,1)} %first_sum.1), calls=%async_computation.3 | async-start | bytes 196608 | tf_op jit(solution)/shard_map/all_to_all | solution.py:373
  138.7 0.0 collective-permute-done.refs_0_
  138.7 0.0 collective-permute-done.1.refs_1_
  138.7 0.0 copy-done
  138.7 0.0 copy-done.1
  138.7 1.5 %gather_slabs.1 = (bf16[8,128,512]{2,1,0:T(8,128)(2,1)}, bf16[8,128,512]{2,1,0:T(8,128)(2,1)}) custom-call(bf16[2,128,512]{2,1,0:T(8,128)(2,1)S(1)} %collective-permute-done.refs_0_, bf16[2,128,512]{2,1,0:T(8,128)(2,1)S(1)} %collective-permute-done.1.refs_1_, bf16[128,512]{1,0:T(8,128)(2,1)S(1)} %copy-done, bf16[128,512]{1,0:T(8,128)(2,1)S(1)} %copy-done.1, ...), custom_call_target="tpu_custom_call" | custom-call | tf_op jit(solution)/shard_map/gather_slabs/pallas_call | solution.py:275
  140.2 7.2 %all-to-all-done.3.shares_ref = bf16[8,2,3072]{2,1,0:T(2,128)(2,1)S(1)} async-done(((bf16[8,2,3072]{2,1,0:T(2,128)(2,1)}), bf16[8,2,3072]{2,1,0:T(2,128)(2,1)S(1)}, u32[]{:S(2)}, u32[]{:S(2)}) %all-to-all-start.3) | async-done | bytes 98336 | tf_op jit(solution)/shard_map/all_to_all | solution.py:373
  147.4 0.7 second_sum.1
Async XLA Ops:
  37.9 31.8 %all-to-all-start.1 = ((bf16[8,128,512]{2,1,0:T(8,128)(2,1)}), bf16[8,128,512]{2,1,0:T(8,128)(2,1)S(1)}, u32[]{:S(2)}, u32[]{:S(2)}) async-start(bf16[8,128,512]{2,1,0:T(8,128)(2,1)} %bitcast.1), calls=%async_computation.1 | async-start | bytes 2097152 | tf_op jit(solution)/shard_map/all_to_all | solution.py:373
  55.5 35.8 %collective-permute-start.2 = (bf16[128,512]{1,0:T(8,128)(2,1)}, bf16[128,512]{1,0:T(8,128)(2,1)S(1)}, u32[]{:S(2)}, u32[]{:S(2)}) collective-permute-start(bf16[128,512]{1,0:T(8,128)(2,1)} %get-tuple-element.58), channel_id=1, source_target_pairs={{0,96},{16,112},{32,0},{48,16},{64,32},{80,48},{96,64},{112,80},{1... | collective-permute-start | bytes 393224 | tf_op jit(solution)/shard_map/ppermute | solution.py:379
  59.6 31.7 %collective-permute-start.3 = (bf16[128,512]{1,0:T(8,128)(2,1)}, bf16[128,512]{1,0:T(8,128)(2,1)S(1)}, u32[]{:S(2)}, u32[]{:S(2)}) collective-permute-start(bf16[128,512]{1,0:T(8,128)(2,1)} %get-tuple-element.59), channel_id=1, source_target_pairs={{0,80},{16,96},{32,112},{48,0},{64,16},{80,32},{96,48},{112,64},{1... | collective-permute-start | bytes 393224 | tf_op jit(solution)/shard_map/ppermute | solution.py:379
  61.9 29.4 %collective-permute-start.4 = (bf16[128,512]{1,0:T(8,128)(2,1)}, bf16[128,512]{1,0:T(8,128)(2,1)S(1)}, u32[]{:S(2)}, u32[]{:S(2)}) collective-permute-start(bf16[128,512]{1,0:T(8,128)(2,1)} %get-tuple-element.60), channel_id=1, source_target_pairs={{0,64},{16,80},{32,96},{48,112},{64,0},{80,16},{96,32},{112,48},{1... | collective-permute-start | bytes 393224 | tf_op jit(solution)/shard_map/ppermute | solution.py:379
  64.6 26.7 %collective-permute-start.5 = (bf16[128,512]{1,0:T(8,128)(2,1)}, bf16[128,512]{1,0:T(8,128)(2,1)S(1)}, u32[]{:S(2)}, u32[]{:S(2)}) collective-permute-start(bf16[128,512]{1,0:T(8,128)(2,1)} %get-tuple-element.61), channel_id=1, source_target_pairs={{0,48},{16,64},{32,80},{48,96},{64,112},{80,0},{96,16},{112,32},{1... | collective-permute-start | bytes 393224 | tf_op jit(solution)/shard_map/ppermute | solution.py:379
  65.7 25.6 %collective-permute-start.6 = (bf16[128,512]{1,0:T(8,128)(2,1)}, bf16[128,512]{1,0:T(8,128)(2,1)S(1)}, u32[]{:S(2)}, u32[]{:S(2)}) collective-permute-start(bf16[128,512]{1,0:T(8,128)(2,1)} %get-tuple-element.62), channel_id=1, source_target_pairs={{0,32},{16,48},{32,64},{48,80},{64,96},{80,112},{96,0},{112,16},{1... | collective-permute-start | bytes 393224 | tf_op jit(solution)/shard_map/ppermute | solution.py:379
  69.8 1.0 copy-start.2
  91.3 3.9 %collective-permute-start.9 = (bf16[16,16,2176]{2,1,0:T(8,128)(2,1)}, bf16[16,16,2176]{2,1,0:T(8,128)(2,1)S(1)}, u32[]{:S(2)}, u32[]{:S(2)}) collective-permute-start(bf16[16,16,2176]{2,1,0:T(8,128)(2,1)} %get-tuple-element.71), channel_id=1, source_target_pairs={{0,1},{1,0},{2,3},{3,2},{4,5},{5,4},{6,7},{7,6},{8,9},{9,8},{10,11... | collective-permute-start | bytes 3342344 | tf_op jit(solution)/shard_map/ppermute | solution.py:400
  91.4 10.3 %collective-permute-start.7 = (bf16[128,512]{1,0:T(8,128)(2,1)}, bf16[128,512]{1,0:T(8,128)(2,1)S(1)}, u32[]{:S(2)}, u32[]{:S(2)}) collective-permute-start(bf16[128,512]{1,0:T(8,128)(2,1)} %get-tuple-element.68), channel_id=1, source_target_pairs={{0,96},{16,112},{32,0},{48,16},{64,32},{80,48},{96,64},{112,80},{1... | collective-permute-start | bytes 393224 | tf_op jit(solution)/shard_map/ppermute | solution.py:379
  95.2 10.7 %collective-permute-start.8 = (bf16[128,512]{1,0:T(8,128)(2,1)}, bf16[128,512]{1,0:T(8,128)(2,1)S(1)}, u32[]{:S(2)}, u32[]{:S(2)}) collective-permute-start(bf16[128,512]{1,0:T(8,128)(2,1)} %get-tuple-element.69), channel_id=1, source_target_pairs={{0,32},{16,48},{32,64},{48,80},{64,96},{80,112},{96,0},{112,16},{1... | collective-permute-start | bytes 393224 | tf_op jit(solution)/shard_map/ppermute | solution.py:379
  97.7 23.4 %copy-start.3 = (bf16[2,128,512]{2,1,0:T(8,128)(2,1)S(1)}, bf16[2,128,512]{2,1,0:T(8,128)(2,1)}, u32[]{:S(2)}) copy-start(bf16[2,128,512]{2,1,0:T(8,128)(2,1)} %get-tuple-element.56) | copy-start | bytes 786436
  105.9 22.7 %all-to-all-start.2 = ((bf16[16,16,2176]{2,1,0:T(8,128)(2,1)}), bf16[16,16,2176]{2,1,0:T(8,128)(2,1)S(1)}, u32[]{:S(2)}, u32[]{:S(2)}) async-start(bf16[16,16,2176]{2,1,0:T(8,128)(2,1)} %add_convert_fusion), calls=%async_computation.2 | async-start | bytes 2228224 | tf_op jit(solution)/shard_map/all_to_all | solution.py:373
  113.4 25.3 %copy-start = (bf16[128,512]{1,0:T(8,128)(2,1)S(1)}, bf16[128,512]{1,0:T(8,128)(2,1)}, u32[]{:S(2)}) copy-start(bf16[128,512]{1,0:T(8,128)(2,1)} %get-tuple-element.65.refs_2_) | copy-start | bytes 393220
  113.4 25.3 %copy-start.1 = (bf16[128,512]{1,0:T(8,128)(2,1)S(1)}, bf16[128,512]{1,0:T(8,128)(2,1)}, u32[]{:S(2)}) copy-start(bf16[128,512]{1,0:T(8,128)(2,1)} %get-tuple-element.66.refs_3_) | copy-start | bytes 393220
  113.4 16.1 %collective-permute-start.10 = (bf16[128,512]{1,0:T(8,128)(2,1)}, bf16[128,512]{1,0:T(8,128)(2,1)S(1)}, u32[]{:S(2)}, u32[]{:S(2)}) collective-permute-start(bf16[128,512]{1,0:T(8,128)(2,1)} %get-tuple-element.74), channel_id=1, source_target_pairs={{0,80},{16,96},{32,112},{48,0},{64,16},{80,32},{96,48},{112,64},{1... | collective-permute-start | bytes 393224 | tf_op jit(solution)/shard_map/ppermute | solution.py:379
  113.5 16.0 %collective-permute-start.11 = (bf16[128,512]{1,0:T(8,128)(2,1)}, bf16[128,512]{1,0:T(8,128)(2,1)S(1)}, u32[]{:S(2)}, u32[]{:S(2)}) collective-permute-start(bf16[128,512]{1,0:T(8,128)(2,1)} %get-tuple-element.75), channel_id=1, source_target_pairs={{0,64},{16,80},{32,96},{48,112},{64,0},{80,16},{96,32},{112,48},{1... | collective-permute-start | bytes 393224 | tf_op jit(solution)/shard_map/ppermute | solution.py:379
  117.6 16.2 %collective-permute-start.12 = (bf16[128,512]{1,0:T(8,128)(2,1)}, bf16[128,512]{1,0:T(8,128)(2,1)S(1)}, u32[]{:S(2)}, u32[]{:S(2)}) collective-permute-start(bf16[128,512]{1,0:T(8,128)(2,1)} %get-tuple-element.76), channel_id=1, source_target_pairs={{0,48},{16,64},{32,80},{48,96},{64,112},{80,0},{96,16},{112,32},{1... | collective-permute-start | bytes 393224 | tf_op jit(solution)/shard_map/ppermute | solution.py:379
  117.6 21.1 %collective-permute-start = (bf16[2,128,512]{2,1,0:T(8,128)(2,1)}, bf16[2,128,512]{2,1,0:T(8,128)(2,1)S(1)}, u32[]{:S(2)}, u32[]{:S(2)}) collective-permute-start(bf16[2,128,512]{2,1,0:T(8,128)(2,1)} %get-tuple-element.55), channel_id=1, source_target_pairs={{0,112},{16,0},{32,16},{48,32},{64,48},{80,64},{96,80},{112,96},{1... | collective-permute-start | bytes 786440 | tf_op jit(solution)/shard_map/ppermute | solution.py:379
  121.1 17.6 %collective-permute-start.1 = (bf16[2,128,512]{2,1,0:T(8,128)(2,1)S(1)}, bf16[2,128,512]{2,1,0:T(8,128)(2,1)S(1)}, u32[]{:S(2)}, u32[]{:S(2)}) collective-permute-start(bf16[2,128,512]{2,1,0:T(8,128)(2,1)S(1)} %copy-done.3), channel_id=1, source_target_pairs={{0,16},{16,32},{32,48},{48,64},{64,80},{80,96},{96,112},{112,0},{1... | collective-permute-start | bytes 786440 | tf_op jit(solution)/shard_map/ppermute | solution.py:379
  133.8 13.6 %all-to-all-start.3 = ((bf16[8,2,3072]{2,1,0:T(2,128)(2,1)}), bf16[8,2,3072]{2,1,0:T(2,128)(2,1)S(1)}, u32[]{:S(2)}, u32[]{:S(2)}) async-start(bf16[8,2,3072]{2,1,0:T(2,128)(2,1)} %first_sum.1), calls=%async_computation.3 | async-start | bytes 196608 | tf_op jit(solution)/shard_map/all_to_all | solution.py:373

commit v3 on v2

--- a/solution.py
+++ b/solution.py
@@ -12,11 +12,10 @@
 GRID = 8
 STEPS = 2
 PACK = 4
-UNROLL = 4
+UNROLL = 8
 VMEM_LIMIT = 56 * 1024 * 1024
 SMALL_LIMIT = 12 * 1024 * 1024
 LOW = jnp.bfloat16
-NEAR = (1, 7)
 
 
 def dot_nn(a, b):
@@ -141,15 +140,29 @@
 def backward_kernel(
     slabs_ref, latent_ref, proj_ref, attended_ref, w_qkv_ref, w_out_ref, gain_ref, bias_ref, *refs
 ):
-    near_refs, piece_refs = refs[:2], refs[2 : 2 + GRID]
-    keep_ref, send_ref, cells_ref, cot_ref, heads_ref, grad_ref, normed_ref = refs[2 + GRID :]
+    hbm_refs = (slabs_ref, w_out_ref, proj_ref, latent_ref, w_qkv_ref, attended_ref)
+    out_hbm_ref, keep_hbm_ref, send_hbm_ref = refs[:3]
+    cells_ref, cot_ref, heads_ref, grad_ref, normed_ref = refs[3:8]
+    vmem_refs = refs[8:14]
+    out_ref, keep_ref, send_ref, in_sems, out_sems = refs[14:]
+    slabs_ref, w_out_ref, proj_ref, latent_ref, w_qkv_ref, attended_ref = vmem_refs
+    loads = [
+        pltpu.make_async_copy(source, target, in_sems.at[i])
+        for i, (source, target) in enumerate(zip(hbm_refs, vmem_refs))
+    ]
+    for load in loads:
+        load.start()
+    slabs_load, w_out_load, proj_load, latent_load, w_qkv_load, attended_load = loads
     width = w_out_ref.shape[0]
     rows = latent_ref.shape[0] // STEPS
+    slabs_load.wait()
     to_windows(slabs_ref, cells_ref)
+    w_out_load.wait()
     for step in range(STEPS):
         at = slice(step * rows, (step + 1) * rows)
         cot_ref[at, :] = step_rows(cells_ref, step).astype(LOW)
         heads_ref[at, :] = dot_nt(cot_ref[at, :], w_out_ref[...]).astype(LOW)
+    proj_load.wait()
     heads = Heads(width)
 
     def window(w, carry):
@@ -173,6 +186,8 @@
         return carry
 
     lax.fori_loop(0, latent_ref.shape[0] // heads.cells, window, 0, unroll=UNROLL)
+    latent_load.wait()
+    w_qkv_load.wait()
     gain_sum = jnp.zeros((1, width), jnp.float32)
     bias_sum = jnp.zeros((1, width), jnp.float32)
     for step in range(STEPS):
@@ -189,14 +204,11 @@
             - scaled * jnp.mean(grad_hat * scaled, -1, keepdims=True)
         )
         put_rows(cells_ref, step, value)
-    spot = lax.axis_index("z")
-    for shift in range(GRID):
-        piece = from_windows(cells_ref, lax.rem(spot + GRID - shift, GRID))
-        if shift in NEAR:
-            piece_refs[shift][0] = near_refs[NEAR.index(shift)][...]
-            piece_refs[shift][1] = piece
-        else:
-            piece_refs[shift][...] = piece
+    for a in range(GRID):
+        out_ref[a] = from_windows(cells_ref, a)
+    out_store = pltpu.make_async_copy(out_ref, out_hbm_ref, out_sems.at[0])
+    out_store.start()
+    attended_load.wait()
     norm = [s[:, i : i + 128] for s in (gain_sum, bias_sum) for i in range(0, width, 128)]
     norm = jnp.concatenate(norm, 0)
     high = norm.astype(LOW).astype(jnp.float32)
@@ -207,37 +219,83 @@
     ]
     planes, share, _ = keep_ref.shape
     core = lax.axis_index("core")
-    for ref, core_at in ((keep_ref, core), (send_ref, 1 - core)):
+    stores = [out_store]
+    for ref, target, core_at in ((send_ref, send_hbm_ref, 1 - core), (keep_ref, keep_hbm_ref, core)):
         order = share_order(width, planes, core_at)
         for lo, part in parts:
             part = dot_nn(order, part).astype(LOW).reshape(planes, share, part.shape[1])
             ref[:, :, lo : lo + part.shape[2]] = part
         ref[:, :, 4 * width :] = jnp.broadcast_to(norm[None], (planes,) + norm.shape)
+        stores.append(pltpu.make_async_copy(ref, target, out_sems.at[len(stores)]))
+        stores[-1].start()
+    for store in stores:
+        store.wait()
 
 
 def share_order(width, planes, core):
     pair = width // (2 * planes * GRID)
-    near = planes // 2
+    ring = planes // 4
     row = lax.broadcasted_iota(jnp.int32, (width // 2, width), 0)
     col = lax.broadcasted_iota(jnp.int32, (width // 2, width), 1)
     plane = row // (pair * GRID)
     spot = row // pair % GRID
-    source = (((plane // near * GRID + spot) * near + plane % near) * 2 + core) * pair + row % pair
+    x = (plane // ring + here_x()) % 4
+    y = (plane % ring + lax.axis_index("y")) % ring
+    source = ((((x % 2 * GRID + spot) * ring + y) * 2 + x // 2) * 2 + core) * pair + row % pair
     return jnp.where(col == source, 1.0, 0.0).astype(LOW)
 
 
-def first_sum_kernel(shares_ref, out_ref):
-    total = jnp.sum(shares_ref[...].astype(jnp.float32), 0)
-    rows, wide = total.shape
-    count = rows // GRID
+def here_x():
+    return lax.axis_index("x_hi") * 2 + lax.axis_index("dp")
+
+
+def split_norm(norm):
+    high = norm.astype(LOW).astype(jnp.float32)
+    return high, norm - high
+
+
+def norm_total(refs, place, here):
+    tiles = [ref[place].astype(jnp.float32) for ref in refs]
+    tiles = [tile[:GRID] + tile[GRID:] for tile in tiles]
+    total = None
+    for at in range(len(refs)):
+        back = lax.rem(here + len(refs) - at, len(refs))
+        part = sum(jnp.where(back == s, tile, 0.0) for s, tile in enumerate(tiles))
+        total = part if total is None else total + part
+    return total
+
+
+def core_sum_kernel(keep_ref, got_ref, *out_refs):
+    ring = out_refs[0].shape[0]
+    for s, out_ref in enumerate(out_refs):
+        place = slice(s * ring, (s + 1) * ring)
+        out_ref[...] = (
+            keep_ref[place].astype(jnp.float32) + got_ref[place].astype(jnp.float32)
+        ).astype(LOW)
+
+
+def x_sum_kernel(*refs):
+    refs, out_refs = refs[:4], refs[4:]
+    main = refs[0].shape[2] - 128
+    norm = norm_total(refs, (0, slice(None), slice(main, main + 128)), here_x())
+    norm = jnp.concatenate(split_norm(norm), 0).astype(LOW)
+    for t, out_ref in enumerate(out_refs):
+        total = sum(ref[t, :, :main].astype(jnp.float32) for ref in refs)
+        out_ref[:, :main] = total.astype(LOW)
+        out_ref[:, main:] = norm
+
+
+def y_sum_kernel(*refs):
+    refs, out_ref = refs[:-1], refs[-1]
+    rows, wide = refs[0].shape
     main = wide - 128
-    norm = total[:GRID, main:] + total[GRID:, main:]
-    high = norm.astype(LOW).astype(jnp.float32)
-    rest = norm - high
-    high = jnp.concatenate([high[i : i + 1] for i in range(GRID)], 1)
-    rest = jnp.concatenate([rest[i : i + 1] for i in range(GRID)], 1)
-    norm = jnp.concatenate([high, rest], 0).astype(LOW)
-    out_ref[:, :, :main] = total[:, :main].reshape(GRID, count, main).astype(LOW)
+    total = sum(ref[:, :main].astype(jnp.float32) for ref in refs)
+    norm = norm_total(refs, (slice(None), slice(main, wide)), lax.axis_index("y"))
+    norm = [
+        jnp.concatenate([part[i : i + 1] for i in range(GRID)], 1) for part in split_norm(norm)
+    ]
+    norm = jnp.concatenate(norm, 0).astype(LOW)
+    out_ref[:, :, :main] = total.reshape(GRID, rows // GRID, main).astype(LOW)
     out_ref[:, :, main:] = jnp.broadcast_to(norm[None], (GRID,) + norm.shape)
 
 
@@ -253,30 +311,24 @@
 
 
 def gather_kernel(*refs):
+    slabs_ref, out_ref, copy_ref = refs[GRID:]
     spot = lax.axis_index("z")
-    out_ref, grad_ref = refs[2 * GRID - 2 :]
-    near = [refs[NEAR.index(shift)] if shift in NEAR else None for shift in range(GRID)]
-    rest = list(refs[2 : 2 * GRID - 2])
     for shift in range(GRID):
-        at = lax.rem(spot + shift, GRID)
-        if shift in NEAR:
-            out_ref[at] = near[shift][0]
-            grad_ref[at] = near[shift][1]
-        else:
-            out_ref[at] = rest.pop(0)[...]
-            grad_ref[at] = rest.pop(0)[...]
+        out_ref[lax.rem(spot + shift, GRID)] = refs[shift][...]
+    copy_ref[...] = slabs_ref[...]
 
 
 VMEM = pl.BlockSpec(memory_space=pltpu.VMEM)
+ANY = pl.BlockSpec(memory_space=pl.ANY)
 SHAPE = jax.ShapeDtypeStruct
 
 
-def call(kernel, name, out_shape, *args, scratch=(), flops=0, moved=0, exps=0, limit=SMALL_LIMIT):
+def call(kernel, name, out_shape, *args, scratch=(), flops=0, moved=0, exps=0, limit=SMALL_LIMIT, in_specs=None, out_specs=None):
     return pl.pallas_call(
         kernel,
         out_shape=out_shape,
-        in_specs=[VMEM] * len(args),
-        out_specs=jax.tree.map(lambda _: VMEM, out_shape),
+        in_specs=in_specs or [VMEM] * len(args),
+        out_specs=out_specs or jax.tree.map(lambda _: VMEM, out_shape),
         scratch_shapes=list(scratch),
         compiler_params=pltpu.CompilerParams(vmem_limit_bytes=limit),
         cost_estimate=pl.CostEstimate(flops=flops, bytes_accessed=moved, transcendentals=exps),
@@ -310,7 +362,7 @@
     )
 
 
-def backward(slabs, saved, near, w_qkv, w_out, gain, bias, planes):
+def backward(slabs, saved, w_qkv, w_out, gain, bias, planes):
     spots, columns, width = slabs.shape
     tokens = spots * columns
     share = width // (2 * planes)
@@ -319,10 +371,7 @@
     results = call(
         backward_kernel,
         "backward",
-        [
-            SHAPE(((2,) if shift in NEAR else ()) + (columns, width), LOW)
-            for shift in range(spots)
-        ]
+        [SHAPE(slabs.shape, LOW)]
         + [SHAPE((planes, share, wide), LOW)] * 2,
         slabs,
         *saved,
@@ -330,26 +379,48 @@
         w_out,
         gain,
         bias,
-        *near,
         scratch=[
             pltpu.VMEM((columns // GRID, spots, GRID, width), jnp.float32),
             pltpu.VMEM((tokens, width), LOW),
             pltpu.VMEM((tokens, width), LOW),
             pltpu.VMEM((tokens, 3 * width), LOW),
             pltpu.VMEM((tokens, width), LOW),
+            pltpu.VMEM(slabs.shape, LOW),
+            pltpu.VMEM(w_out.shape, LOW),
+            pltpu.VMEM((tokens, 3 * width), LOW),
+            pltpu.VMEM((tokens, width), LOW),
+            pltpu.VMEM(w_qkv.shape, LOW),
+            pltpu.VMEM((tokens, width), LOW),
+            pltpu.VMEM(slabs.shape, LOW),
+            pltpu.VMEM((planes, share, wide), LOW),
+            pltpu.VMEM((planes, share, wide), LOW),
+            pltpu.SemaphoreType.DMA((6,)),
+            pltpu.SemaphoreType.DMA((3,)),
         ],
+        in_specs=[ANY] * 6 + [VMEM] * 2,
+        out_specs=[ANY] * 3,
         flops=flops,
         moved=16 * 2**20,
         exps=tokens * HEADS * GRID * GRID,
         limit=VMEM_LIMIT,
     )
-    return results[:spots], results[spots:]
-
-
-def first_sum(shares):
-    _, rows, wide = shares.shape
+    return results
+
+
+def core_sum(keep, got):
+    planes, rows, wide = keep.shape
+    return call(core_sum_kernel, "core_sum", [SHAPE((planes // 4, rows, wide), LOW)] * 4, keep, got)
+
+
+def x_sum(parts):
+    ring, rows, wide = parts[0].shape
+    return call(x_sum_kernel, "x_sum", [SHAPE((rows, wide), LOW)] * ring, *parts)
+
+
+def y_sum(parts):
+    rows, wide = parts[0].shape
     result = SHAPE((GRID, rows // GRID, wide - 128 + GRID * 128), LOW)
-    return call(first_sum_kernel, "first_sum", result, shares)
+    return call(y_sum_kernel, "y_sum", result, *parts)
 
 
 def second_sum(shares, width):
@@ -362,11 +433,8 @@
     return call(second_sum_kernel, "second_sum", result, shares)
 
 
-def gather_slabs(outs, grads):
-    columns, width = outs[0].shape
-    pairs = [part for shift in range(GRID) if shift not in NEAR for part in (outs[shift], grads[shift])]
-    near = [grads[shift] for shift in NEAR]
-    return call(gather_kernel, "gather_slabs", [SHAPE((GRID, columns, width), LOW)] * 2, *near, *pairs)
+def gather_slabs(pieces, slabs):
+    return call(gather_kernel, "gather_slabs", [SHAPE(slabs.shape, LOW)] * 2, *pieces, slabs)
 
 
 def swap(value, axes):
@@ -379,8 +447,10 @@
     return lax.ppermute(value, "z", [(a, (a + shift) % GRID) for a in range(GRID)])
 
 
-def add(a, b):
-    return (a.astype(jnp.float32) + b.astype(jnp.float32)).astype(LOW)
+def ring_parts(parts, axes, place=lambda at: at):
+    size = len(parts)
+    pairs = [[(place(a), place((a + s) % size)) for a in range(size)] for s in range(size)]
+    return [part if s == 0 else lax.ppermute(part, axes, pairs[s]) for s, part in enumerate(parts)]
 
 
 def body(latent, cotangent, w_qkv, w_out, norm_gain, norm_bias):
@@ -392,17 +462,17 @@
     cotangent = swap(cotangent, "z")
     results = forward(slabs, w_qkv, w_out, gain, bias)
     outs, saved = list(results[:GRID]), results[GRID:]
-    near = [outs[shift] for shift in NEAR]
-    outs = [piece if shift in NEAR else turn(piece, -shift) for shift, piece in enumerate(outs)]
-    grads, (keep, send) = backward(cotangent, saved, near, w_qkv, w_out, gain, bias, planes)
-    outs, keep, send = lax.optimization_barrier((outs, keep, send))
-    grads = [turn(piece, -shift) for shift, piece in enumerate(grads)]
-    shares = add(keep, lax.ppermute(send, "core", [(0, 1), (1, 0)]))
-    grads[2], grads[6], shares = lax.optimization_barrier((grads[2], grads[6], shares))
-    shares = first_sum(swap(shares, ("dp", "y", "x_hi")))
-    grads[3:6], shares = lax.optimization_barrier((grads[3:6], shares))
+    outs = [turn(piece, -shift) for shift, piece in enumerate(outs)]
+    grad_input, keep, send = backward(cotangent, saved, w_qkv, w_out, gain, bias, planes)
+    outs[2:7], grad_input, keep, send = lax.optimization_barrier((outs[2:7], grad_input, keep, send))
+    grad_input = swap(grad_input, "z")
+    parts = core_sum(keep, lax.ppermute(send, "core", [(0, 1), (1, 0)]))
+    parts = x_sum(ring_parts(parts, ("dp", "x_hi"), lambda x: x % 2 * 2 + x // 2))
+    outs[1], outs[7], parts = lax.optimization_barrier((outs[1], outs[7], parts))
+    shares = y_sum(ring_parts(parts, "y"))
+    grad_input, shares = lax.optimization_barrier((grad_input, shares))
     grad_qkv, grad_out, grad_norm = second_sum(swap(shares, "z"), width)
-    output, grad_input = gather_slabs(outs, grads)
+    output, grad_input = gather_slabs(outs, grad_input)
     return (output[None], grad_input[None], grad_qkv, grad_out, grad_norm)
 
 

time: 148 us -> 144 us (0.973)
  waiting for transfers between devices: 27.7 us -> 24 us
  starting transfers between devices: 41.3 us -> 44.8 us
  other arithmetic: 2.53 us -> 0 us
  Pallas kernels: 37.6 us -> 35.8 us
    ppermute x1 -> x7, waiting for transfers between devices: 0.01 us -> 14.8 us  [the longest x6 11.9 us: ring_parts(): lax.ppermute(part, axes, pairs[s])]
    ppermute x12 -> x7, waiting for transfers between devices: 12.5 us -> 1.3 us  [turn(): lax.ppermute(value, 'z', [(a, (a + shift) % GRID) for a in range(GRID)])]
    ppermute x1 -> x7, starting transfers between devices: 0.09 us -> 10.7 us  [the longest x6 10.6 us: ring_parts(): lax.ppermute(part, axes, pairs[s])]
    ppermute x12 -> x7, starting transfers between devices: 25.3 us -> 16.9 us  [turn(): lax.ppermute(value, 'z', [(a, (a + shift) % GRID) for a in range(GRID)])]
    all_to_all x3, waiting for transfers between devices: 15.2 us -> 7.88 us  [swap(): return lax.all_to_all(value, axes, split_axis=0, concat_axis=0, tiled=True)]
    convert_element_type x1 -> x0, other arithmetic: 2.53 us -> none  [add(): return (a.astype(jnp.float32) + b.astype(jnp.float32)).astype(LOW)]
    pallas_call x5 -> x7, Pallas kernels: 37.6 us -> 35.8 us  [call(): pl.pallas_call(kernel, out_shape=out_shape, in_specs=in_specs or [VMEM] *...]
  transfers between devices with their start and end apart: 16 -> 17, of which waited for: 6 -> 9; matrix products, arithmetic and copies ran while one was open for 2% -> 0% of each run, Pallas kernels for 25% -> 24%
where the time goes in v3:
time: 144 us
  starting transfers between devices  44.8 us (31%)
  blocking collectives  37.3 us (26%)
  Pallas kernels  35.8 us (25%)
  waiting for transfers between devices  24 us (17%)
    all_to_all x1, blocking collectives, swap(): return lax.all_to_all(value, axes, split_axis=0, concat_axis=0, tiled=True)  37.3 us
    pallas_call x7, Pallas kernels, call(): pl.pallas_call(kernel, out_shape=out_shape, in_specs=in_specs or [VMEM] *...  35.8 us
    all_to_all x3, starting transfers between devices, swap(): return lax.all_to_all(value, axes, split_axis=0, concat_axis=0, tiled=True)  17.1 us
    ppermute x7, starting transfers between devices, turn(): lax.ppermute(value, 'z', [(a, (a + shift) % GRID) for a in range(GRID)])  16.9 us
    ppermute x6, waiting for transfers between devices, ring_parts(): lax.ppermute(part, axes, pairs[s])  11.9 us
    ppermute x6, starting transfers between devices, ring_parts(): lax.ppermute(part, axes, pairs[s])  10.6 us
    all_to_all x3, waiting for transfers between devices, swap(): return lax.all_to_all(value, axes, split_axis=0, concat_axis=0, tiled=True)  7.88 us
    ppermute x1, waiting for transfers between devices, body(): parts = core_sum(keep, lax.ppermute(send, 'core', [(0, 1), (1, 0)]))  2.95 us
  transfers between devices with their start and end apart: 17, of which 9 were waited for; matrix products, arithmetic and copies ran while one was open for 0% of the time, Pallas kernels for 24%

profile of v3, /device:TPU:2, one launch (start us, length us, event | category | flops | bytes accessed | tf_op | source)
XLA Modules:
  0.0 143.6 jit_solution(357067326728459447)
XLA Ops:
  0.6 37.3 %all_to_all.20.slabs_ref = bf16[8,128,512]{2,1,0:T(8,128)(2,1)} all-to-all(bf16[8,128,512]{2,1,0:T(8,128)(2,1)} %bitcast.6), channel_id=1, replica_groups=mesh['dp'=2,'z'=8,'y'=4,'x_hi'=2,'core'=2] {'z'}, dimensions={0} | all-to-all | bytes 2097152 | tf_op jit(solution)/shard_map/all_to_all | solution.py:441
  37.9 3.6 %all-to-all-start.1 = ((bf16[8,128,512]{2,1,0:T(8,128)(2,1)}), bf16[8,128,512]{2,1,0:T(8,128)(2,1)S(1)}, u32[]{:S(2)}, u32[]{:S(2)}) async-start(bf16[8,128,512]{2,1,0:T(8,128)(2,1)} %bitcast.1), calls=%async_computation.1 | async-start | bytes 2097152 | tf_op jit(solution)/shard_map/all_to_all | solution.py:441
  41.5 13.6 %forward.1 = (bf16[128,512]{1,0:T(8,128)(2,1)}, bf16[128,512]{1,0:T(8,128)(2,1)}, bf16[128,512]{1,0:T(8,128)(2,1)}, bf16[128,512]{1,0:T(8,128)(2,1)}, bf16[128,5...) custom-call(bf16[8,128,512]{2,1,0:T(8,128)(2,1)} %all_to_all.20.slab, ...), custom_call_target="tpu_custom_call" | custom-call | flops 2684354560 | bytes 10485760 | tf_op jit(solution)/shard_map/forward/pallas_call | solution.py:327
  55.1 4.1 %collective-permute-start.2 = (bf16[128,512]{1,0:T(8,128)(2,1)}, bf16[128,512]{1,0:T(8,128)(2,1)S(1)}, u32[]{:S(2)}, u32[]{:S(2)}) collective-permute-start(bf16[128,512]{1,0:T(8,128)(2,1)} %get-tuple-element.54), channel_id=1, source_target_pairs={{0,96},{16,112},{32,0},{48,16},{64,32},{80,48},{96,64},{112,80},{1... | collective-permute-start | bytes 393224 | tf_op jit(solution)/shard_map/ppermute | solution.py:447
  59.2 2.3 %collective-permute-start.3 = (bf16[128,512]{1,0:T(8,128)(2,1)}, bf16[128,512]{1,0:T(8,128)(2,1)S(1)}, u32[]{:S(2)}, u32[]{:S(2)}) collective-permute-start(bf16[128,512]{1,0:T(8,128)(2,1)} %get-tuple-element.55), channel_id=1, source_target_pairs={{0,80},{16,96},{32,112},{48,0},{64,16},{80,32},{96,48},{112,64},{1... | collective-permute-start | bytes 393224 | tf_op jit(solution)/shard_map/ppermute | solution.py:447
  61.6 2.7 %collective-permute-start.4 = (bf16[128,512]{1,0:T(8,128)(2,1)}, bf16[128,512]{1,0:T(8,128)(2,1)S(1)}, u32[]{:S(2)}, u32[]{:S(2)}) collective-permute-start(bf16[128,512]{1,0:T(8,128)(2,1)} %get-tuple-element.56), channel_id=1, source_target_pairs={{0,64},{16,80},{32,96},{48,112},{64,0},{80,16},{96,32},{112,48},{1... | collective-permute-start | bytes 393224 | tf_op jit(solution)/shard_map/ppermute | solution.py:447
  64.3 1.1 collective-permute-start.5
  65.4 3.6 %collective-permute-start.6 = (bf16[128,512]{1,0:T(8,128)(2,1)}, bf16[128,512]{1,0:T(8,128)(2,1)S(1)}, u32[]{:S(2)}, u32[]{:S(2)}) collective-permute-start(bf16[128,512]{1,0:T(8,128)(2,1)} %get-tuple-element.58), channel_id=1, source_target_pairs={{0,32},{16,48},{32,64},{48,80},{64,96},{80,112},{96,0},{112,16},{1... | collective-permute-start | bytes 393224 | tf_op jit(solution)/shard_map/ppermute | solution.py:447
  69.0 0.6 all-to-all-done.1.slabs_ref
  69.6 0.0 copy-start.2
  69.6 1.0 copy-done.2
  70.5 18.8 %backward.1 = (bf16[8,128,512]{2,1,0:T(8,128)(2,1)}, bf16[16,16,2176]{2,1,0:T(8,128)(2,1)}, bf16[16,16,2176]{2,1,0:T(8,128)(2,1)}) custom-call(bf16[8,128,512]{2,1,0:T(8,128)(2,1)} %copy-done.2, bf16[1024,512]{1,0:T(8,128)(2,1)} %get-tuple-element.60.latent_ref, bf16[1024,1536]{1,0:T(8,128)(2,1)} %get-tuple-element.61.proj_ref, ...), custom_call_target="tpu_custom_call" | custom-call | flops 6174015488 | bytes 16777216 | tf_op jit(solution)/shard_map/backward/pallas_call | solution.py:327
  89.4 0.0 copy-start
  89.4 0.0 collective-permute-done.2.refs_2_
  89.4 0.0 collective-permute-done.3.refs_3_
  89.4 0.0 collective-permute-done.4.refs_4_
  89.4 0.0 collective-permute-done.5.refs_5_
  89.4 0.0 collective-permute-done.6.refs_6_
  89.4 7.6 %all-to-all-start.2 = ((bf16[8,128,512]{2,1,0:T(8,128)(2,1)}), bf16[8,128,512]{2,1,0:T(8,128)(2,1)S(1)}, u32[]{:S(2)}, u32[]{:S(2)}) async-start(bf16[8,128,512]{2,1,0:T(8,128)(2,1)} %get-tuple-element.83), calls=%async_computation.2 | async-start | bytes 2097152 | tf_op jit(solution)/shard_map/all_to_all | solution.py:441
  97.1 0.0 copy-start.4
  97.1 0.0 copy-start.3
  97.1 0.1 collective-permute-start.7
  97.2 3.0 %collective-permute-done.7.got_ref = bf16[16,16,2176]{2,1,0:T(8,128)(2,1)S(1)} collective-permute-done((bf16[16,16,2176]{2,1,0:T(8,128)(2,1)}, bf16[16,16,2176]{2,1,0:T(8,128)(2,1)S(1)}, u32[]{:S(2)}, u32[]{:S(2)}) %collective-permute-start.7) | collective-permute-done | bytes 1114144 | tf_op jit(solution)/shard_map/ppermute | solution.py:469
  100.1 0.0 copy-done
  100.1 0.3 core_sum.1
  100.4 0.0 copy-start.1
  100.4 1.5 %collective-permute-start.8 = (bf16[4,16,2176]{2,1,0:T(8,128)(2,1)S(1)}, bf16[4,16,2176]{2,1,0:T(8,128)(2,1)S(1)}, u32[]{:S(2)}, u32[]{:S(2)}) collective-permute-start(bf16[4,16,2176]{2,1,0:T(8,128)(2,1)S(1)} %get-tuple-element.69), channel_id=1, source_target_pairs={{0,128},{128,2},{2,130},{130,0},{1,129},{129,3},{3,131},{131,1},{4... | collective-permute-start | bytes 835592 | tf_op jit(solution)/shard_map/ppermute | solution.py:453
  101.9 1.1 collective-permute-start.9
  103.0 2.2 %collective-permute-start.10 = (bf16[4,16,2176]{2,1,0:T(8,128)(2,1)S(1)}, bf16[4,16,2176]{2,1,0:T(8,128)(2,1)S(1)}, u32[]{:S(2)}, u32[]{:S(2)}) collective-permute-start(bf16[4,16,2176]{2,1,0:T(8,128)(2,1)S(1)} %get-tuple-element.71), channel_id=1, source_target_pairs={{0,130},{128,0},{2,128},{130,2},{1,131},{129,1},{3,129},{131,3},{4... | collective-permute-start | bytes 835592 | tf_op jit(solution)/shard_map/ppermute | solution.py:453
  105.2 0.0 copy-done.4
  105.2 3.1 %collective-permute-start = (bf16[128,512]{1,0:T(8,128)(2,1)S(1)}, bf16[128,512]{1,0:T(8,128)(2,1)S(1)}, u32[]{:S(2)}, u32[]{:S(2)}) collective-permute-start(bf16[128,512]{1,0:T(8,128)(2,1)S(1)} %copy-done.4), channel_id=1, source_target_pairs={{0,112},{16,0},{32,16},{48,32},{64,48},{80,64},{96,80},{112,96},{1... | collective-permute-start | bytes 393224 | tf_op jit(solution)/shard_map/ppermute | solution.py:447
  108.4 0.0 copy-done.3
  108.4 0.0 collective-permute-start.1
  108.4 1.6 %collective-permute-done.8.refs_1_ = bf16[4,16,2176]{2,1,0:T(8,128)(2,1)S(1)} collective-permute-done((bf16[4,16,2176]{2,1,0:T(8,128)(2,1)S(1)}, bf16[4,16,2176]{2,1,0:T(8,128)(2,1)S(1)}, u32[]{:S(2)}, u32[]{:S(2)}) %collective-permute-start.8) | collective-permute-done | bytes 278560 | tf_op jit(solution)/shard_map/ppermute | solution.py:453
  110.0 3.0 %collective-permute-done.9.refs_2_ = bf16[4,16,2176]{2,1,0:T(8,128)(2,1)S(1)} collective-permute-done((bf16[4,16,2176]{2,1,0:T(8,128)(2,1)S(1)}, bf16[4,16,2176]{2,1,0:T(8,128)(2,1)S(1)}, u32[]{:S(2)}, u32[]{:S(2)}) %collective-permute-start.9) | collective-permute-done | bytes 278560 | tf_op jit(solution)/shard_map/ppermute | solution.py:453
  113.0 4.3 %collective-permute-done.10.refs_3_ = bf16[4,16,2176]{2,1,0:T(8,128)(2,1)S(1)} collective-permute-done((bf16[4,16,2176]{2,1,0:T(8,128)(2,1)S(1)}, bf16[4,16,2176]{2,1,0:T(8,128)(2,1)S(1)}, u32[]{:S(2)}, u32[]{:S(2)}) %collective-permute-start.10) | collective-permute-done | bytes 278560 | tf_op jit(solution)/shard_map/ppermute | solution.py:453
  117.3 0.1 x_sum.1
  117.4 1.3 collective-permute-done.refs_1_
  118.7 0.0 collective-permute-done.1.refs_7_
  118.7 1.6 %collective-permute-start.11 = (bf16[16,2176]{1,0:T(8,128)(2,1)S(1)}, bf16[16,2176]{1,0:T(8,128)(2,1)S(1)}, u32[]{:S(2)}, u32[]{:S(2)}) collective-permute-start(bf16[16,2176]{1,0:T(8,128)(2,1)S(1)} %get-tuple-element.85), channel_id=1, source_target_pairs={{0,4},{4,8},{8,12},{12,0},{1,5},{5,9},{9,13},{13,1},{2,6},{6,10},{... | collective-permute-start | bytes 208904 | tf_op jit(solution)/shard_map/ppermute | solution.py:453
  120.3 2.9 %collective-permute-start.12 = (bf16[16,2176]{1,0:T(8,128)(2,1)S(1)}, bf16[16,2176]{1,0:T(8,128)(2,1)S(1)}, u32[]{:S(2)}, u32[]{:S(2)}) collective-permute-start(bf16[16,2176]{1,0:T(8,128)(2,1)S(1)} %get-tuple-element.86), channel_id=1, source_target_pairs={{0,8},{4,12},{8,0},{12,4},{1,9},{5,13},{9,1},{13,5},{2,10},{6,14},... | collective-permute-start | bytes 208904 | tf_op jit(solution)/shard_map/ppermute | solution.py:453
  123.2 1.3 collective-permute-start.13
  124.6 0.0 collective-permute-done.11.refs_1_
  124.6 1.7 %collective-permute-done.12.refs_2_ = bf16[16,2176]{1,0:T(8,128)(2,1)S(1)} collective-permute-done((bf16[16,2176]{1,0:T(8,128)(2,1)S(1)}, bf16[16,2176]{1,0:T(8,128)(2,1)S(1)}, u32[]{:S(2)}, u32[]{:S(2)}) %collective-permute-start.12) | collective-permute-done | bytes 69664 | tf_op jit(solution)/shard_map/ppermute | solution.py:453
  126.2 1.3 collective-permute-done.13.refs_3_
  127.5 0.8 y_sum.1
  128.3 0.0 all-to-all-done.2.refs_8_
  128.3 5.9 %all-to-all-start.3 = ((bf16[8,2,3072]{2,1,0:T(2,128)(2,1)}), bf16[8,2,3072]{2,1,0:T(2,128)(2,1)S(1)}, u32[]{:S(2)}, u32[]{:S(2)}) async-start(bf16[8,2,3072]{2,1,0:T(2,128)(2,1)} %y_sum.1), calls=%async_computation.3 | async-start | bytes 196608 | tf_op jit(solution)/shard_map/all_to_all | solution.py:441
  134.2 0.0 copy-done.1
  134.2 1.5 %gather_slabs.1 = (bf16[8,128,512]{2,1,0:T(8,128)(2,1)}, bf16[8,128,512]{2,1,0:T(8,128)(2,1)}) custom-call(bf16[128,512]{1,0:T(8,128)(2,1)S(1)} %copy-done.1, bf16[128,512]{1,0:T(8,128)(2,1)S(1)} %collective-permute-done.refs_1_, bf16[128,512]{1,0:T(8,128)(2,1)S(1)} %collective-permute-done.2.refs_2_, bf16[128,512]{1,0:T(8,128)(2,1)S(1)} %collective-permute-done.3.refs_3_, ...), custom_call_target="tpu_custom_call" | custom-call | tf_op jit(solution)/shard_map/gather_slabs/pallas_call | solution.py:327
  135.7 7.2 %all-to-all-done.3.shares_ref = bf16[8,2,3072]{2,1,0:T(2,128)(2,1)S(1)} async-done(((bf16[8,2,3072]{2,1,0:T(2,128)(2,1)}), bf16[8,2,3072]{2,1,0:T(2,128)(2,1)S(1)}, u32[]{:S(2)}, u32[]{:S(2)}) %all-to-all-start.3) | async-done | bytes 98336 | tf_op jit(solution)/shard_map/all_to_all | solution.py:441
  142.9 0.7 second_sum.1
Async XLA Ops:
  37.9 31.6 %all-to-all-start.1 = ((bf16[8,128,512]{2,1,0:T(8,128)(2,1)}), bf16[8,128,512]{2,1,0:T(8,128)(2,1)S(1)}, u32[]{:S(2)}, u32[]{:S(2)}) async-start(bf16[8,128,512]{2,1,0:T(8,128)(2,1)} %bitcast.1), calls=%async_computation.1 | async-start | bytes 2097152 | tf_op jit(solution)/shard_map/all_to_all | solution.py:441
  55.1 34.2 %collective-permute-start.2 = (bf16[128,512]{1,0:T(8,128)(2,1)}, bf16[128,512]{1,0:T(8,128)(2,1)S(1)}, u32[]{:S(2)}, u32[]{:S(2)}) collective-permute-start(bf16[128,512]{1,0:T(8,128)(2,1)} %get-tuple-element.54), channel_id=1, source_target_pairs={{0,96},{16,112},{32,0},{48,16},{64,32},{80,48},{96,64},{112,80},{1... | collective-permute-start | bytes 393224 | tf_op jit(solution)/shard_map/ppermute | solution.py:447
  59.2 30.2 %collective-permute-start.3 = (bf16[128,512]{1,0:T(8,128)(2,1)}, bf16[128,512]{1,0:T(8,128)(2,1)S(1)}, u32[]{:S(2)}, u32[]{:S(2)}) collective-permute-start(bf16[128,512]{1,0:T(8,128)(2,1)} %get-tuple-element.55), channel_id=1, source_target_pairs={{0,80},{16,96},{32,112},{48,0},{64,16},{80,32},{96,48},{112,64},{1... | collective-permute-start | bytes 393224 | tf_op jit(solution)/shard_map/ppermute | solution.py:447
  61.6 27.8 %collective-permute-start.4 = (bf16[128,512]{1,0:T(8,128)(2,1)}, bf16[128,512]{1,0:T(8,128)(2,1)S(1)}, u32[]{:S(2)}, u32[]{:S(2)}) collective-permute-start(bf16[128,512]{1,0:T(8,128)(2,1)} %get-tuple-element.56), channel_id=1, source_target_pairs={{0,64},{16,80},{32,96},{48,112},{64,0},{80,16},{96,32},{112,48},{1... | collective-permute-start | bytes 393224 | tf_op jit(solution)/shard_map/ppermute | solution.py:447
  64.3 25.2 %collective-permute-start.5 = (bf16[128,512]{1,0:T(8,128)(2,1)}, bf16[128,512]{1,0:T(8,128)(2,1)S(1)}, u32[]{:S(2)}, u32[]{:S(2)}) collective-permute-start(bf16[128,512]{1,0:T(8,128)(2,1)} %get-tuple-element.57), channel_id=1, source_target_pairs={{0,48},{16,64},{32,80},{48,96},{64,112},{80,0},{96,16},{112,32},{1... | collective-permute-start | bytes 393224 | tf_op jit(solution)/shard_map/ppermute | solution.py:447
  65.4 24.1 %collective-permute-start.6 = (bf16[128,512]{1,0:T(8,128)(2,1)}, bf16[128,512]{1,0:T(8,128)(2,1)S(1)}, u32[]{:S(2)}, u32[]{:S(2)}) collective-permute-start(bf16[128,512]{1,0:T(8,128)(2,1)} %get-tuple-element.58), channel_id=1, source_target_pairs={{0,32},{16,48},{32,64},{48,80},{64,96},{80,112},{96,0},{112,16},{1... | collective-permute-start | bytes 393224 | tf_op jit(solution)/shard_map/ppermute | solution.py:447
  69.6 1.0 copy-start.2
  89.4 10.8 %copy-start = (bf16[16,16,2176]{2,1,0:T(8,128)(2,1)S(1)}, bf16[16,16,2176]{2,1,0:T(8,128)(2,1)}, u32[]{:S(2)}) copy-start(bf16[16,16,2176]{2,1,0:T(8,128)(2,1)} %get-tuple-element.66.keep_ref) | copy-start | bytes 3342340
  89.4 38.9 %all-to-all-start.2 = ((bf16[8,128,512]{2,1,0:T(8,128)(2,1)}), bf16[8,128,512]{2,1,0:T(8,128)(2,1)S(1)}, u32[]{:S(2)}, u32[]{:S(2)}) async-start(bf16[8,128,512]{2,1,0:T(8,128)(2,1)} %get-tuple-element.83), calls=%async_computation.2 | async-start | bytes 2097152 | tf_op jit(solution)/shard_map/all_to_all | solution.py:441
  97.1 8.2 %copy-start.4 = (bf16[128,512]{1,0:T(8,128)(2,1)S(1)}, bf16[128,512]{1,0:T(8,128)(2,1)}, u32[]{:S(2)}) copy-start(bf16[128,512]{1,0:T(8,128)(2,1)} %get-tuple-element.52) | copy-start | bytes 393220
  97.1 11.3 %copy-start.3 = (bf16[128,512]{1,0:T(8,128)(2,1)S(1)}, bf16[128,512]{1,0:T(8,128)(2,1)}, u32[]{:S(2)}) copy-start(bf16[128,512]{1,0:T(8,128)(2,1)} %get-tuple-element.53) | copy-start | bytes 393220
  97.1 3.1 %collective-permute-start.7 = (bf16[16,16,2176]{2,1,0:T(8,128)(2,1)}, bf16[16,16,2176]{2,1,0:T(8,128)(2,1)S(1)}, u32[]{:S(2)}, u32[]{:S(2)}) collective-permute-start(bf16[16,16,2176]{2,1,0:T(8,128)(2,1)} %get-tuple-element.67), channel_id=1, source_target_pairs={{0,1},{1,0},{2,3},{3,2},{4,5},{5,4},{6,7},{7,6},{8,9},{9,8},{10,11... | collective-permute-start | bytes 3342344 | tf_op jit(solution)/shard_map/ppermute | solution.py:469
  100.4 33.8 %copy-start.1 = (bf16[128,512]{1,0:T(8,128)(2,1)S(1)}, bf16[128,512]{1,0:T(8,128)(2,1)}, u32[]{:S(2)}) copy-start(bf16[128,512]{1,0:T(8,128)(2,1)} %get-tuple-element.51.refs_0_) | copy-start | bytes 393220
  100.4 9.6 %collective-permute-start.8 = (bf16[4,16,2176]{2,1,0:T(8,128)(2,1)S(1)}, bf16[4,16,2176]{2,1,0:T(8,128)(2,1)S(1)}, u32[]{:S(2)}, u32[]{:S(2)}) collective-permute-start(bf16[4,16,2176]{2,1,0:T(8,128)(2,1)S(1)} %get-tuple-element.69), channel_id=1, source_target_pairs={{0,128},{128,2},{2,130},{130,0},{1,129},{129,3},{3,131},{131,1},{4... | collective-permute-start | bytes 835592 | tf_op jit(solution)/shard_map/ppermute | solution.py:453
  101.9 11.0 %collective-permute-start.9 = (bf16[4,16,2176]{2,1,0:T(8,128)(2,1)S(1)}, bf16[4,16,2176]{2,1,0:T(8,128)(2,1)S(1)}, u32[]{:S(2)}, u32[]{:S(2)}) collective-permute-start(bf16[4,16,2176]{2,1,0:T(8,128)(2,1)S(1)} %get-tuple-element.70), channel_id=1, source_target_pairs={{0,2},{128,130},{2,0},{130,128},{1,3},{129,131},{3,1},{131,129},{4... | collective-permute-start | bytes 835592 | tf_op jit(solution)/shard_map/ppermute | solution.py:453
  103.0 14.2 %collective-permute-start.10 = (bf16[4,16,2176]{2,1,0:T(8,128)(2,1)S(1)}, bf16[4,16,2176]{2,1,0:T(8,128)(2,1)S(1)}, u32[]{:S(2)}, u32[]{:S(2)}) collective-permute-start(bf16[4,16,2176]{2,1,0:T(8,128)(2,1)S(1)} %get-tuple-element.71), channel_id=1, source_target_pairs={{0,130},{128,0},{2,128},{130,2},{1,131},{129,1},{3,129},{131,3},{4... | collective-permute-start | bytes 835592 | tf_op jit(solution)/shard_map/ppermute | solution.py:453
  105.2 13.5 %collective-permute-start = (bf16[128,512]{1,0:T(8,128)(2,1)S(1)}, bf16[128,512]{1,0:T(8,128)(2,1)S(1)}, u32[]{:S(2)}, u32[]{:S(2)}) collective-permute-start(bf16[128,512]{1,0:T(8,128)(2,1)S(1)} %copy-done.4), channel_id=1, source_target_pairs={{0,112},{16,0},{32,16},{48,32},{64,48},{80,64},{96,80},{112,96},{1... | collective-permute-start | bytes 393224 | tf_op jit(solution)/shard_map/ppermute | solution.py:447
  108.4 10.4 %collective-permute-start.1 = (bf16[128,512]{1,0:T(8,128)(2,1)S(1)}, bf16[128,512]{1,0:T(8,128)(2,1)S(1)}, u32[]{:S(2)}, u32[]{:S(2)}) collective-permute-start(bf16[128,512]{1,0:T(8,128)(2,1)S(1)} %copy-done.3), channel_id=1, source_target_pairs={{0,16},{16,32},{32,48},{48,64},{64,80},{80,96},{96,112},{112,0},{1... | collective-permute-start | bytes 393224 | tf_op jit(solution)/shard_map/ppermute | solution.py:447
  118.7 5.8 %collective-permute-start.11 = (bf16[16,2176]{1,0:T(8,128)(2,1)S(1)}, bf16[16,2176]{1,0:T(8,128)(2,1)S(1)}, u32[]{:S(2)}, u32[]{:S(2)}) collective-permute-start(bf16[16,2176]{1,0:T(8,128)(2,1)S(1)} %get-tuple-element.85), channel_id=1, source_target_pairs={{0,4},{4,8},{8,12},{12,0},{1,5},{5,9},{9,13},{13,1},{2,6},{6,10},{... | collective-permute-start | bytes 208904 | tf_op jit(solution)/shard_map/ppermute | solution.py:453
  120.3 5.9 %collective-permute-start.12 = (bf16[16,2176]{1,0:T(8,128)(2,1)S(1)}, bf16[16,2176]{1,0:T(8,128)(2,1)S(1)}, u32[]{:S(2)}, u32[]{:S(2)}) collective-permute-start(bf16[16,2176]{1,0:T(8,128)(2,1)S(1)} %get-tuple-element.86), channel_id=1, source_target_pairs={{0,8},{4,12},{8,0},{12,4},{1,9},{5,13},{9,1},{13,5},{2,10},{6,14},... | collective-permute-start | bytes 208904 | tf_op jit(solution)/shard_map/ppermute | solution.py:453
  123.2 4.3 %collective-permute-start.13 = (bf16[16,2176]{1,0:T(8,128)(2,1)S(1)}, bf16[16,2176]{1,0:T(8,128)(2,1)S(1)}, u32[]{:S(2)}, u32[]{:S(2)}) collective-permute-start(bf16[16,2176]{1,0:T(8,128)(2,1)S(1)} %get-tuple-element.87), channel_id=1, source_target_pairs={{0,12},{4,0},{8,4},{12,8},{1,13},{5,1},{9,5},{13,9},{2,14},{6,2},{... | collective-permute-start | bytes 208904 | tf_op jit(solution)/shard_map/ppermute | solution.py:453
  128.3 14.6 %all-to-all-start.3 = ((bf16[8,2,3072]{2,1,0:T(2,128)(2,1)}), bf16[8,2,3072]{2,1,0:T(2,128)(2,1)S(1)}, u32[]{:S(2)}, u32[]{:S(2)}) async-start(bf16[8,2,3072]{2,1,0:T(2,128)(2,1)} %y_sum.1), calls=%async_computation.3 | async-start | bytes 196608 | tf_op jit(solution)/shard_map/all_to_all | solution.py:441

commit v4 on v3

--- a/solution.py
+++ b/solution.py
@@ -87,6 +87,9 @@
         self.lane_of = lax.broadcasted_iota(jnp.int32, (self.cells, self.lanes), 1) // self.head_size
         self.slices = [slice(g * self.lanes, (g + 1) * self.lanes) for g in range(HEADS // PACK)]
 
+    def columns(self, group):
+        return slice(group * PACK * self.cells, (group + 1) * PACK * self.cells)
+
     def spread(self, part):
         return jnp.concatenate([part] * PACK, 0) * self.own
 
@@ -104,7 +107,7 @@
 
 def forward_kernel(slabs_ref, w_qkv_ref, w_out_ref, gain_ref, bias_ref, *refs):
     piece_refs = refs[:GRID]
-    latent_ref, proj_ref, attended_ref, cells_ref = refs[GRID:]
+    latent_ref, proj_ref, attended_ref, probs_ref, cells_ref = refs[GRID:]
     width = w_out_ref.shape[0]
     rows = latent_ref.shape[0] // STEPS
     to_windows(slabs_ref, cells_ref)
@@ -122,7 +125,8 @@
         keys = [proj_ref[at, width + s.start : width + s.stop] for s in heads.slices]
         wide_q = [heads.spread(proj_ref[at, s]) for s in heads.slices]
         probs = [p.astype(LOW) for p in heads.probs(keys, wide_q)]
-        for s, p in zip(heads.slices, probs):
+        for g, (s, p) in enumerate(zip(heads.slices, probs)):
+            probs_ref[at, heads.columns(g)] = p
             values = proj_ref[at, 2 * width + s.start : 2 * width + s.stop]
             attended_ref[at, s] = heads.gather(dot_tn(p, values)).astype(LOW)
         return carry
@@ -138,24 +142,26 @@
 
 
 def backward_kernel(
-    slabs_ref, latent_ref, proj_ref, attended_ref, w_qkv_ref, w_out_ref, gain_ref, bias_ref, *refs
+    slabs_ref, latent_ref, proj_ref, attended_ref, probs_ref, w_qkv_ref, w_out_ref, gain_ref, bias_ref, *refs
 ):
-    hbm_refs = (slabs_ref, w_out_ref, proj_ref, latent_ref, w_qkv_ref, attended_ref)
+    hbm_refs = (slabs_ref, w_out_ref, proj_ref, probs_ref, latent_ref, w_qkv_ref, attended_ref)
     out_hbm_ref, keep_hbm_ref, send_hbm_ref = refs[:3]
     cells_ref, cot_ref, heads_ref, grad_ref, normed_ref = refs[3:8]
-    vmem_refs = refs[8:14]
-    out_ref, keep_ref, send_ref, in_sems, out_sems = refs[14:]
-    slabs_ref, w_out_ref, proj_ref, latent_ref, w_qkv_ref, attended_ref = vmem_refs
+    vmem_refs = refs[8:15]
+    out_ref, keep_ref, send_ref, in_sems, out_sems = refs[15:]
+    slabs_ref, w_out_ref, proj_ref, probs_ref, latent_ref, w_qkv_ref, attended_ref = vmem_refs
     loads = [
         pltpu.make_async_copy(source, target, in_sems.at[i])
         for i, (source, target) in enumerate(zip(hbm_refs, vmem_refs))
     ]
-    for load in loads:
+    for load in loads[:4]:
         load.start()
-    slabs_load, w_out_load, proj_load, latent_load, w_qkv_load, attended_load = loads
+    slabs_load, w_out_load, proj_load, probs_load, latent_load, w_qkv_load, attended_load = loads
     width = w_out_ref.shape[0]
     rows = latent_ref.shape[0] // STEPS
     slabs_load.wait()
+    for load in loads[4:]:
+        load.start()
     to_windows(slabs_ref, cells_ref)
     w_out_load.wait()
     for step in range(STEPS):
@@ -163,6 +169,7 @@
         cot_ref[at, :] = step_rows(cells_ref, step).astype(LOW)
         heads_ref[at, :] = dot_nt(cot_ref[at, :], w_out_ref[...]).astype(LOW)
     proj_load.wait()
+    probs_load.wait()
     heads = Heads(width)
 
     def window(w, carry):
@@ -172,13 +179,14 @@
         wide_q = [heads.spread(proj_ref[at, s]) for s in heads.slices]
         wide_g = [heads.spread(heads_ref[at, s]) for s in heads.slices]
         grad_probs = [dot_nt(v, g) for v, g in zip(values, wide_g)]
-        probs = heads.probs(keys, wide_q)
+        probs_low = [probs_ref[at, heads.columns(g)] for g in range(len(heads.slices))]
+        probs = [p.astype(jnp.float32) for p in probs_low]
         grad_scores = [
             (p * (d - jnp.sum(p * d, 0, keepdims=True))).astype(LOW)
             for p, d in zip(probs, grad_probs)
         ]
         for i, s in enumerate(heads.slices):
-            grad_v = dot_nn(probs[i].astype(LOW), wide_g[i])
+            grad_v = dot_nn(probs_low[i], wide_g[i])
             grad_k = dot_nn(grad_scores[i], wide_q[i]) * heads.factor
             grad_q = heads.gather(dot_tn(grad_scores[i], keys[i])) * heads.factor
             for j, part in enumerate((grad_q, grad_k, grad_v)):
@@ -348,6 +356,7 @@
             SHAPE((tokens, width), LOW),
             SHAPE((tokens, 3 * width), LOW),
             SHAPE((tokens, width), LOW),
+            SHAPE((tokens, HEADS * GRID * GRID), LOW),
         ],
         slabs,
         w_qkv,
@@ -388,16 +397,17 @@
             pltpu.VMEM(slabs.shape, LOW),
             pltpu.VMEM(w_out.shape, LOW),
             pltpu.VMEM((tokens, 3 * width), LOW),
+            pltpu.VMEM((tokens, HEADS * GRID * GRID), LOW),
             pltpu.VMEM((tokens, width), LOW),
             pltpu.VMEM(w_qkv.shape, LOW),
             pltpu.VMEM((tokens, width), LOW),
             pltpu.VMEM(slabs.shape, LOW),
             pltpu.VMEM((planes, share, wide), LOW),
             pltpu.VMEM((planes, share, wide), LOW),
-            pltpu.SemaphoreType.DMA((6,)),
+            pltpu.SemaphoreType.DMA((7,)),
             pltpu.SemaphoreType.DMA((3,)),
         ],
-        in_specs=[ANY] * 6 + [VMEM] * 2,
+        in_specs=[ANY] * 7 + [VMEM] * 2,
         out_specs=[ANY] * 3,
         flops=flops,
         moved=16 * 2**20,
@@ -468,9 +478,10 @@
     grad_input = swap(grad_input, "z")
     parts = core_sum(keep, lax.ppermute(send, "core", [(0, 1), (1, 0)]))
     parts = x_sum(ring_parts(parts, ("dp", "x_hi"), lambda x: x % 2 * 2 + x // 2))
-    outs[1], outs[7], parts = lax.optimization_barrier((outs[1], outs[7], parts))
     shares = y_sum(ring_parts(parts, "y"))
-    grad_input, shares = lax.optimization_barrier((grad_input, shares))
+    outs[1], outs[7], grad_input, shares = lax.optimization_barrier(
+        (outs[1], outs[7], grad_input, shares)
+    )
     grad_qkv, grad_out, grad_norm = second_sum(swap(shares, "z"), width)
     output, grad_input = gather_slabs(outs, grad_input)
     return (output[None], grad_input[None], grad_qkv, grad_out, grad_norm)

time: 144 us -> 143 us (level)
  waiting for transfers between devices: 24 us -> 22 us
where the time goes in v4:
time: 143 us; the launch traced here: 142 us
  starting transfers between devices  46.1 us (32%)
  blocking collectives  37.3 us (26%)
  Pallas kernels  35.2 us (25%)
  waiting for transfers between devices  22 us (15%)
    all_to_all x1, blocking collectives, swap(): return lax.all_to_all(value, axes, split_axis=0, concat_axis=0, tiled=True)  37.3 us
    pallas_call x7, Pallas kernels, call(): pl.pallas_call(kernel, out_shape=out_shape, in_specs=in_specs or [VMEM] *...  35.2 us
    all_to_all x3, starting transfers between devices, swap(): return lax.all_to_all(value, axes, split_axis=0, concat_axis=0, tiled=True)  18.2 us
    ppermute x7, starting transfers between devices, turn(): lax.ppermute(value, 'z', [(a, (a + shift) % GRID) for a in range(GRID)])  17 us
    ppermute x6, waiting for transfers between devices, ring_parts(): lax.ppermute(part, axes, pairs[s])  11.7 us
    ppermute x6, starting transfers between devices, ring_parts(): lax.ppermute(part, axes, pairs[s])  10.7 us
    all_to_all x3, waiting for transfers between devices, swap(): return lax.all_to_all(value, axes, split_axis=0, concat_axis=0, tiled=True)  7.33 us
    ppermute x1, waiting for transfers between devices, body(): parts = core_sum(keep, lax.ppermute(send, 'core', [(0, 1), (1, 0)]))  2.95 us
  transfers between devices with their start and end apart: 17, of which 9 were waited for; matrix products, arithmetic and copies ran while one was open for 0% of the time, Pallas kernels for 24%

profile of v4, /device:TPU:2, one launch (start us, length us, event | category | flops | bytes accessed | tf_op | source)
XLA Modules:
  0.0 142.4 jit_solution(14644721796368496151)
XLA Ops:
  0.6 37.3 %all_to_all.20.slabs_ref = bf16[8,128,512]{2,1,0:T(8,128)(2,1)} all-to-all(bf16[8,128,512]{2,1,0:T(8,128)(2,1)} %bitcast.6), channel_id=1, replica_groups=mesh['dp'=2,'z'=8,'y'=4,'x_hi'=2,'core'=2] {'z'}, dimensions={0} | all-to-all | bytes 2097152 | tf_op jit(solution)/shard_map/all_to_all | solution.py:451
  37.9 3.6 %all-to-all-start.1 = ((bf16[8,128,512]{2,1,0:T(8,128)(2,1)}), bf16[8,128,512]{2,1,0:T(8,128)(2,1)S(1)}, u32[]{:S(2)}, u32[]{:S(2)}) async-start(bf16[8,128,512]{2,1,0:T(8,128)(2,1)} %bitcast.1), calls=%async_computation.1 | async-start | bytes 2097152 | tf_op jit(solution)/shard_map/all_to_all | solution.py:451
  41.5 14.4 %forward.1 = (bf16[128,512]{1,0:T(8,128)(2,1)}, bf16[128,512]{1,0:T(8,128)(2,1)}, bf16[128,512]{1,0:T(8,128)(2,1)}, bf16[128,512]{1,0:T(8,128)(2,1)}, bf16[128,5...) custom-call(bf16[8,128,512]{2,1,0:T(8,128)(2,1)} %all_to_all.20.slab, ...), custom_call_target="tpu_custom_call" | custom-call | flops 2684354560 | bytes 10485760 | tf_op jit(solution)/shard_map/forward/pallas_call | solution.py:335
  55.9 4.1 %collective-permute-start.2 = (bf16[128,512]{1,0:T(8,128)(2,1)}, bf16[128,512]{1,0:T(8,128)(2,1)S(1)}, u32[]{:S(2)}, u32[]{:S(2)}) collective-permute-start(bf16[128,512]{1,0:T(8,128)(2,1)} %get-tuple-element.51), channel_id=1, source_target_pairs={{0,96},{16,112},{32,0},{48,16},{64,32},{80,48},{96,64},{112,80},{1... | collective-permute-start | bytes 393224 | tf_op jit(solution)/shard_map/ppermute | solution.py:457
  59.9 2.3 %collective-permute-start.3 = (bf16[128,512]{1,0:T(8,128)(2,1)}, bf16[128,512]{1,0:T(8,128)(2,1)S(1)}, u32[]{:S(2)}, u32[]{:S(2)}) collective-permute-start(bf16[128,512]{1,0:T(8,128)(2,1)} %get-tuple-element.52), channel_id=1, source_target_pairs={{0,80},{16,96},{32,112},{48,0},{64,16},{80,32},{96,48},{112,64},{1... | collective-permute-start | bytes 393224 | tf_op jit(solution)/shard_map/ppermute | solution.py:457
  62.3 2.7 %collective-permute-start.4 = (bf16[128,512]{1,0:T(8,128)(2,1)}, bf16[128,512]{1,0:T(8,128)(2,1)S(1)}, u32[]{:S(2)}, u32[]{:S(2)}) collective-permute-start(bf16[128,512]{1,0:T(8,128)(2,1)} %get-tuple-element.53), channel_id=1, source_target_pairs={{0,64},{16,80},{32,96},{48,112},{64,0},{80,16},{96,32},{112,48},{1... | collective-permute-start | bytes 393224 | tf_op jit(solution)/shard_map/ppermute | solution.py:457
  65.0 1.1 collective-permute-start.5
  66.1 3.6 %collective-permute-start.6 = (bf16[128,512]{1,0:T(8,128)(2,1)}, bf16[128,512]{1,0:T(8,128)(2,1)S(1)}, u32[]{:S(2)}, u32[]{:S(2)}) collective-permute-start(bf16[128,512]{1,0:T(8,128)(2,1)} %get-tuple-element.55), channel_id=1, source_target_pairs={{0,32},{16,48},{32,64},{48,80},{64,96},{80,112},{96,0},{112,16},{1... | collective-permute-start | bytes 393224 | tf_op jit(solution)/shard_map/ppermute | solution.py:457
  69.7 0.1 all-to-all-done.1.slabs_ref
  69.8 0.0 copy-start.2
  69.8 1.0 copy-done.2
  70.8 17.5 %backward.1 = (bf16[8,128,512]{2,1,0:T(8,128)(2,1)}, bf16[16,16,2176]{2,1,0:T(8,128)(2,1)}, bf16[16,16,2176]{2,1,0:T(8,128)(2,1)}) custom-call(bf16[8,128,512]{2,1,0:T(8,128)(2,1)} %copy-done.2, bf16[1024,512]{1,0:T(8,128)(2,1)} %get-tuple-element.57.latent_ref, bf16[1024,1536]{1,0:T(8,128)(2,1)} %get-tuple-element.58.proj_ref, ...), custom_call_target="tpu_custom_call" | custom-call | flops 6174015488 | bytes 16777216 | tf_op jit(solution)/shard_map/backward/pallas_call | solution.py:335
  88.3 0.0 copy-start
  88.3 0.0 collective-permute-done.2.refs_2_
  88.3 0.0 collective-permute-done.3.refs_3_
  88.3 0.0 collective-permute-done.4.refs_4_
  88.4 0.0 collective-permute-done.5.refs_5_
  88.4 0.0 collective-permute-done.6.refs_6_
  88.4 7.4 %all-to-all-start.2 = ((bf16[8,128,512]{2,1,0:T(8,128)(2,1)}), bf16[8,128,512]{2,1,0:T(8,128)(2,1)S(1)}, u32[]{:S(2)}, u32[]{:S(2)}) async-start(bf16[8,128,512]{2,1,0:T(8,128)(2,1)} %get-tuple-element.64), calls=%async_computation.2 | async-start | bytes 2097152 | tf_op jit(solution)/shard_map/all_to_all | solution.py:451
  95.8 0.0 copy-start.4
  95.8 0.0 copy-start.3
  95.8 0.0 copy-start.1
  95.9 0.1 collective-permute-start.7
  96.0 3.0 %collective-permute-done.7.got_ref = bf16[16,16,2176]{2,1,0:T(8,128)(2,1)S(1)} collective-permute-done((bf16[16,16,2176]{2,1,0:T(8,128)(2,1)}, bf16[16,16,2176]{2,1,0:T(8,128)(2,1)S(1)}, u32[]{:S(2)}, u32[]{:S(2)}) %collective-permute-start.7) | collective-permute-done | bytes 1114144 | tf_op jit(solution)/shard_map/ppermute | solution.py:479
  98.9 0.0 copy-done
  98.9 0.3 core_sum.1
  99.2 1.6 %collective-permute-start.8 = (bf16[4,16,2176]{2,1,0:T(8,128)(2,1)S(1)}, bf16[4,16,2176]{2,1,0:T(8,128)(2,1)S(1)}, u32[]{:S(2)}, u32[]{:S(2)}) collective-permute-start(bf16[4,16,2176]{2,1,0:T(8,128)(2,1)S(1)} %get-tuple-element.68), channel_id=1, source_target_pairs={{0,128},{128,2},{2,130},{130,0},{1,129},{129,3},{3,131},{131,1},{4... | collective-permute-start | bytes 835592 | tf_op jit(solution)/shard_map/ppermute | solution.py:463
  100.7 1.1 collective-permute-start.9
  101.8 2.2 %collective-permute-start.10 = (bf16[4,16,2176]{2,1,0:T(8,128)(2,1)S(1)}, bf16[4,16,2176]{2,1,0:T(8,128)(2,1)S(1)}, u32[]{:S(2)}, u32[]{:S(2)}) collective-permute-start(bf16[4,16,2176]{2,1,0:T(8,128)(2,1)S(1)} %get-tuple-element.70), channel_id=1, source_target_pairs={{0,130},{128,0},{2,128},{130,2},{1,131},{129,1},{3,129},{131,3},{4... | collective-permute-start | bytes 835592 | tf_op jit(solution)/shard_map/ppermute | solution.py:463
  104.0 0.0 copy-done.4
  104.0 3.2 %collective-permute-start = (bf16[128,512]{1,0:T(8,128)(2,1)S(1)}, bf16[128,512]{1,0:T(8,128)(2,1)S(1)}, u32[]{:S(2)}, u32[]{:S(2)}) collective-permute-start(bf16[128,512]{1,0:T(8,128)(2,1)S(1)} %copy-done.4), channel_id=1, source_target_pairs={{0,112},{16,0},{32,16},{48,32},{64,48},{80,64},{96,80},{112,96},{1... | collective-permute-start | bytes 393224 | tf_op jit(solution)/shard_map/ppermute | solution.py:457
  107.2 0.0 copy-done.3
  107.2 0.0 collective-permute-start.1
  107.2 1.5 %collective-permute-done.8.refs_1_ = bf16[4,16,2176]{2,1,0:T(8,128)(2,1)S(1)} collective-permute-done((bf16[4,16,2176]{2,1,0:T(8,128)(2,1)S(1)}, bf16[4,16,2176]{2,1,0:T(8,128)(2,1)S(1)}, u32[]{:S(2)}, u32[]{:S(2)}) %collective-permute-start.8) | collective-permute-done | bytes 278560 | tf_op jit(solution)/shard_map/ppermute | solution.py:463
  108.7 3.0 %collective-permute-done.9.refs_2_ = bf16[4,16,2176]{2,1,0:T(8,128)(2,1)S(1)} collective-permute-done((bf16[4,16,2176]{2,1,0:T(8,128)(2,1)S(1)}, bf16[4,16,2176]{2,1,0:T(8,128)(2,1)S(1)}, u32[]{:S(2)}, u32[]{:S(2)}) %collective-permute-start.9) | collective-permute-done | bytes 278560 | tf_op jit(solution)/shard_map/ppermute | solution.py:463
  111.8 4.2 %collective-permute-done.10.refs_3_ = bf16[4,16,2176]{2,1,0:T(8,128)(2,1)S(1)} collective-permute-done((bf16[4,16,2176]{2,1,0:T(8,128)(2,1)S(1)}, bf16[4,16,2176]{2,1,0:T(8,128)(2,1)S(1)}, u32[]{:S(2)}, u32[]{:S(2)}) %collective-permute-start.10) | collective-permute-done | bytes 278560 | tf_op jit(solution)/shard_map/ppermute | solution.py:463
  115.9 0.1 x_sum.1
  116.1 1.7 %collective-permute-start.11 = (bf16[16,2176]{1,0:T(8,128)(2,1)S(1)}, bf16[16,2176]{1,0:T(8,128)(2,1)S(1)}, u32[]{:S(2)}, u32[]{:S(2)}) collective-permute-start(bf16[16,2176]{1,0:T(8,128)(2,1)S(1)} %get-tuple-element.72), channel_id=1, source_target_pairs={{0,4},{4,8},{8,12},{12,0},{1,5},{5,9},{9,13},{13,1},{2,6},{6,10},{... | collective-permute-start | bytes 208904 | tf_op jit(solution)/shard_map/ppermute | solution.py:463
  117.7 2.9 %collective-permute-start.12 = (bf16[16,2176]{1,0:T(8,128)(2,1)S(1)}, bf16[16,2176]{1,0:T(8,128)(2,1)S(1)}, u32[]{:S(2)}, u32[]{:S(2)}) collective-permute-start(bf16[16,2176]{1,0:T(8,128)(2,1)S(1)} %get-tuple-element.73), channel_id=1, source_target_pairs={{0,8},{4,12},{8,0},{12,4},{1,9},{5,13},{9,1},{13,5},{2,10},{6,14},... | collective-permute-start | bytes 208904 | tf_op jit(solution)/shard_map/ppermute | solution.py:463
  120.7 1.3 collective-permute-start.13
  122.0 0.4 collective-permute-done.11.refs_1_
  122.4 1.3 collective-permute-done.12.refs_2_
  123.7 1.3 collective-permute-done.13.refs_3_
  125.0 0.8 y_sum.1
  125.7 0.0 collective-permute-done.refs_1_
  125.7 0.0 collective-permute-done.1.refs_7_
  125.7 0.0 all-to-all-done.2.refs_8_
  125.7 7.2 %all-to-all-start.3 = ((bf16[8,2,3072]{2,1,0:T(2,128)(2,1)}), bf16[8,2,3072]{2,1,0:T(2,128)(2,1)S(1)}, u32[]{:S(2)}, u32[]{:S(2)}) async-start(bf16[8,2,3072]{2,1,0:T(2,128)(2,1)} %y_sum.1), calls=%async_computation.3 | async-start | bytes 196608 | tf_op jit(solution)/shard_map/all_to_all | solution.py:451
  132.9 0.0 copy-done.1
  133.0 1.5 %gather_slabs.1 = (bf16[8,128,512]{2,1,0:T(8,128)(2,1)}, bf16[8,128,512]{2,1,0:T(8,128)(2,1)}) custom-call(bf16[128,512]{1,0:T(8,128)(2,1)S(1)} %copy-done.1, bf16[128,512]{1,0:T(8,128)(2,1)S(1)} %collective-permute-done.refs_1_, bf16[128,512]{1,0:T(8,128)(2,1)S(1)} %collective-permute-done.2.refs_2_, bf16[128,512]{1,0:T(8,128)(2,1)S(1)} %collective-permute-done.3.refs_3_, ...), custom_call_target="tpu_custom_call" | custom-call | tf_op jit(solution)/shard_map/gather_slabs/pallas_call | solution.py:335
  134.4 7.2 %all-to-all-done.3.shares_ref = bf16[8,2,3072]{2,1,0:T(2,128)(2,1)S(1)} async-done(((bf16[8,2,3072]{2,1,0:T(2,128)(2,1)}), bf16[8,2,3072]{2,1,0:T(2,128)(2,1)S(1)}, u32[]{:S(2)}, u32[]{:S(2)}) %all-to-all-start.3) | async-done | bytes 98336 | tf_op jit(solution)/shard_map/all_to_all | solution.py:451
  141.7 0.7 second_sum.1
Async XLA Ops:
  37.9 31.8 %all-to-all-start.1 = ((bf16[8,128,512]{2,1,0:T(8,128)(2,1)}), bf16[8,128,512]{2,1,0:T(8,128)(2,1)S(1)}, u32[]{:S(2)}, u32[]{:S(2)}) async-start(bf16[8,128,512]{2,1,0:T(8,128)(2,1)} %bitcast.1), calls=%async_computation.1 | async-start | bytes 2097152 | tf_op jit(solution)/shard_map/all_to_all | solution.py:451
  55.9 32.5 %collective-permute-start.2 = (bf16[128,512]{1,0:T(8,128)(2,1)}, bf16[128,512]{1,0:T(8,128)(2,1)S(1)}, u32[]{:S(2)}, u32[]{:S(2)}) collective-permute-start(bf16[128,512]{1,0:T(8,128)(2,1)} %get-tuple-element.51), channel_id=1, source_target_pairs={{0,96},{16,112},{32,0},{48,16},{64,32},{80,48},{96,64},{112,80},{1... | collective-permute-start | bytes 393224 | tf_op jit(solution)/shard_map/ppermute | solution.py:457
  59.9 28.4 %collective-permute-start.3 = (bf16[128,512]{1,0:T(8,128)(2,1)}, bf16[128,512]{1,0:T(8,128)(2,1)S(1)}, u32[]{:S(2)}, u32[]{:S(2)}) collective-permute-start(bf16[128,512]{1,0:T(8,128)(2,1)} %get-tuple-element.52), channel_id=1, source_target_pairs={{0,80},{16,96},{32,112},{48,0},{64,16},{80,32},{96,48},{112,64},{1... | collective-permute-start | bytes 393224 | tf_op jit(solution)/shard_map/ppermute | solution.py:457
  62.3 26.1 %collective-permute-start.4 = (bf16[128,512]{1,0:T(8,128)(2,1)}, bf16[128,512]{1,0:T(8,128)(2,1)S(1)}, u32[]{:S(2)}, u32[]{:S(2)}) collective-permute-start(bf16[128,512]{1,0:T(8,128)(2,1)} %get-tuple-element.53), channel_id=1, source_target_pairs={{0,64},{16,80},{32,96},{48,112},{64,0},{80,16},{96,32},{112,48},{1... | collective-permute-start | bytes 393224 | tf_op jit(solution)/shard_map/ppermute | solution.py:457
  65.0 23.4 %collective-permute-start.5 = (bf16[128,512]{1,0:T(8,128)(2,1)}, bf16[128,512]{1,0:T(8,128)(2,1)S(1)}, u32[]{:S(2)}, u32[]{:S(2)}) collective-permute-start(bf16[128,512]{1,0:T(8,128)(2,1)} %get-tuple-element.54), channel_id=1, source_target_pairs={{0,48},{16,64},{32,80},{48,96},{64,112},{80,0},{96,16},{112,32},{1... | collective-permute-start | bytes 393224 | tf_op jit(solution)/shard_map/ppermute | solution.py:457
  66.1 22.3 %collective-permute-start.6 = (bf16[128,512]{1,0:T(8,128)(2,1)}, bf16[128,512]{1,0:T(8,128)(2,1)S(1)}, u32[]{:S(2)}, u32[]{:S(2)}) collective-permute-start(bf16[128,512]{1,0:T(8,128)(2,1)} %get-tuple-element.55), channel_id=1, source_target_pairs={{0,32},{16,48},{32,64},{48,80},{64,96},{80,112},{96,0},{112,16},{1... | collective-permute-start | bytes 393224 | tf_op jit(solution)/shard_map/ppermute | solution.py:457
  69.8 1.0 copy-start.2
  88.3 10.6 %copy-start = (bf16[16,16,2176]{2,1,0:T(8,128)(2,1)S(1)}, bf16[16,16,2176]{2,1,0:T(8,128)(2,1)}, u32[]{:S(2)}) copy-start(bf16[16,16,2176]{2,1,0:T(8,128)(2,1)} %get-tuple-element.65.keep_ref) | copy-start | bytes 3342340
  88.4 37.4 %all-to-all-start.2 = ((bf16[8,128,512]{2,1,0:T(8,128)(2,1)}), bf16[8,128,512]{2,1,0:T(8,128)(2,1)S(1)}, u32[]{:S(2)}, u32[]{:S(2)}) async-start(bf16[8,128,512]{2,1,0:T(8,128)(2,1)} %get-tuple-element.64), calls=%async_computation.2 | async-start | bytes 2097152 | tf_op jit(solution)/shard_map/all_to_all | solution.py:451
  95.8 8.2 %copy-start.4 = (bf16[128,512]{1,0:T(8,128)(2,1)S(1)}, bf16[128,512]{1,0:T(8,128)(2,1)}, u32[]{:S(2)}) copy-start(bf16[128,512]{1,0:T(8,128)(2,1)} %get-tuple-element.49) | copy-start | bytes 393220
  95.8 11.4 %copy-start.3 = (bf16[128,512]{1,0:T(8,128)(2,1)S(1)}, bf16[128,512]{1,0:T(8,128)(2,1)}, u32[]{:S(2)}) copy-start(bf16[128,512]{1,0:T(8,128)(2,1)} %get-tuple-element.50) | copy-start | bytes 393220
  95.8 37.1 %copy-start.1 = (bf16[128,512]{1,0:T(8,128)(2,1)S(1)}, bf16[128,512]{1,0:T(8,128)(2,1)}, u32[]{:S(2)}) copy-start(bf16[128,512]{1,0:T(8,128)(2,1)} %get-tuple-element.48.refs_0_) | copy-start | bytes 393220
  95.9 3.1 %collective-permute-start.7 = (bf16[16,16,2176]{2,1,0:T(8,128)(2,1)}, bf16[16,16,2176]{2,1,0:T(8,128)(2,1)S(1)}, u32[]{:S(2)}, u32[]{:S(2)}) collective-permute-start(bf16[16,16,2176]{2,1,0:T(8,128)(2,1)} %get-tuple-element.66), channel_id=1, source_target_pairs={{0,1},{1,0},{2,3},{3,2},{4,5},{5,4},{6,7},{7,6},{8,9},{9,8},{10,11... | collective-permute-start | bytes 3342344 | tf_op jit(solution)/shard_map/ppermute | solution.py:479
  99.2 9.6 %collective-permute-start.8 = (bf16[4,16,2176]{2,1,0:T(8,128)(2,1)S(1)}, bf16[4,16,2176]{2,1,0:T(8,128)(2,1)S(1)}, u32[]{:S(2)}, u32[]{:S(2)}) collective-permute-start(bf16[4,16,2176]{2,1,0:T(8,128)(2,1)S(1)} %get-tuple-element.68), channel_id=1, source_target_pairs={{0,128},{128,2},{2,130},{130,0},{1,129},{129,3},{3,131},{131,1},{4... | collective-permute-start | bytes 835592 | tf_op jit(solution)/shard_map/ppermute | solution.py:463
  100.7 11.0 %collective-permute-start.9 = (bf16[4,16,2176]{2,1,0:T(8,128)(2,1)S(1)}, bf16[4,16,2176]{2,1,0:T(8,128)(2,1)S(1)}, u32[]{:S(2)}, u32[]{:S(2)}) collective-permute-start(bf16[4,16,2176]{2,1,0:T(8,128)(2,1)S(1)} %get-tuple-element.69), channel_id=1, source_target_pairs={{0,2},{128,130},{2,0},{130,128},{1,3},{129,131},{3,1},{131,129},{4... | collective-permute-start | bytes 835592 | tf_op jit(solution)/shard_map/ppermute | solution.py:463
  101.8 14.1 %collective-permute-start.10 = (bf16[4,16,2176]{2,1,0:T(8,128)(2,1)S(1)}, bf16[4,16,2176]{2,1,0:T(8,128)(2,1)S(1)}, u32[]{:S(2)}, u32[]{:S(2)}) collective-permute-start(bf16[4,16,2176]{2,1,0:T(8,128)(2,1)S(1)} %get-tuple-element.70), channel_id=1, source_target_pairs={{0,130},{128,0},{2,128},{130,2},{1,131},{129,1},{3,129},{131,3},{4... | collective-permute-start | bytes 835592 | tf_op jit(solution)/shard_map/ppermute | solution.py:463
  104.0 21.7 %collective-permute-start = (bf16[128,512]{1,0:T(8,128)(2,1)S(1)}, bf16[128,512]{1,0:T(8,128)(2,1)S(1)}, u32[]{:S(2)}, u32[]{:S(2)}) collective-permute-start(bf16[128,512]{1,0:T(8,128)(2,1)S(1)} %copy-done.4), channel_id=1, source_target_pairs={{0,112},{16,0},{32,16},{48,32},{64,48},{80,64},{96,80},{112,96},{1... | collective-permute-start | bytes 393224 | tf_op jit(solution)/shard_map/ppermute | solution.py:457
  107.2 18.5 %collective-permute-start.1 = (bf16[128,512]{1,0:T(8,128)(2,1)S(1)}, bf16[128,512]{1,0:T(8,128)(2,1)S(1)}, u32[]{:S(2)}, u32[]{:S(2)}) collective-permute-start(bf16[128,512]{1,0:T(8,128)(2,1)S(1)} %copy-done.3), channel_id=1, source_target_pairs={{0,16},{16,32},{32,48},{48,64},{64,80},{80,96},{96,112},{112,0},{1... | collective-permute-start | bytes 393224 | tf_op jit(solution)/shard_map/ppermute | solution.py:457
  116.1 6.3 %collective-permute-start.11 = (bf16[16,2176]{1,0:T(8,128)(2,1)S(1)}, bf16[16,2176]{1,0:T(8,128)(2,1)S(1)}, u32[]{:S(2)}, u32[]{:S(2)}) collective-permute-start(bf16[16,2176]{1,0:T(8,128)(2,1)S(1)} %get-tuple-element.72), channel_id=1, source_target_pairs={{0,4},{4,8},{8,12},{12,0},{1,5},{5,9},{9,13},{13,1},{2,6},{6,10},{... | collective-permute-start | bytes 208904 | tf_op jit(solution)/shard_map/ppermute | solution.py:463
  117.7 5.9 %collective-permute-start.12 = (bf16[16,2176]{1,0:T(8,128)(2,1)S(1)}, bf16[16,2176]{1,0:T(8,128)(2,1)S(1)}, u32[]{:S(2)}, u32[]{:S(2)}) collective-permute-start(bf16[16,2176]{1,0:T(8,128)(2,1)S(1)} %get-tuple-element.73), channel_id=1, source_target_pairs={{0,8},{4,12},{8,0},{12,4},{1,9},{5,13},{9,1},{13,5},{2,10},{6,14},... | collective-permute-start | bytes 208904 | tf_op jit(solution)/shard_map/ppermute | solution.py:463
  120.7 4.3 %collective-permute-start.13 = (bf16[16,2176]{1,0:T(8,128)(2,1)S(1)}, bf16[16,2176]{1,0:T(8,128)(2,1)S(1)}, u32[]{:S(2)}, u32[]{:S(2)}) collective-permute-start(bf16[16,2176]{1,0:T(8,128)(2,1)S(1)} %get-tuple-element.74), channel_id=1, source_target_pairs={{0,12},{4,0},{8,4},{12,8},{1,13},{5,1},{9,5},{13,9},{2,14},{6,2},{... | collective-permute-start | bytes 208904 | tf_op jit(solution)/shard_map/ppermute | solution.py:463
  125.7 15.9 %all-to-all-start.3 = ((bf16[8,2,3072]{2,1,0:T(2,128)(2,1)}), bf16[8,2,3072]{2,1,0:T(2,128)(2,1)S(1)}, u32[]{:S(2)}, u32[]{:S(2)}) async-start(bf16[8,2,3072]{2,1,0:T(2,128)(2,1)} %y_sum.1), calls=%async_computation.3 | async-start | bytes 196608 | tf_op jit(solution)/shard_map/all_to_all | solution.py:451

commit v5 on v4

--- a/solution.py
+++ b/solution.py
@@ -107,7 +107,12 @@
 
 def forward_kernel(slabs_ref, w_qkv_ref, w_out_ref, gain_ref, bias_ref, *refs):
     piece_refs = refs[:GRID]
-    latent_ref, proj_ref, attended_ref, probs_ref, cells_ref = refs[GRID:]
+    saved_refs, cells_ref = refs[GRID : GRID + 4], refs[GRID + 4]
+    latent_ref, proj_ref, attended_ref, probs_ref, sems = refs[GRID + 5 :]
+    stores = [
+        pltpu.make_async_copy(source, target, sems.at[i])
+        for i, (source, target) in enumerate(zip(refs[GRID + 5 :], saved_refs))
+    ]
     width = w_out_ref.shape[0]
     rows = latent_ref.shape[0] // STEPS
     to_windows(slabs_ref, cells_ref)
@@ -118,6 +123,8 @@
         scaled, _ = norm_parts(latent)
         normed = (scaled * gain_ref[...] + bias_ref[...]).astype(LOW)
         proj_ref[at, :] = dot_nn(normed, w_qkv_ref[...]).astype(LOW)
+    stores[0].start()
+    stores[1].start()
     heads = Heads(width)
 
     def window(w, carry):
@@ -132,6 +139,8 @@
         return carry
 
     lax.fori_loop(0, latent_ref.shape[0] // heads.cells, window, 0, unroll=UNROLL)
+    stores[2].start()
+    stores[3].start()
     for step in range(STEPS):
         at = slice(step * rows, (step + 1) * rows)
         value = step_rows(cells_ref, step) + dot_nn(attended_ref[at, :], w_out_ref[...])
@@ -139,6 +148,8 @@
     spot = lax.axis_index("z")
     for shift in range(GRID):
         piece_refs[shift][...] = from_windows(cells_ref, lax.rem(spot + GRID - shift, GRID))
+    for store in stores:
+        store.wait()
 
 
 def backward_kernel(
@@ -363,7 +374,15 @@
         w_out,
         gain,
         bias,
-        scratch=[pltpu.VMEM((columns // GRID, spots, GRID, width), jnp.float32)],
+        scratch=[
+            pltpu.VMEM((columns // GRID, spots, GRID, width), jnp.float32),
+            pltpu.VMEM((tokens, width), LOW),
+            pltpu.VMEM((tokens, 3 * width), LOW),
+            pltpu.VMEM((tokens, width), LOW),
+            pltpu.VMEM((tokens, HEADS * GRID * GRID), LOW),
+            pltpu.SemaphoreType.DMA((4,)),
+        ],
+        out_specs=[VMEM] * spots + [ANY] * 4,
         flops=flops,
         moved=10 * 2**20,
         exps=tokens * HEADS * GRID * GRID,

time: 143 us -> 143 us (level)
  no operation moved by 1% of the time
where the time goes in v5:
time: 143 us; the launch traced here: 142 us
  starting transfers between devices  46.5 us (33%)
  blocking collectives  37.3 us (26%)
  Pallas kernels  34.2 us (24%)
  waiting for transfers between devices  22.6 us (16%)
    all_to_all x1, blocking collectives, swap(): return lax.all_to_all(value, axes, split_axis=0, concat_axis=0, tiled=True)  37.3 us
    pallas_call x7, Pallas kernels, call(): pl.pallas_call(kernel, out_shape=out_shape, in_specs=in_specs or [VMEM] *...  34.2 us
    all_to_all x3, starting transfers between devices, swap(): return lax.all_to_all(value, axes, split_axis=0, concat_axis=0, tiled=True)  18.6 us
    ppermute x7, starting transfers between devices, turn(): lax.ppermute(value, 'z', [(a, (a + shift) % GRID) for a in range(GRID)])  17.1 us
    ppermute x6, waiting for transfers between devices, ring_parts(): lax.ppermute(part, axes, pairs[s])  11.7 us
    ppermute x6, starting transfers between devices, ring_parts(): lax.ppermute(part, axes, pairs[s])  10.7 us
    all_to_all x3, waiting for transfers between devices, swap(): return lax.all_to_all(value, axes, split_axis=0, concat_axis=0, tiled=True)  7.92 us
    ppermute x1, waiting for transfers between devices, body(): parts = core_sum(keep, lax.ppermute(send, 'core', [(0, 1), (1, 0)]))  2.95 us
  transfers between devices with their start and end apart: 17, of which 9 were waited for; matrix products, arithmetic and copies ran while one was open for 0% of the time, Pallas kernels for 24%

profile of v5, /device:TPU:2, one launch (start us, length us, event | category | flops | bytes accessed | tf_op | source)
XLA Modules:
  0.0 142.4 jit_solution(13567203021147158889)
XLA Ops:
  0.6 37.3 %all_to_all.20.slabs_ref = bf16[8,128,512]{2,1,0:T(8,128)(2,1)} all-to-all(bf16[8,128,512]{2,1,0:T(8,128)(2,1)} %bitcast.6), channel_id=1, replica_groups=mesh['dp'=2,'z'=8,'y'=4,'x_hi'=2,'core'=2] {'z'}, dimensions={0} | all-to-all | bytes 2097152 | tf_op jit(solution)/shard_map/all_to_all | solution.py:470
  37.9 3.6 %all-to-all-start.1 = ((bf16[8,128,512]{2,1,0:T(8,128)(2,1)}), bf16[8,128,512]{2,1,0:T(8,128)(2,1)S(1)}, u32[]{:S(2)}, u32[]{:S(2)}) async-start(bf16[8,128,512]{2,1,0:T(8,128)(2,1)} %bitcast.1), calls=%async_computation.1 | async-start | bytes 2097152 | tf_op jit(solution)/shard_map/all_to_all | solution.py:470
  41.5 13.4 %forward.1 = (bf16[128,512]{1,0:T(8,128)(2,1)}, bf16[128,512]{1,0:T(8,128)(2,1)}, bf16[128,512]{1,0:T(8,128)(2,1)}, bf16[128,512]{1,0:T(8,128)(2,1)}, bf16[128,5...) custom-call(bf16[8,128,512]{2,1,0:T(8,128)(2,1)} %all_to_all.20.slab, ...), custom_call_target="tpu_custom_call" | custom-call | flops 2684354560 | bytes 10485760 | tf_op jit(solution)/shard_map/forward/pallas_call | solution.py:346
  54.9 4.1 %collective-permute-start.2 = (bf16[128,512]{1,0:T(8,128)(2,1)}, bf16[128,512]{1,0:T(8,128)(2,1)S(1)}, u32[]{:S(2)}, u32[]{:S(2)}) collective-permute-start(bf16[128,512]{1,0:T(8,128)(2,1)} %get-tuple-element.51), channel_id=1, source_target_pairs={{0,96},{16,112},{32,0},{48,16},{64,32},{80,48},{96,64},{112,80},{1... | collective-permute-start | bytes 393224 | tf_op jit(solution)/shard_map/ppermute | solution.py:476
  59.0 2.3 %collective-permute-start.3 = (bf16[128,512]{1,0:T(8,128)(2,1)}, bf16[128,512]{1,0:T(8,128)(2,1)S(1)}, u32[]{:S(2)}, u32[]{:S(2)}) collective-permute-start(bf16[128,512]{1,0:T(8,128)(2,1)} %get-tuple-element.52), channel_id=1, source_target_pairs={{0,80},{16,96},{32,112},{48,0},{64,16},{80,32},{96,48},{112,64},{1... | collective-permute-start | bytes 393224 | tf_op jit(solution)/shard_map/ppermute | solution.py:476
  61.3 2.7 %collective-permute-start.4 = (bf16[128,512]{1,0:T(8,128)(2,1)}, bf16[128,512]{1,0:T(8,128)(2,1)S(1)}, u32[]{:S(2)}, u32[]{:S(2)}) collective-permute-start(bf16[128,512]{1,0:T(8,128)(2,1)} %get-tuple-element.53), channel_id=1, source_target_pairs={{0,64},{16,80},{32,96},{48,112},{64,0},{80,16},{96,32},{112,48},{1... | collective-permute-start | bytes 393224 | tf_op jit(solution)/shard_map/ppermute | solution.py:476
  64.0 1.1 collective-permute-start.5
  65.1 3.6 %collective-permute-start.6 = (bf16[128,512]{1,0:T(8,128)(2,1)}, bf16[128,512]{1,0:T(8,128)(2,1)S(1)}, u32[]{:S(2)}, u32[]{:S(2)}) collective-permute-start(bf16[128,512]{1,0:T(8,128)(2,1)} %get-tuple-element.55), channel_id=1, source_target_pairs={{0,32},{16,48},{32,64},{48,80},{64,96},{80,112},{96,0},{112,16},{1... | collective-permute-start | bytes 393224 | tf_op jit(solution)/shard_map/ppermute | solution.py:476
  68.7 0.7 all-to-all-done.1.slabs_ref
  69.4 0.0 copy-start.2
  69.4 1.0 copy-done.2
  70.4 17.5 %backward.1 = (bf16[8,128,512]{2,1,0:T(8,128)(2,1)}, bf16[16,16,2176]{2,1,0:T(8,128)(2,1)}, bf16[16,16,2176]{2,1,0:T(8,128)(2,1)}) custom-call(bf16[8,128,512]{2,1,0:T(8,128)(2,1)} %copy-done.2, bf16[1024,512]{1,0:T(8,128)(2,1)} %get-tuple-element.57.latent_ref, bf16[1024,1536]{1,0:T(8,128)(2,1)} %get-tuple-element.58.proj_ref, ...), custom_call_target="tpu_custom_call" | custom-call | flops 6174015488 | bytes 16777216 | tf_op jit(solution)/shard_map/backward/pallas_call | solution.py:346
  88.0 0.0 copy-start
  88.0 0.0 collective-permute-done.2.refs_2_
  88.0 0.0 collective-permute-done.3.refs_3_
  88.0 0.0 collective-permute-done.4.refs_4_
  88.0 0.0 collective-permute-done.5.refs_5_
  88.0 0.0 collective-permute-done.6.refs_6_
  88.0 7.8 %all-to-all-start.2 = ((bf16[8,128,512]{2,1,0:T(8,128)(2,1)}), bf16[8,128,512]{2,1,0:T(8,128)(2,1)S(1)}, u32[]{:S(2)}, u32[]{:S(2)}) async-start(bf16[8,128,512]{2,1,0:T(8,128)(2,1)} %get-tuple-element.64), calls=%async_computation.2 | async-start | bytes 2097152 | tf_op jit(solution)/shard_map/all_to_all | solution.py:470
  95.8 0.0 copy-start.4
  95.8 0.0 copy-start.3
  95.8 0.0 copy-start.1
  95.9 0.1 collective-permute-start.7
  96.0 3.0 %collective-permute-done.7.got_ref = bf16[16,16,2176]{2,1,0:T(8,128)(2,1)S(1)} collective-permute-done((bf16[16,16,2176]{2,1,0:T(8,128)(2,1)}, bf16[16,16,2176]{2,1,0:T(8,128)(2,1)S(1)}, u32[]{:S(2)}, u32[]{:S(2)}) %collective-permute-start.7) | collective-permute-done | bytes 1114144 | tf_op jit(solution)/shard_map/ppermute | solution.py:498
  98.9 0.0 copy-done
  98.9 0.3 core_sum.1
  99.2 1.6 %collective-permute-start.8 = (bf16[4,16,2176]{2,1,0:T(8,128)(2,1)S(1)}, bf16[4,16,2176]{2,1,0:T(8,128)(2,1)S(1)}, u32[]{:S(2)}, u32[]{:S(2)}) collective-permute-start(bf16[4,16,2176]{2,1,0:T(8,128)(2,1)S(1)} %get-tuple-element.68), channel_id=1, source_target_pairs={{0,128},{128,2},{2,130},{130,0},{1,129},{129,3},{3,131},{131,1},{4... | collective-permute-start | bytes 835592 | tf_op jit(solution)/shard_map/ppermute | solution.py:482
  100.7 1.1 collective-permute-start.9
  101.8 2.2 %collective-permute-start.10 = (bf16[4,16,2176]{2,1,0:T(8,128)(2,1)S(1)}, bf16[4,16,2176]{2,1,0:T(8,128)(2,1)S(1)}, u32[]{:S(2)}, u32[]{:S(2)}) collective-permute-start(bf16[4,16,2176]{2,1,0:T(8,128)(2,1)S(1)} %get-tuple-element.70), channel_id=1, source_target_pairs={{0,130},{128,0},{2,128},{130,2},{1,131},{129,1},{3,129},{131,3},{4... | collective-permute-start | bytes 835592 | tf_op jit(solution)/shard_map/ppermute | solution.py:482
  104.0 0.0 copy-done.4
  104.0 3.2 %collective-permute-start = (bf16[128,512]{1,0:T(8,128)(2,1)S(1)}, bf16[128,512]{1,0:T(8,128)(2,1)S(1)}, u32[]{:S(2)}, u32[]{:S(2)}) collective-permute-start(bf16[128,512]{1,0:T(8,128)(2,1)S(1)} %copy-done.4), channel_id=1, source_target_pairs={{0,112},{16,0},{32,16},{48,32},{64,48},{80,64},{96,80},{112,96},{1... | collective-permute-start | bytes 393224 | tf_op jit(solution)/shard_map/ppermute | solution.py:476
  107.2 0.0 copy-done.3
  107.2 0.0 collective-permute-start.1
  107.2 1.5 %collective-permute-done.8.refs_1_ = bf16[4,16,2176]{2,1,0:T(8,128)(2,1)S(1)} collective-permute-done((bf16[4,16,2176]{2,1,0:T(8,128)(2,1)S(1)}, bf16[4,16,2176]{2,1,0:T(8,128)(2,1)S(1)}, u32[]{:S(2)}, u32[]{:S(2)}) %collective-permute-start.8) | collective-permute-done | bytes 278560 | tf_op jit(solution)/shard_map/ppermute | solution.py:482
  108.7 3.0 %collective-permute-done.9.refs_2_ = bf16[4,16,2176]{2,1,0:T(8,128)(2,1)S(1)} collective-permute-done((bf16[4,16,2176]{2,1,0:T(8,128)(2,1)S(1)}, bf16[4,16,2176]{2,1,0:T(8,128)(2,1)S(1)}, u32[]{:S(2)}, u32[]{:S(2)}) %collective-permute-start.9) | collective-permute-done | bytes 278560 | tf_op jit(solution)/shard_map/ppermute | solution.py:482
  111.8 4.2 %collective-permute-done.10.refs_3_ = bf16[4,16,2176]{2,1,0:T(8,128)(2,1)S(1)} collective-permute-done((bf16[4,16,2176]{2,1,0:T(8,128)(2,1)S(1)}, bf16[4,16,2176]{2,1,0:T(8,128)(2,1)S(1)}, u32[]{:S(2)}, u32[]{:S(2)}) %collective-permute-start.10) | collective-permute-done | bytes 278560 | tf_op jit(solution)/shard_map/ppermute | solution.py:482
  115.9 0.1 x_sum.1
  116.1 1.7 %collective-permute-start.11 = (bf16[16,2176]{1,0:T(8,128)(2,1)S(1)}, bf16[16,2176]{1,0:T(8,128)(2,1)S(1)}, u32[]{:S(2)}, u32[]{:S(2)}) collective-permute-start(bf16[16,2176]{1,0:T(8,128)(2,1)S(1)} %get-tuple-element.72), channel_id=1, source_target_pairs={{0,4},{4,8},{8,12},{12,0},{1,5},{5,9},{9,13},{13,1},{2,6},{6,10},{... | collective-permute-start | bytes 208904 | tf_op jit(solution)/shard_map/ppermute | solution.py:482
  117.7 2.9 %collective-permute-start.12 = (bf16[16,2176]{1,0:T(8,128)(2,1)S(1)}, bf16[16,2176]{1,0:T(8,128)(2,1)S(1)}, u32[]{:S(2)}, u32[]{:S(2)}) collective-permute-start(bf16[16,2176]{1,0:T(8,128)(2,1)S(1)} %get-tuple-element.73), channel_id=1, source_target_pairs={{0,8},{4,12},{8,0},{12,4},{1,9},{5,13},{9,1},{13,5},{2,10},{6,14},... | collective-permute-start | bytes 208904 | tf_op jit(solution)/shard_map/ppermute | solution.py:482
  120.7 1.3 collective-permute-start.13
  122.0 0.4 collective-permute-done.11.refs_1_
  122.4 1.3 collective-permute-done.12.refs_2_
  123.7 1.3 collective-permute-done.13.refs_3_
  125.0 0.8 y_sum.1
  125.7 0.0 collective-permute-done.refs_1_
  125.7 0.0 collective-permute-done.1.refs_7_
  125.7 0.0 all-to-all-done.2.refs_8_
  125.7 7.2 %all-to-all-start.3 = ((bf16[8,2,3072]{2,1,0:T(2,128)(2,1)}), bf16[8,2,3072]{2,1,0:T(2,128)(2,1)S(1)}, u32[]{:S(2)}, u32[]{:S(2)}) async-start(bf16[8,2,3072]{2,1,0:T(2,128)(2,1)} %y_sum.1), calls=%async_computation.3 | async-start | bytes 196608 | tf_op jit(solution)/shard_map/all_to_all | solution.py:470
  132.9 0.0 copy-done.1
  133.0 1.5 %gather_slabs.1 = (bf16[8,128,512]{2,1,0:T(8,128)(2,1)}, bf16[8,128,512]{2,1,0:T(8,128)(2,1)}) custom-call(bf16[128,512]{1,0:T(8,128)(2,1)S(1)} %copy-done.1, bf16[128,512]{1,0:T(8,128)(2,1)S(1)} %collective-permute-done.refs_1_, bf16[128,512]{1,0:T(8,128)(2,1)S(1)} %collective-permute-done.2.refs_2_, bf16[128,512]{1,0:T(8,128)(2,1)S(1)} %collective-permute-done.3.refs_3_, ...), custom_call_target="tpu_custom_call" | custom-call | tf_op jit(solution)/shard_map/gather_slabs/pallas_call | solution.py:346
  134.4 7.2 %all-to-all-done.3.shares_ref = bf16[8,2,3072]{2,1,0:T(2,128)(2,1)S(1)} async-done(((bf16[8,2,3072]{2,1,0:T(2,128)(2,1)}), bf16[8,2,3072]{2,1,0:T(2,128)(2,1)S(1)}, u32[]{:S(2)}, u32[]{:S(2)}) %all-to-all-start.3) | async-done | bytes 98336 | tf_op jit(solution)/shard_map/all_to_all | solution.py:470
  141.7 0.7 second_sum.1
Async XLA Ops:
  37.9 31.5 %all-to-all-start.1 = ((bf16[8,128,512]{2,1,0:T(8,128)(2,1)}), bf16[8,128,512]{2,1,0:T(8,128)(2,1)S(1)}, u32[]{:S(2)}, u32[]{:S(2)}) async-start(bf16[8,128,512]{2,1,0:T(8,128)(2,1)} %bitcast.1), calls=%async_computation.1 | async-start | bytes 2097152 | tf_op jit(solution)/shard_map/all_to_all | solution.py:470
  54.9 33.1 %collective-permute-start.2 = (bf16[128,512]{1,0:T(8,128)(2,1)}, bf16[128,512]{1,0:T(8,128)(2,1)S(1)}, u32[]{:S(2)}, u32[]{:S(2)}) collective-permute-start(bf16[128,512]{1,0:T(8,128)(2,1)} %get-tuple-element.51), channel_id=1, source_target_pairs={{0,96},{16,112},{32,0},{48,16},{64,32},{80,48},{96,64},{112,80},{1... | collective-permute-start | bytes 393224 | tf_op jit(solution)/shard_map/ppermute | solution.py:476
  59.0 29.0 %collective-permute-start.3 = (bf16[128,512]{1,0:T(8,128)(2,1)}, bf16[128,512]{1,0:T(8,128)(2,1)S(1)}, u32[]{:S(2)}, u32[]{:S(2)}) collective-permute-start(bf16[128,512]{1,0:T(8,128)(2,1)} %get-tuple-element.52), channel_id=1, source_target_pairs={{0,80},{16,96},{32,112},{48,0},{64,16},{80,32},{96,48},{112,64},{1... | collective-permute-start | bytes 393224 | tf_op jit(solution)/shard_map/ppermute | solution.py:476
  61.3 26.7 %collective-permute-start.4 = (bf16[128,512]{1,0:T(8,128)(2,1)}, bf16[128,512]{1,0:T(8,128)(2,1)S(1)}, u32[]{:S(2)}, u32[]{:S(2)}) collective-permute-start(bf16[128,512]{1,0:T(8,128)(2,1)} %get-tuple-element.53), channel_id=1, source_target_pairs={{0,64},{16,80},{32,96},{48,112},{64,0},{80,16},{96,32},{112,48},{1... | collective-permute-start | bytes 393224 | tf_op jit(solution)/shard_map/ppermute | solution.py:476
  64.0 24.0 %collective-permute-start.5 = (bf16[128,512]{1,0:T(8,128)(2,1)}, bf16[128,512]{1,0:T(8,128)(2,1)S(1)}, u32[]{:S(2)}, u32[]{:S(2)}) collective-permute-start(bf16[128,512]{1,0:T(8,128)(2,1)} %get-tuple-element.54), channel_id=1, source_target_pairs={{0,48},{16,64},{32,80},{48,96},{64,112},{80,0},{96,16},{112,32},{1... | collective-permute-start | bytes 393224 | tf_op jit(solution)/shard_map/ppermute | solution.py:476
  65.1 22.9 %collective-permute-start.6 = (bf16[128,512]{1,0:T(8,128)(2,1)}, bf16[128,512]{1,0:T(8,128)(2,1)S(1)}, u32[]{:S(2)}, u32[]{:S(2)}) collective-permute-start(bf16[128,512]{1,0:T(8,128)(2,1)} %get-tuple-element.55), channel_id=1, source_target_pairs={{0,32},{16,48},{32,64},{48,80},{64,96},{80,112},{96,0},{112,16},{1... | collective-permute-start | bytes 393224 | tf_op jit(solution)/shard_map/ppermute | solution.py:476
  69.4 1.0 copy-start.2
  88.0 10.9 %copy-start = (bf16[16,16,2176]{2,1,0:T(8,128)(2,1)S(1)}, bf16[16,16,2176]{2,1,0:T(8,128)(2,1)}, u32[]{:S(2)}) copy-start(bf16[16,16,2176]{2,1,0:T(8,128)(2,1)} %get-tuple-element.65.keep_ref) | copy-start | bytes 3342340
  88.0 37.7 %all-to-all-start.2 = ((bf16[8,128,512]{2,1,0:T(8,128)(2,1)}), bf16[8,128,512]{2,1,0:T(8,128)(2,1)S(1)}, u32[]{:S(2)}, u32[]{:S(2)}) async-start(bf16[8,128,512]{2,1,0:T(8,128)(2,1)} %get-tuple-element.64), calls=%async_computation.2 | async-start | bytes 2097152 | tf_op jit(solution)/shard_map/all_to_all | solution.py:470
  95.8 8.2 %copy-start.4 = (bf16[128,512]{1,0:T(8,128)(2,1)S(1)}, bf16[128,512]{1,0:T(8,128)(2,1)}, u32[]{:S(2)}) copy-start(bf16[128,512]{1,0:T(8,128)(2,1)} %get-tuple-element.49) | copy-start | bytes 393220
  95.8 11.4 %copy-start.3 = (bf16[128,512]{1,0:T(8,128)(2,1)S(1)}, bf16[128,512]{1,0:T(8,128)(2,1)}, u32[]{:S(2)}) copy-start(bf16[128,512]{1,0:T(8,128)(2,1)} %get-tuple-element.50) | copy-start | bytes 393220
  95.8 37.1 %copy-start.1 = (bf16[128,512]{1,0:T(8,128)(2,1)S(1)}, bf16[128,512]{1,0:T(8,128)(2,1)}, u32[]{:S(2)}) copy-start(bf16[128,512]{1,0:T(8,128)(2,1)} %get-tuple-element.48.refs_0_) | copy-start | bytes 393220
  95.9 3.1 %collective-permute-start.7 = (bf16[16,16,2176]{2,1,0:T(8,128)(2,1)}, bf16[16,16,2176]{2,1,0:T(8,128)(2,1)S(1)}, u32[]{:S(2)}, u32[]{:S(2)}) collective-permute-start(bf16[16,16,2176]{2,1,0:T(8,128)(2,1)} %get-tuple-element.66), channel_id=1, source_target_pairs={{0,1},{1,0},{2,3},{3,2},{4,5},{5,4},{6,7},{7,6},{8,9},{9,8},{10,11... | collective-permute-start | bytes 3342344 | tf_op jit(solution)/shard_map/ppermute | solution.py:498
  99.2 9.6 %collective-permute-start.8 = (bf16[4,16,2176]{2,1,0:T(8,128)(2,1)S(1)}, bf16[4,16,2176]{2,1,0:T(8,128)(2,1)S(1)}, u32[]{:S(2)}, u32[]{:S(2)}) collective-permute-start(bf16[4,16,2176]{2,1,0:T(8,128)(2,1)S(1)} %get-tuple-element.68), channel_id=1, source_target_pairs={{0,128},{128,2},{2,130},{130,0},{1,129},{129,3},{3,131},{131,1},{4... | collective-permute-start | bytes 835592 | tf_op jit(solution)/shard_map/ppermute | solution.py:482
  100.7 11.0 %collective-permute-start.9 = (bf16[4,16,2176]{2,1,0:T(8,128)(2,1)S(1)}, bf16[4,16,2176]{2,1,0:T(8,128)(2,1)S(1)}, u32[]{:S(2)}, u32[]{:S(2)}) collective-permute-start(bf16[4,16,2176]{2,1,0:T(8,128)(2,1)S(1)} %get-tuple-element.69), channel_id=1, source_target_pairs={{0,2},{128,130},{2,0},{130,128},{1,3},{129,131},{3,1},{131,129},{4... | collective-permute-start | bytes 835592 | tf_op jit(solution)/shard_map/ppermute | solution.py:482
  101.8 14.1 %collective-permute-start.10 = (bf16[4,16,2176]{2,1,0:T(8,128)(2,1)S(1)}, bf16[4,16,2176]{2,1,0:T(8,128)(2,1)S(1)}, u32[]{:S(2)}, u32[]{:S(2)}) collective-permute-start(bf16[4,16,2176]{2,1,0:T(8,128)(2,1)S(1)} %get-tuple-element.70), channel_id=1, source_target_pairs={{0,130},{128,0},{2,128},{130,2},{1,131},{129,1},{3,129},{131,3},{4... | collective-permute-start | bytes 835592 | tf_op jit(solution)/shard_map/ppermute | solution.py:482
  104.0 21.7 %collective-permute-start = (bf16[128,512]{1,0:T(8,128)(2,1)S(1)}, bf16[128,512]{1,0:T(8,128)(2,1)S(1)}, u32[]{:S(2)}, u32[]{:S(2)}) collective-permute-start(bf16[128,512]{1,0:T(8,128)(2,1)S(1)} %copy-done.4), channel_id=1, source_target_pairs={{0,112},{16,0},{32,16},{48,32},{64,48},{80,64},{96,80},{112,96},{1... | collective-permute-start | bytes 393224 | tf_op jit(solution)/shard_map/ppermute | solution.py:476
  107.2 18.5 %collective-permute-start.1 = (bf16[128,512]{1,0:T(8,128)(2,1)S(1)}, bf16[128,512]{1,0:T(8,128)(2,1)S(1)}, u32[]{:S(2)}, u32[]{:S(2)}) collective-permute-start(bf16[128,512]{1,0:T(8,128)(2,1)S(1)} %copy-done.3), channel_id=1, source_target_pairs={{0,16},{16,32},{32,48},{48,64},{64,80},{80,96},{96,112},{112,0},{1... | collective-permute-start | bytes 393224 | tf_op jit(solution)/shard_map/ppermute | solution.py:476
  116.1 6.3 %collective-permute-start.11 = (bf16[16,2176]{1,0:T(8,128)(2,1)S(1)}, bf16[16,2176]{1,0:T(8,128)(2,1)S(1)}, u32[]{:S(2)}, u32[]{:S(2)}) collective-permute-start(bf16[16,2176]{1,0:T(8,128)(2,1)S(1)} %get-tuple-element.72), channel_id=1, source_target_pairs={{0,4},{4,8},{8,12},{12,0},{1,5},{5,9},{9,13},{13,1},{2,6},{6,10},{... | collective-permute-start | bytes 208904 | tf_op jit(solution)/shard_map/ppermute | solution.py:482
  117.7 5.9 %collective-permute-start.12 = (bf16[16,2176]{1,0:T(8,128)(2,1)S(1)}, bf16[16,2176]{1,0:T(8,128)(2,1)S(1)}, u32[]{:S(2)}, u32[]{:S(2)}) collective-permute-start(bf16[16,2176]{1,0:T(8,128)(2,1)S(1)} %get-tuple-element.73), channel_id=1, source_target_pairs={{0,8},{4,12},{8,0},{12,4},{1,9},{5,13},{9,1},{13,5},{2,10},{6,14},... | collective-permute-start | bytes 208904 | tf_op jit(solution)/shard_map/ppermute | solution.py:482
  120.7 4.3 %collective-permute-start.13 = (bf16[16,2176]{1,0:T(8,128)(2,1)S(1)}, bf16[16,2176]{1,0:T(8,128)(2,1)S(1)}, u32[]{:S(2)}, u32[]{:S(2)}) collective-permute-start(bf16[16,2176]{1,0:T(8,128)(2,1)S(1)} %get-tuple-element.74), channel_id=1, source_target_pairs={{0,12},{4,0},{8,4},{12,8},{1,13},{5,1},{9,5},{13,9},{2,14},{6,2},{... | collective-permute-start | bytes 208904 | tf_op jit(solution)/shard_map/ppermute | solution.py:482
  125.7 15.9 %all-to-all-start.3 = ((bf16[8,2,3072]{2,1,0:T(2,128)(2,1)}), bf16[8,2,3072]{2,1,0:T(2,128)(2,1)S(1)}, u32[]{:S(2)}, u32[]{:S(2)}) async-start(bf16[8,2,3072]{2,1,0:T(2,128)(2,1)} %y_sum.1), calls=%async_computation.3 | async-start | bytes 196608 | tf_op jit(solution)/shard_map/all_to_all | solution.py:470
